TPU v7x, 128 devices: a whole 4x4x4 slice. The times are simulated.
128 devices in a mesh: section: 2 (over z_lo), dp: 4 (over x), fsdp: 16 (over z_hi, y, core).
Axes of the slice: x: 4, y: 4, z: 4 (z_hi: 2, z_lo: 2; z = z_hi * 2 + z_lo), core: 2. Of those that a mesh axis runs over, the one named last changes fastest.
Arguments:
- boundary: bfloat16 [2, 2, 64, 128, 1024], P('section', None, ('dp', 'fsdp')), may hold values from -6 to 6
- mixer_gain: bfloat16 [2, 1024], P('section', 'fsdp'), may hold values from 0.25 to 1.75
- query_weight: bfloat16 [2, 1024, 2048], P('section', 'fsdp'), may hold values from -0.1875 to 0.1875
- key_weight: bfloat16 [2, 1024, 1024], P('section', 'fsdp'), may hold values from -0.1875 to 0.1875
- value_weight: bfloat16 [2, 1024, 1024], P('section', 'fsdp'), may hold values from -0.1875 to 0.1875
- output_weight: bfloat16 [2, 2048, 1024], P('section', 'fsdp'), may hold values from -0.5 to 0.5
- query_gain: bfloat16 [2, 128], P('section', 'fsdp'), may hold values from 0.25 to 1.75
- key_gain: bfloat16 [2, 128], P('section', 'fsdp'), may hold values from 0.25 to 1.75
- dense_gain: bfloat16 [2, 1024], P('section', 'fsdp'), may hold values from 0.25 to 1.75
- gate_weight: bfloat16 [2, 1024, 3072], P('section', 'fsdp'), may hold values from -0.1875 to 0.1875
- up_weight: bfloat16 [2, 1024, 3072], P('section', 'fsdp'), may hold values from -0.1875 to 0.1875
- down_weight: bfloat16 [2, 3072, 1024], P('section', 'fsdp'), may hold values from -0.109375 to 0.109375
Outputs:
- endpoints: float32 [2, 2, 64, 128, 1024], P('section', None, ('dp', 'fsdp'))
- mixer_gain_gradient: float32 [2, 1024], P('section', 'fsdp')
- query_weight_gradient: float32 [2, 1024, 2048], P('section', 'fsdp')
- key_weight_gradient: float32 [2, 1024, 1024], P('section', 'fsdp')
- value_weight_gradient: float32 [2, 1024, 1024], P('section', 'fsdp')
- output_weight_gradient: float32 [2, 2048, 1024], P('section', 'fsdp')
- query_gain_gradient: float32 [2, 128], P('section', 'fsdp')
- key_gain_gradient: float32 [2, 128], P('section', 'fsdp')
- dense_gain_gradient: float32 [2, 1024], P('section', 'fsdp')
- gate_weight_gradient: float32 [2, 1024, 3072], P('section', 'fsdp')
- up_weight_gradient: float32 [2, 1024, 3072], P('section', 'fsdp')
- down_weight_gradient: float32 [2, 3072, 1024], P('section', 'fsdp')
All inputs are finite; a program needn't handle non-finite values.
Results may differ from a plain program's by a relative error of at most 0.035.
Values may be sent and summed in bfloat16 or wider, within the bound.
No kernel may reach another device: no remote copies, remote signals or barrier semaphores. Data moves between devices by JAX's collectives and lax.ppermute only.
A program may use at most 640 MiB of HBM per device.

v0:
```python
import math

import jax
import jax.numpy as jnp
from jax import lax
from jax.sharding import PartitionSpec as P

epsilon = 1e-06
rope_base = 1000000.0


def sent_together(arrays, axis, dim, along):
    widths = [math.prod(a.shape[along:]) for a in arrays]
    both = jnp.concatenate(
        [a.reshape(*a.shape[:along], w) for a, w in zip(arrays, widths)], axis=along
    )
    whole = lax.all_gather(both, axis, axis=dim, tiled=True)
    parts = jnp.split(whole, [sum(widths[:k]) for k in range(1, len(widths))], axis=along)
    return tuple((b.reshape(*whole.shape[:along], *a.shape[along:]) for a, b in zip(arrays, parts)))


def in_one_piece(arrays, axis, dim, along):
    both = jnp.concatenate(arrays, axis=along)
    whole, at, outs = (lax.all_gather(both, axis, axis=dim, tiled=True), 0, [])
    for a in arrays:
        outs.append(lax.slice_in_dim(whole, at, at + a.shape[along], axis=along))
        at += a.shape[along]
    return tuple(outs)


def from_behind(value, axis, steps):
    count = lax.axis_size(axis)
    initial, last = (max(0, -steps), min(count, count - steps))
    return lax.ppermute(value, axis, [(source, source + steps) for source in range(initial, last)])


def shortened(shard):

    def short(part):
        return part.astype(jnp.bfloat16) if part.dtype == jnp.float32 else part

    return jax.tree.map(short, shard)


def row_scale(values):
    return lax.rsqrt(jnp.mean(values * values, axis=-1, keepdims=True) + epsilon)


def rotation_tables(length, head_size):
    half_size = head_size // 2
    places = jnp.arange(length, dtype=jnp.float32)
    frequencies = rope_base ** (-jnp.arange(half_size, dtype=jnp.float32) * 2.0 / head_size)
    angles = places[:, None] * frequencies[None, :]
    return (jnp.cos(angles)[:, None, :], jnp.sin(angles)[:, None, :])


def rotate_heads(values, tables):
    cosine_table, sine_table = tables
    half_size = values.shape[-1] // 2
    first_half = values[..., :half_size]
    second_half = values[..., half_size:]
    return jnp.concatenate(
        [
            first_half * cosine_table - second_half * sine_table,
            second_half * cosine_table + first_half * sine_table,
        ],
        axis=-1,
    )


def unrotate_heads(upstream, tables):
    cosine_table, sine_table = tables
    half_size = upstream.shape[-1] // 2
    first_half = upstream[..., :half_size]
    second_half = upstream[..., half_size:]
    return jnp.concatenate(
        [
            first_half * cosine_table + second_half * sine_table,
            second_half * cosine_table - first_half * sine_table,
        ],
        axis=-1,
    )


def norm_backward(upstream, normed, scaling, gain_vector):
    gain_part = jnp.sum(upstream * normed, axis=tuple(range(upstream.ndim - 1)))
    scaled = upstream * gain_vector
    return (
        scaling * (scaled - normed * jnp.mean(scaled * normed, axis=-1, keepdims=True)),
        gain_part,
    )


def forward_layer(hidden_in, parts, tables):
    (
        mixer_gain,
        query_weight,
        key_weight,
        value_weight,
        output_weight,
        query_gain,
        key_gain,
        dense_gain,
        gate_weight,
        up_weight,
        down_weight,
    ) = parts
    length = hidden_in.shape[0]
    head_size = query_gain.shape[0]
    query_heads = query_weight.shape[1] // head_size
    key_heads = key_weight.shape[1] // head_size
    group_size = query_heads // key_heads
    scale_one = row_scale(hidden_in)
    normed_one = hidden_in * scale_one
    mixer_input = (normed_one * mixer_gain.astype(jnp.float32)).astype(jnp.bfloat16)
    query_raw = jnp.dot(mixer_input, query_weight, preferred_element_type=jnp.float32).reshape(
        length, query_heads, head_size
    )
    key_raw = jnp.dot(mixer_input, key_weight, preferred_element_type=jnp.float32).reshape(
        length, key_heads, head_size
    )
    value_low = jnp.dot(mixer_input, value_weight, preferred_element_type=jnp.float32).astype(
        jnp.bfloat16
    )
    value_low = value_low.reshape(length, key_heads, head_size)
    query_scale = row_scale(query_raw)
    query_normed = query_raw * query_scale
    key_scale = row_scale(key_raw)
    key_normed = key_raw * key_scale
    query_turned = rotate_heads(query_normed * query_gain.astype(jnp.float32), tables).astype(
        jnp.bfloat16
    )
    key_turned = rotate_heads(key_normed * key_gain.astype(jnp.float32), tables).astype(
        jnp.bfloat16
    )
    query_groups = query_turned.reshape(length, key_heads, group_size, head_size)
    scores = jnp.einsum(
        "qkgd,skd->kgqs", query_groups, key_turned, preferred_element_type=jnp.float32
    ) * head_size ** (-0.5)
    causal = jnp.arange(length)[:, None] >= jnp.arange(length)[None, :]
    scores = jnp.where(causal, scores, -1e30)
    probabilities = jax.nn.softmax(scores, axis=-1)
    soft_low = probabilities.astype(jnp.bfloat16)
    attended = jnp.einsum("kgqs,skd->qkgd", soft_low, value_low, preferred_element_type=jnp.float32)
    attended = attended.astype(jnp.bfloat16).reshape(length, query_heads * head_size)
    after_mixer = hidden_in + jnp.dot(attended, output_weight, preferred_element_type=jnp.float32)
    scale_two = row_scale(after_mixer)
    normed_two = after_mixer * scale_two
    dense_input = (normed_two * dense_gain.astype(jnp.float32)).astype(jnp.bfloat16)
    gate_value = jnp.dot(dense_input, gate_weight, preferred_element_type=jnp.float32)
    up_value = jnp.dot(dense_input, up_weight, preferred_element_type=jnp.float32)
    hidden_units = (jax.nn.silu(gate_value) * up_value).astype(jnp.bfloat16)
    block_output = after_mixer + jnp.dot(
        hidden_units, down_weight, preferred_element_type=jnp.float32
    )
    residues = (
        scale_one,
        normed_one,
        mixer_input,
        query_scale,
        query_normed,
        key_scale,
        key_normed,
        query_groups,
        key_turned,
        value_low,
        probabilities,
        soft_low,
        attended,
        scale_two,
        normed_two,
        dense_input,
        gate_value,
        up_value,
        hidden_units,
    )
    return (block_output, residues)


def backward_layer(cotangent, residues, parts, tables):
    (
        mixer_gain,
        query_weight,
        key_weight,
        value_weight,
        output_weight,
        query_gain,
        key_gain,
        dense_gain,
        gate_weight,
        up_weight,
        down_weight,
    ) = parts
    (
        scale_one,
        normed_one,
        mixer_input,
        query_scale,
        query_normed,
        key_scale,
        key_normed,
        query_groups,
        key_turned,
        value_low,
        probabilities,
        soft_low,
        attended,
        scale_two,
        normed_two,
        dense_input,
        gate_value,
        up_value,
        hidden_units,
    ) = residues
    length = cotangent.shape[0]
    key_heads, group_size, head_size = (
        query_groups.shape[1],
        query_groups.shape[2],
        query_groups.shape[3],
    )
    query_heads = key_heads * group_size
    dense_back = cotangent.astype(jnp.bfloat16)
    down_gradient = jnp.dot(hidden_units.T, dense_back, preferred_element_type=jnp.float32)
    hidden_gradient = jnp.dot(dense_back, down_weight.T, preferred_element_type=jnp.float32)
    sigmoid_gate = jax.nn.sigmoid(gate_value)
    gate_back = (
        hidden_gradient * up_value * sigmoid_gate * (1.0 + gate_value * (1.0 - sigmoid_gate))
    ).astype(jnp.bfloat16)
    up_back = (hidden_gradient * (gate_value * sigmoid_gate)).astype(jnp.bfloat16)
    gate_gradient = jnp.dot(dense_input.T, gate_back, preferred_element_type=jnp.float32)
    up_gradient = jnp.dot(dense_input.T, up_back, preferred_element_type=jnp.float32)
    dense_input_back = jnp.dot(
        gate_back, gate_weight.T, preferred_element_type=jnp.float32
    ) + jnp.dot(up_back, up_weight.T, preferred_element_type=jnp.float32)
    dense_part, dense_gain_gradient = norm_backward(
        dense_input_back, normed_two, scale_two, dense_gain.astype(jnp.float32)
    )
    residual_back = cotangent + dense_part
    mixer_back = residual_back.astype(jnp.bfloat16)
    output_gradient = jnp.dot(attended.T, mixer_back, preferred_element_type=jnp.float32)
    attended_back = jnp.dot(mixer_back, output_weight.T, preferred_element_type=jnp.float32).astype(
        jnp.bfloat16
    )
    attended_back = attended_back.reshape(length, key_heads, group_size, head_size)
    soft_back = jnp.einsum(
        "qkgd,skd->kgqs", attended_back, value_low, preferred_element_type=jnp.float32
    )
    value_back = jnp.einsum(
        "kgqs,qkgd->skd", soft_low, attended_back, preferred_element_type=jnp.float32
    )
    value_back = value_back.astype(jnp.bfloat16).reshape(length, key_heads * head_size)
    score_back = probabilities * (
        soft_back - jnp.sum(soft_back * probabilities, axis=-1, keepdims=True)
    )
    score_back = score_back.astype(jnp.bfloat16)
    inverse_root = head_size ** (-0.5)
    turned_query_back = jnp.einsum(
        "kgqs,skd->qkgd", score_back, key_turned, preferred_element_type=jnp.float32
    )
    turned_query_back = turned_query_back.reshape(length, query_heads, head_size) * inverse_root
    turned_key_back = (
        jnp.einsum("kgqs,qkgd->skd", score_back, query_groups, preferred_element_type=jnp.float32)
        * inverse_root
    )
    query_back, query_gain_gradient = norm_backward(
        unrotate_heads(turned_query_back, tables),
        query_normed,
        query_scale,
        query_gain.astype(jnp.float32),
    )
    key_back, key_gain_gradient = norm_backward(
        unrotate_heads(turned_key_back, tables), key_normed, key_scale, key_gain.astype(jnp.float32)
    )
    query_low = query_back.astype(jnp.bfloat16).reshape(length, query_heads * head_size)
    key_low = key_back.astype(jnp.bfloat16).reshape(length, key_heads * head_size)
    query_gradient = jnp.dot(mixer_input.T, query_low, preferred_element_type=jnp.float32)
    key_gradient = jnp.dot(mixer_input.T, key_low, preferred_element_type=jnp.float32)
    value_gradient = jnp.dot(mixer_input.T, value_back, preferred_element_type=jnp.float32)
    mixer_input_back = (
        jnp.dot(query_low, query_weight.T, preferred_element_type=jnp.float32)
        + jnp.dot(key_low, key_weight.T, preferred_element_type=jnp.float32)
        + jnp.dot(value_back, value_weight.T, preferred_element_type=jnp.float32)
    )
    input_part, mixer_gain_gradient = norm_backward(
        mixer_input_back, normed_one, scale_one, mixer_gain.astype(jnp.float32)
    )
    input_back = residual_back + input_part
    gradients = (
        mixer_gain_gradient,
        query_gradient,
        key_gradient,
        value_gradient,
        output_gradient,
        query_gain_gradient,
        key_gain_gradient,
        dense_gain_gradient,
        gate_gradient,
        up_gradient,
        down_gradient,
    )
    return (input_back, gradients)


def on_device(
    boundary,
    mixer_gain,
    query_weight,
    key_weight,
    value_weight,
    output_weight,
    query_gain,
    key_gain,
    dense_gain,
    gate_weight,
    up_weight,
    down_weight,
):
    owned_shards = (
        mixer_gain,
        query_weight,
        key_weight,
        value_weight,
        output_weight,
        query_gain,
        key_gain,
        dense_gain,
        gate_weight,
        up_weight,
        down_weight,
    )
    section_index = lax.axis_index("section")
    first_section = section_index == 0
    micro_count = boundary.shape[1]
    length = boundary.shape[3]
    features = boundary.shape[4]
    local_rows = boundary[0, :, 0].astype(jnp.float32)
    forward_parts = tuple(
        (
            member[0]
            for member in (
                *sent_together(
                    (owned_shards[0], owned_shards[1], owned_shards[2], owned_shards[3]),
                    "fsdp",
                    1,
                    2,
                ),
                lax.all_gather(owned_shards[4], "fsdp", axis=1, tiled=True),
                *in_one_piece((owned_shards[5], owned_shards[6]), "fsdp", 1, 0),
                *sent_together((owned_shards[7], owned_shards[8], owned_shards[9]), "fsdp", 1, 2),
                lax.all_gather(owned_shards[10], "fsdp", axis=1, tiled=True),
            )
        )
    )
    tables = rotation_tables(length, forward_parts[5].shape[0])
    arrived = jnp.zeros((length, features), jnp.bfloat16)
    saved_ticks = []
    outputs = []
    for moment in range(micro_count + 1):
        active = (moment - section_index >= 0) & (moment - section_index < micro_count)
        block_input = jnp.where(
            first_section, local_rows[min(moment, micro_count - 1)], arrived.astype(jnp.float32)
        )
        result, residues = lax.cond(
            active,
            lambda values: forward_layer(values, forward_parts, tables),
            lambda values: jax.tree.map(
                jnp.zeros_like, forward_layer(values, forward_parts, tables)
            ),
            block_input,
        )
        arrived = from_behind(result.astype(jnp.bfloat16), "section", 1)
        saved_ticks.append(residues)
        outputs.append(result)
    stacked = jax.tree.map(lambda *members: jnp.stack(members), *saved_ticks)
    backward_parts = tuple(
        (
            member[0]
            for member in (
                lax.all_gather(owned_shards[0], "fsdp", axis=1, tiled=True),
                lax.all_gather(owned_shards[1], "fsdp", axis=1, tiled=True),
                lax.all_gather(owned_shards[2], "fsdp", axis=1, tiled=True),
                lax.all_gather(owned_shards[3], "fsdp", axis=1, tiled=True),
                lax.all_gather(owned_shards[4], "fsdp", axis=1, tiled=True),
                lax.all_gather(owned_shards[5], "fsdp", axis=1, tiled=True),
                lax.all_gather(owned_shards[6], "fsdp", axis=1, tiled=True),
                lax.all_gather(owned_shards[7], "fsdp", axis=1, tiled=True),
                lax.all_gather(owned_shards[8], "fsdp", axis=1, tiled=True),
                lax.all_gather(owned_shards[9], "fsdp", axis=1, tiled=True),
                lax.all_gather(owned_shards[10], "fsdp", axis=1, tiled=True),
            )
        )
    )
    returned = jnp.zeros((length, features), jnp.bfloat16)
    input_backs = []
    owner_totals = None
    carried = None
    for moment in range(micro_count + 1):
        micro_index = moment - 1 + section_index
        active = (micro_index >= 0) & (micro_index < micro_count)
        forward_moment = jnp.clip(micro_index + section_index, 0, micro_count)
        residues = jax.tree.map(
            lambda member: lax.dynamic_index_in_dim(member, forward_moment, 0, keepdims=False),
            stacked,
        )
        cotangent = jnp.where(
            first_section, returned.astype(jnp.float32), local_rows[min(moment, micro_count - 1)]
        )
        input_back, gradients = lax.cond(
            active,
            lambda upstream, saved: backward_layer(upstream, saved, backward_parts, tables),
            lambda upstream, saved: jax.tree.map(
                jnp.zeros_like, backward_layer(upstream, saved, backward_parts, tables)
            ),
            cotangent,
            residues,
        )
        returned = from_behind(input_back.astype(jnp.bfloat16), "section", -1)
        input_backs.append(input_back)
        if moment == 0:
            carried = gradients
        else:
            if carried is not None:
                gradients = jax.tree.map(jnp.add, carried, gradients)
                carried = None
            shares = jax.tree.map(
                lambda part: part.astype(jnp.float32),
                lax.psum_scatter(shortened(gradients), "fsdp", scatter_dimension=0, tiled=True),
            )
            owner_totals = (
                shares if owner_totals is None else jax.tree.map(jnp.add, owner_totals, shares)
            )
    summed = jax.tree.map(
        lambda part: part.astype(jnp.float32), lax.psum(shortened(owner_totals), "dp")
    )
    finals = jnp.stack(
        [
            jnp.where(first_section, input_backs[moment], outputs[moment])
            for moment in range(1, micro_count + 1)
        ]
    )
    endpoints = finals[None, :, None]
    return (endpoints,) + tuple((member[None] for member in summed))


def solution(mesh):
    placed = (
        P("section", None, ("dp", "fsdp"), None, None),
        P("section", "fsdp"),
        P("section", "fsdp", None),
        P("section", "fsdp", None),
        P("section", "fsdp", None),
        P("section", "fsdp", None),
        P("section", "fsdp"),
        P("section", "fsdp"),
        P("section", "fsdp"),
        P("section", "fsdp", None),
        P("section", "fsdp", None),
        P("section", "fsdp", None),
    )
    return jax.shard_map(
        on_device,
        mesh=mesh,
        in_specs=placed,
        out_specs=(
            P("section", None, ("dp", "fsdp"), None, None),
            P("section", "fsdp"),
            P("section", "fsdp", None),
            P("section", "fsdp", None),
            P("section", "fsdp", None),
            P("section", "fsdp", None),
            P("section", "fsdp"),
            P("section", "fsdp"),
            P("section", "fsdp"),
            P("section", "fsdp", None),
            P("section", "fsdp", None),
            P("section", "fsdp", None),
        ),
        check_vma=False,
    )
```

profile of v0, /device:TPU:1, one launch (start us, length us, event | category | flops | bytes accessed | tf_op | source)
XLA Modules:
  0.0 2026.7 jit_solution(10335379350828700025)
XLA Ops:
  18.3 26.5 %all-gather = bf16[16,8,2]{1,2,0:T(2,128)(2,1)S(1)} all-gather(bf16[1,8,2]{1,2,0:T(2,128)(2,1)S(1)} %maximum_bitcast_fusion.31), channel_id=1, replica_groups=mesh['section'=2,'dp'=4,'fsdp'=16] {'fsdp'}, dimensions={0}, use_global_device_ids=true | all-gather | bytes 544 | tf_op jit(solution)/shard_map/all_gather | solution.py:24
  48.5 34.3 %all-reduce.13 = (bf16[1024]{0:T(1024)(128)(2,1)}, bf16[128]{0:T(256)(128)(2,1)}, bf16[128]{0:T(256)(128)(2,1)}, bf16[1024]{0:T(1024)(128)(2,1)}) all-reduce(bf16[1024]{0:T(1024)(128)(2,1)S(1)} %dynamic-update-slice, bf16[128]{0:T(256)(128)(2,1)S(1)} %dynamic-update-slice.1, ...), channel_id=1, replica_groups=mesh['section'=2,'dp'=4,'fsdp'=16] {'fsdp'}, use_global_device_ids=true, to_apply=%add | all-reduce | flops 2304 | bytes 9216 | tf_op jit(solution)/shard_map/squeeze | solution.py:377
  90.4 5.9 slice_bitcast_fusion.3
  96.3 6.3 slice_bitcast_fusion.2
  102.6 79.5 %all-gather.15.cloned.1.call-done = bf16[1,1024,6145]{2,1,0:T(8,128)(2,1)} async-done(((bf16[1,64,6145]{2,1,0:T(8,128)(2,1)}), bf16[1,1024,6145]{2,1,0:T(8,128)(2,1)}) %all-gather.15.cloned.1.call-update) | async-done | bytes 12584976 | tf_op jit(solution)/shard_map/all_gather | solution.py:17
  183.2 13.3 slice_bitcast_fusion
  196.4 41.8 %all-gather.13.cloned.1.call-done = bf16[1,2048,1024]{2,1,0:T(8,128)(2,1)} async-done(((bf16[1,128,1024]{2,1,0:T(8,128)(2,1)}), bf16[1,2048,1024]{2,1,0:T(8,128)(2,1)}) %all-gather.13.cloned.1.call-update) | async-done | bytes 4194320 | tf_op jit(solution)/shard_map/all_gather | solution.py:347
  238.2 65.3 %all-gather.17.cloned.1.call-done = bf16[1,3072,1024]{2,1,0:T(8,128)(2,1)} async-done(((bf16[1,192,1024]{2,1,0:T(8,128)(2,1)}), bf16[1,3072,1024]{2,1,0:T(8,128)(2,1)}) %all-gather.17.cloned.1.call-update) | async-done | bytes 6291472 | tf_op jit(solution)/shard_map/all_gather | solution.py:350
  304.3 86.0 %conditional.6 = (bf16[128,1024]{1,0:T(8,128)(2,1)}, f32[1,128,1]{1,2,0:T(1,128)}, f32[1,128,1024]{2,1,0:T(8,128)}, bf16[1,128,1024]{2,1,0:T(8,128)(2,1)S(1)}, f...) conditional(s32[]{:T(128)} %convert_element_type.636, ...), branch_computations={%region_0.1_spmd, %region_1.8_spmd} | conditional | flops 4243611392 | bytes 130791592 | solution.py:363
  418.2 75.9 %conditional.7 = (f32[128,1024]{1,0:T(8,128)S(1)}, f32[1,128,1]{1,2,0:T(1,128)}, f32[1,128,1024]{2,1,0:T(8,128)}, bf16[1,128,1024]{2,1,0:T(8,128)(2,1)S(1)}, f32...) conditional(s32[]{:T(128)} %convert_element_type.637, ...), branch_computations={%region_8.9_spmd, %region_9.16_spmd} | conditional | flops 4243480320 | bytes 133149864 | solution.py:363
  526.9 12.9 conditional.8
  569.4 25.2 %all-gather.21.cloned.1.call-done = bf16[1,1024,3072]{2,1,0:T(8,128)(2,1)} async-done(((bf16[1,64,3072]{2,1,0:T(8,128)(2,1)}), bf16[1,1024,3072]{2,1,0:T(8,128)(2,1)}) %all-gather.21.cloned.1.call-update) | async-done | bytes 6291472 | tf_op jit(solution)/shard_map/all_gather | solution.py:388
  595.3 42.1 %conditional.9 = (bf16[128,1024]{1,0:T(8,128)(2,1)}, f32[1024]{0:T(1024)S(1)}, f32[1024,2048]{1,0:T(8,128)}, f32[1024,1024]{1,0:T(8,128)}, f32[1024,1024]{1,0:T(...) conditional(s32[]{:T(128)} %convert_element_type.634, ...), branch_computations={%region_24.25_spmd, %region_25.35_spmd} | conditional | flops 8340371456 | bytes 272177376 | solution.py:408
  595.3 6.2 broadcast.1006
  601.5 6.1 broadcast.1006.clone
  607.6 6.2 broadcast.1007
  638.8 35.2 %collective-permute-done.2 = bf16[128,1024]{1,0:T(8,128)(2,1)S(1)} collective-permute-done((bf16[128,1024]{1,0:T(8,128)(2,1)}, bf16[128,1024]{1,0:T(8,128)(2,1)S(1)}, u32[]{:S(2)}, u32[]{:S(2)}) %collective-permute-start.2) | collective-permute-done | bytes 262176 | tf_op jit(solution)/shard_map/ppermute | solution.py:34
  674.0 71.1 %conditional.10 = (f32[128,1024]{1,0:T(8,128)}, f32[1024]{0:T(1024)S(1)}, f32[1024,2048]{1,0:T(8,128)}, f32[1024,1024]{1,0:T(8,128)}, f32[1024,1024]{1,0:T(8,128...) conditional(s32[]{:T(128)} %convert_element_type.633, ...), branch_computations={%region_35.36_spmd, %region_36.46_spmd} | conditional | flops 8340240384 | bytes 272439520 | solution.py:408
  675.2 6.8 fusion.195
  716.5 5.6 fusion.214
  724.8 6.5 fusion.241
  731.3 6.4 fusion.243
  737.7 7.5 fusion.211
  745.1 5.5 add_convert_fusion.11
  754.4 7.4 collective-permute-done.3
  763.5 63.6 %conditional.11 = (f32[128,1024]{1,0:T(8,128)}, bf16[1024]{0:T(1024)(128)(2,1)S(1)}, bf16[1024,2048]{1,0:T(8,128)(2,1)}, bf16[1024,1024]{1,0:T(8,128)(2,1)}, bf1...) conditional(s32[]{:T(128)} %convert_element_type.645, ...), branch_computations={%region_46.47_spmd, %region_47.57_spmd} | conditional | flops 8340240384 | bytes 226301664 | solution.py:408
  765.1 7.4 fusion.284
  821.3 5.6 fusion.300
  827.3 5.5 add_convert_fusion.12
  833.6 9.6 add_convert_fusion.9
  843.9 9.7 add_convert_fusion.10
  854.2 12.2 add_convert_fusion.6
  867.2 12.2 add_convert_fusion.7
  880.2 12.1 add_convert_fusion.8
  898.5 72.1 %reduce-scatter.19.cloned.1.call-done = bf16[64,1024]{1,0:T(8,128)(2,1)} async-done(((bf16[1024,1024]{1,0:T(8,128)(2,1)}), bf16[64,1024]{1,0:T(8,128)(2,1)}) %reduce-scatter.19.cloned.1.call-update) | async-done | bytes 131088 | tf_op jit(solution)/shard_map/reduce_scatter | solution.py:427
  970.6 73.9 %reduce-scatter.21.cloned.1.call-done = bf16[64,1024]{1,0:T(8,128)(2,1)} async-done(((bf16[1024,1024]{1,0:T(8,128)(2,1)}), bf16[64,1024]{1,0:T(8,128)(2,1)}) %reduce-scatter.21.cloned.1.call-update) | async-done | bytes 131088 | tf_op jit(solution)/shard_map/reduce_scatter | solution.py:427
  1046.1 82.2 %reduce-scatter.27.cloned.1.call-done = bf16[128,1024]{1,0:T(8,128)(2,1)} async-done(((bf16[2048,1024]{1,0:T(8,128)(2,1)}), bf16[128,1024]{1,0:T(8,128)(2,1)}) %reduce-scatter.27.cloned.1.call-update) | async-done | bytes 262160 | tf_op jit(solution)/shard_map/reduce_scatter | solution.py:427
  1128.4 83.4 %reduce-scatter.29.cloned.1.call-done = bf16[128,1024]{1,0:T(8,128)(2,1)} async-done(((bf16[2048,1024]{1,0:T(8,128)(2,1)}), bf16[128,1024]{1,0:T(8,128)(2,1)}) %reduce-scatter.29.cloned.1.call-update) | async-done | bytes 262160 | tf_op jit(solution)/shard_map/reduce_scatter | solution.py:427
  1213.6 81.1 %reduce-scatter.15.cloned.1.call-done = bf16[64,2048]{1,0:T(8,128)(2,1)} async-done(((bf16[1024,2048]{1,0:T(8,128)(2,1)}), bf16[64,2048]{1,0:T(8,128)(2,1)}) %reduce-scatter.15.cloned.1.call-update) | async-done | bytes 262160 | tf_op jit(solution)/shard_map/reduce_scatter | solution.py:427
  1294.7 83.4 %reduce-scatter.17.cloned.1.call-done = bf16[64,2048]{1,0:T(8,128)(2,1)} async-done(((bf16[1024,2048]{1,0:T(8,128)(2,1)}), bf16[64,2048]{1,0:T(8,128)(2,1)}) %reduce-scatter.17.cloned.1.call-update) | async-done | bytes 262160 | tf_op jit(solution)/shard_map/reduce_scatter | solution.py:427
  1379.9 90.6 %reduce-scatter.39.cloned.1.call-done = bf16[192,1024]{1,0:T(8,128)(2,1)} async-done(((bf16[3072,1024]{1,0:T(8,128)(2,1)}), bf16[192,1024]{1,0:T(8,128)(2,1)}) %reduce-scatter.39.cloned.1.call-update) | async-done | bytes 393232 | tf_op jit(solution)/shard_map/reduce_scatter | solution.py:427
  1470.5 92.5 %reduce-scatter.41.cloned.1.call-done = bf16[192,1024]{1,0:T(8,128)(2,1)} async-done(((bf16[3072,1024]{1,0:T(8,128)(2,1)}), bf16[192,1024]{1,0:T(8,128)(2,1)}) %reduce-scatter.41.cloned.1.call-update) | async-done | bytes 393232 | tf_op jit(solution)/shard_map/reduce_scatter | solution.py:427
  1565.0 90.3 %reduce-scatter.35.cloned.1.call-done = bf16[64,3072]{1,0:T(8,128)(2,1)} async-done(((bf16[1024,3072]{1,0:T(8,128)(2,1)}), bf16[64,3072]{1,0:T(8,128)(2,1)}) %reduce-scatter.35.cloned.1.call-update) | async-done | bytes 393232 | tf_op jit(solution)/shard_map/reduce_scatter | solution.py:427
  1655.3 92.5 %reduce-scatter.37.cloned.1.call-done = bf16[64,3072]{1,0:T(8,128)(2,1)} async-done(((bf16[1024,3072]{1,0:T(8,128)(2,1)}), bf16[64,3072]{1,0:T(8,128)(2,1)}) %reduce-scatter.37.cloned.1.call-update) | async-done | bytes 393232 | tf_op jit(solution)/shard_map/reduce_scatter | solution.py:427
  1749.8 90.5 %reduce-scatter.31.cloned.1.call-done = bf16[64,3072]{1,0:T(8,128)(2,1)} async-done(((bf16[1024,3072]{1,0:T(8,128)(2,1)}), bf16[64,3072]{1,0:T(8,128)(2,1)}) %reduce-scatter.31.cloned.1.call-update) | async-done | bytes 393232 | tf_op jit(solution)/shard_map/reduce_scatter | solution.py:427
  1840.3 92.5 %reduce-scatter.33.cloned.1.call-done = bf16[64,3072]{1,0:T(8,128)(2,1)} async-done(((bf16[1024,3072]{1,0:T(8,128)(2,1)}), bf16[64,3072]{1,0:T(8,128)(2,1)}) %reduce-scatter.33.cloned.1.call-update) | async-done | bytes 393232 | tf_op jit(solution)/shard_map/reduce_scatter | solution.py:427
  1936.2 61.0 %all-reduce.12 = (bf16[1024]{0:T(1024)(128)(2,1)S(1)}, bf16[1024]{0:T(1024)(128)(2,1)S(1)}, bf16[128]{0:T(256)(128)(2,1)S(1)}, bf16[128]{0:T(256)(128)(2,1)S(1)}...) all-reduce(bf16[1024]{0:T(1024)(128)(2,1)S(1)} %get-tuple-element.1, ...), channel_id=3, replica_groups=mesh['section'=2,'dp'=4,'fsdp'=16] {'fsdp'}, use_global_device_ids=true, to_apply=%region_58.59.clone | all-reduce | flops 4608 | bytes 18432
  1997.5 8.7 all-reduce.14
  (642 shorter events, 422.4 us)
Async XLA Ops:
  7.2 38.3 %copy-start.96 = (bf16[1,2,1,128,1024]{4,3,2,1,0:T(8,128)(2,1)S(1)}, bf16[1,2,1,128,1024]{4,3,2,1,0:T(8,128)(2,1)}, u32[]{:S(2)}) copy-start(bf16[1,2,1,128,1024]{4,3,2,1,0:T(8,128)(2,1)} %param.24) | copy-start | bytes 1572868
  7.2 82.1 %all-gather.11.cloned.1.call-start = ((), (), s32[]{:S(2)}) async-start(), calls=%async_computation.14 | async-start | bytes 9191424 | tf_op jit(solution)/shard_map/all_gather | solution.py:17
  10.2 35.5 %copy-start.115 = (u32[128]{0:T(128)S(1)}, u32[128]{0:T(128)}, u32[]{:S(2)}) copy-start(u32[128]{0:T(128)} %constant.589) | copy-start | bytes 1540
  10.2 37.4 %copy-start.116 = (bf16[1,64]{1,0:T(2,128)(2,1)S(1)}, bf16[1,64]{1,0:T(2,128)(2,1)}, u32[]{:S(2)}) copy-start(bf16[1,64]{1,0:T(2,128)(2,1)} %param.32) | copy-start | bytes 388
  10.2 37.6 %copy-start.117 = (bf16[1,64]{1,0:T(2,128)(2,1)S(1)}, bf16[1,64]{1,0:T(2,128)(2,1)}, u32[]{:S(2)}) copy-start(bf16[1,64]{1,0:T(2,128)(2,1)} %param.25) | copy-start | bytes 388
  10.3 171.8 %all-gather.15.cloned.1.call-start = ((), (), s32[]{:S(2)}) async-start(), calls=%async_computation.16 | async-start | bytes 13647872 | tf_op jit(solution)/shard_map/all_gather | solution.py:17
  13.5 224.7 %all-gather.13.cloned.1.call-start = ((), (), s32[]{:S(2)}) async-start(), calls=%async_computation.15 | async-start | bytes 4456448 | tf_op jit(solution)/shard_map/all_gather | solution.py:347
  14.3 289.2 %all-gather.17.cloned.1.call-start = ((), (), s32[]{:S(2)}) async-start(), calls=%async_computation.17 | async-start | bytes 6684672 | tf_op jit(solution)/shard_map/all_gather | solution.py:350
  14.9 554.5 %all-gather.25.cloned.1.call-start = ((), (), s32[]{:S(2)}) async-start(), calls=%async_computation.21 | async-start | bytes 2228224 | tf_op jit(solution)/shard_map/all_gather | solution.py:381
  15.4 553.9 %all-gather.27.cloned.1.call-start = ((), (), s32[]{:S(2)}) async-start(), calls=%async_computation.22 | async-start | bytes 2228224 | tf_op jit(solution)/shard_map/all_gather | solution.py:382
  16.0 553.3 %all-gather.23.cloned.1.call-start = ((), (), s32[]{:S(2)}) async-start(), calls=%async_computation.20 | async-start | bytes 4456448 | tf_op jit(solution)/shard_map/all_gather | solution.py:380
  16.8 552.6 %all-gather.19.cloned.1.call-start = ((), (), s32[]{:S(2)}) async-start(), calls=%async_computation.18 | async-start | bytes 6684672 | tf_op jit(solution)/shard_map/all_gather | solution.py:387
  17.5 577.1 %all-gather.21.cloned.1.call-start = ((), (), s32[]{:S(2)}) async-start(), calls=%async_computation.19 | async-start | bytes 6684672 | tf_op jit(solution)/shard_map/all_gather | solution.py:388
  18.3 874.9 %reduce-scatter.23.cloned.1.call-start = ((), (), s32[]{:S(2)}) async-start(), calls=%async_computation.27 | async-start | bytes 2228224 | tf_op jit(solution)/shard_map/reduce_scatter | solution.py:427
  307.3 31.3 %copy-start.30 = (bf16[128,1024]{1,0:T(8,128)(2,1)}, bf16[128,1024]{1,0:T(8,128)(2,1)S(1)}, u32[]{:S(2)}) copy-start(bf16[128,1024]{1,0:T(8,128)(2,1)S(1)} %get-tuple-element.2073) | copy-start | bytes 786436 | tf_op jit(solution)/shard_map/cond
  390.4 27.8 %collective-permute-start = (bf16[128,1024]{1,0:T(8,128)(2,1)}, bf16[128,1024]{1,0:T(8,128)(2,1)S(1)}, u32[]{:S(2)}, u32[]{:S(2)}) collective-permute-start(bf16[128,1024]{1,0:T(8,128)(2,1)} %get-tuple-element.1507), channel_id=1, source_target_pairs={{0,64},{1,65},{2,66},{3,67},{4,68},{5,69},{6,70},{7,71},{8,72},{9,... | collective-permute-start | bytes 786440 | tf_op jit(solution)/shard_map/ppermute | solution.py:34
  494.2 32.7 %collective-permute-start.1 = (bf16[128,1024]{1,0:T(8,128)(2,1)S(1)}, bf16[128,1024]{1,0:T(8,128)(2,1)S(1)}, u32[]{:S(2)}, u32[]{:S(2)}) collective-permute-start(bf16[128,1024]{1,0:T(8,128)(2,1)S(1)} %convert_element_type.641), channel_id=1, source_target_pairs={{0,64},{1,65},{2,66},{3,67},{4,68},{5,69},{6,70},{7,71},{8,72},{9,... | collective-permute-start | bytes 786440 | tf_op jit(solution)/shard_map/ppermute | solution.py:34
  563.7 31.0 %copy-start.106 = (f32[3,128,8,1]{1,2,3,0:T(8,128)S(1)}, f32[3,128,8,1]{1,2,3,0:T(8,128)}, u32[]{:S(2)}) copy-start(f32[3,128,8,1]{1,2,3,0:T(8,128)} %constant_dynamic-update-slice_fusion.30) | copy-start | bytes 36868
  563.7 31.0 %copy-start.107 = (bf16[1024]{0:T(1024)(128)(2,1)S(1)}, bf16[1024]{0:T(1024)(128)(2,1)}, u32[]{:S(2)}) copy-start(bf16[1024]{0:T(1024)(128)(2,1)} %get-tuple-element.2039) | copy-start | bytes 6148
  563.8 31.0 %copy-start.108 = (bf16[1024]{0:T(1024)(128)(2,1)S(1)}, bf16[1024]{0:T(1024)(128)(2,1)}, u32[]{:S(2)}) copy-start(bf16[1024]{0:T(1024)(128)(2,1)} %get-tuple-element.2042) | copy-start | bytes 6148
  563.8 31.0 %copy-start.113 = (f32[3,128,1]{1,2,0:T(1,128)S(1)}, f32[3,128,1]{1,2,0:T(1,128)}, u32[]{:S(2)}) copy-start(f32[3,128,1]{1,2,0:T(1,128)} %constant_dynamic-update-slice_fusion) | copy-start | bytes 4612
  594.8 79.2 %copy-start.17 = (f32[128,1024]{1,0:T(8,128)S(1)}, f32[128,1024]{1,0:T(8,128)}, u32[]{:S(2)}) copy-start(f32[128,1024]{1,0:T(8,128)} %get-tuple-element.2190) | copy-start | bytes 1572868
  637.4 36.6 %copy-start.109 = (f32[1024]{0:T(1024)}, f32[1024]{0:T(1024)S(1)}, u32[]{:S(2)}) copy-start(f32[1024]{0:T(1024)S(1)} %get-tuple-element.1569) | copy-start | bytes 12292
  637.4 36.6 %copy-start.111 = (f32[1024]{0:T(1024)}, f32[1024]{0:T(1024)S(1)}, u32[]{:S(2)}) copy-start(f32[1024]{0:T(1024)S(1)} %get-tuple-element.1590) | copy-start | bytes 12292
  637.5 36.6 %copy-start.132 = (f32[128]{0:T(128)}, f32[128]{0:T(128)S(1)}, u32[]{:S(2)}) copy-start(f32[128]{0:T(128)S(1)} %get-tuple-element.1584) | copy-start | bytes 1540
  637.5 36.5 %collective-permute-start.2 = (bf16[128,1024]{1,0:T(8,128)(2,1)}, bf16[128,1024]{1,0:T(8,128)(2,1)S(1)}, u32[]{:S(2)}, u32[]{:S(2)}) collective-permute-start(bf16[128,1024]{1,0:T(8,128)(2,1)} %get-tuple-element.1565), channel_id=1, source_target_pairs={{64,0},{65,1},{66,2},{67,3},{68,4},{69,5},{70,6},{71,7},{72,8},{73... | collective-permute-start | bytes 786440 | tf_op jit(solution)/shard_map/ppermute | solution.py:34
  750.7 146.2 %reduce-scatter.25.cloned.1.call-start = ((), (), s32[]{:S(2)}) async-start(), calls=%async_computation.28 | async-start | bytes 2228224 | tf_op jit(solution)/shard_map/reduce_scatter | solution.py:427
  753.1 8.7 collective-permute-start.3
  827.2 143.4 %reduce-scatter.19.cloned.1.call-start = ((), (), s32[]{:S(2)}) async-start(), calls=%async_computation.25 | async-start | bytes 2228224 | tf_op jit(solution)/shard_map/reduce_scatter | solution.py:427
  832.8 211.7 %reduce-scatter.21.cloned.1.call-start = ((), (), s32[]{:S(2)}) async-start(), calls=%async_computation.26 | async-start | bytes 2228224 | tf_op jit(solution)/shard_map/reduce_scatter | solution.py:427
  833.5 294.8 %reduce-scatter.27.cloned.1.call-start = ((), (), s32[]{:S(2)}) async-start(), calls=%async_computation.29 | async-start | bytes 4456448 | tf_op jit(solution)/shard_map/reduce_scatter | solution.py:427
  843.2 368.5 %reduce-scatter.29.cloned.1.call-start = ((), (), s32[]{:S(2)}) async-start(), calls=%async_computation.30 | async-start | bytes 4456448 | tf_op jit(solution)/shard_map/reduce_scatter | solution.py:427
  843.8 450.8 %reduce-scatter.15.cloned.1.call-start = ((), (), s32[]{:S(2)}) async-start(), calls=%async_computation.23 | async-start | bytes 4456448 | tf_op jit(solution)/shard_map/reduce_scatter | solution.py:427
  853.6 524.5 %reduce-scatter.17.cloned.1.call-start = ((), (), s32[]{:S(2)}) async-start(), calls=%async_computation.24 | async-start | bytes 4456448 | tf_op jit(solution)/shard_map/reduce_scatter | solution.py:427
  854.2 616.3 %reduce-scatter.39.cloned.1.call-start = ((), (), s32[]{:S(2)}) async-start(), calls=%async_computation.35 | async-start | bytes 6684672 | tf_op jit(solution)/shard_map/reduce_scatter | solution.py:427
  866.4 696.6 %reduce-scatter.41.cloned.1.call-start = ((), (), s32[]{:S(2)}) async-start(), calls=%async_computation.36 | async-start | bytes 6684672 | tf_op jit(solution)/shard_map/reduce_scatter | solution.py:427
  867.2 788.1 %reduce-scatter.35.cloned.1.call-start = ((), (), s32[]{:S(2)}) async-start(), calls=%async_computation.33 | async-start | bytes 6684672 | tf_op jit(solution)/shard_map/reduce_scatter | solution.py:427
  879.4 868.4 %reduce-scatter.37.cloned.1.call-start = ((), (), s32[]{:S(2)}) async-start(), calls=%async_computation.34 | async-start | bytes 6684672 | tf_op jit(solution)/shard_map/reduce_scatter | solution.py:427
  880.2 960.1 %reduce-scatter.31.cloned.1.call-start = ((), (), s32[]{:S(2)}) async-start(), calls=%async_computation.31 | async-start | bytes 6684672 | tf_op jit(solution)/shard_map/reduce_scatter | solution.py:427
  892.4 1040.4 %reduce-scatter.33.cloned.1.call-start = ((), (), s32[]{:S(2)}) async-start(), calls=%async_computation.32 | async-start | bytes 6684672 | tf_op jit(solution)/shard_map/reduce_scatter | solution.py:427
  893.1 1117.3 %all-reduce.18.cloned.1.call-start = ((), (), s32[]{:S(2)}) async-start(), calls=%async_computation.37 | async-start | bytes 3932160 | tf_op jit(solution)/shard_map/psum | solution.py:433
  1213.5 722.5 %copy-start.134 = (f32[128]{0:T(128)S(1)}, f32[128]{0:T(128)}, u32[]{:S(2)}) copy-start(f32[128]{0:T(128)} %get-tuple-element.1587) | copy-start | bytes 1540
  1213.5 722.5 %copy-start.137 = (f32[128]{0:T(128)S(1)}, f32[128]{0:T(128)}, u32[]{:S(2)}) copy-start(f32[128]{0:T(128)} %get-tuple-element.1588) | copy-start | bytes 1540
  1213.5 722.5 %copy-start.133 = (f32[128]{0:T(128)S(1)}, f32[128]{0:T(128)}, u32[]{:S(2)}) copy-start(f32[128]{0:T(128)} %copy-done.132) | copy-start | bytes 1540
  1213.5 722.5 %copy-start.136 = (f32[128]{0:T(128)S(1)}, f32[128]{0:T(128)}, u32[]{:S(2)}) copy-start(f32[128]{0:T(128)} %copy-done.135) | copy-start | bytes 1540
  1213.6 722.6 %copy-start.112 = (f32[1024]{0:T(1024)S(1)}, f32[1024]{0:T(1024)}, u32[]{:S(2)}) copy-start(f32[1024]{0:T(1024)} %copy-done.111) | copy-start | bytes 12292
  1213.6 722.6 %copy-start.110 = (f32[1024]{0:T(1024)S(1)}, f32[1024]{0:T(1024)}, u32[]{:S(2)}) copy-start(f32[1024]{0:T(1024)} %copy-done.109) | copy-start | bytes 12292
  1565.0 444.4 %copy-start.89 = (f32[1,128,1024]{2,1,0:T(8,128)S(1)}, f32[1,128,1024]{2,1,0:T(8,128)}, u32[]{:S(2)}) copy-start(f32[1,128,1024]{2,1,0:T(8,128)} %get-tuple-element.2192) | copy-start | bytes 1572868
  (99 other events, 761.5 us)
Sparse Core Ops, SparseCore 0:
  11.0 78.2 all-gather.10
  92.3 89.7 all-gather.14
  184.5 53.6 all-gather.12
  240.5 62.9 all-gather.16
  305.8 46.6 all-gather.24
  354.8 48.2 all-gather.26
  405.5 53.6 all-gather.22
  461.7 67.9 all-gather.18
  532.2 62.3 all-gather.20
  750.8 68.0 reduce-scatter.22
  827.3 69.4 reduce-scatter.24
  900.7 69.8 reduce-scatter.18
  974.5 69.8 reduce-scatter.20
  1048.4 79.9 reduce-scatter.26
  1132.8 78.8 reduce-scatter.28
  1215.7 78.9 reduce-scatter.14
  1299.1 78.9 reduce-scatter.16
  1382.1 88.3 reduce-scatter.38
  1474.6 88.3 reduce-scatter.40
  1567.0 88.3 reduce-scatter.34
  1659.5 88.3 reduce-scatter.36
  1752.0 88.2 reduce-scatter.30
  1844.5 88.3 reduce-scatter.32
  1936.7 57.3 all-reduce.17
where the time goes:
time: 2040 us; the launch traced here: 2030 us
  waiting for transfers between devices  1300 us (64%)
  local copies, waits for them, and re-layouts  224 us (11%)
  other arithmetic  166 us (8%)
  matrix products  166 us (8%)
  blocking collectives  130 us (6%)
    reduce_scatter x14, waiting for transfers between devices, on_device(): lax.psum_scatter(shortened(gradients), 'fsdp', scatter_dimension=0, tiled...  1030 us
    all_gather x2, waiting for transfers between devices, sent_together(): whole = lax.all_gather(both, axis, axis=dim, tiled=True)  84.7 us
    convert_element_type x11, other arithmetic, short(): return part.astype(jnp.bfloat16) if part.dtype == jnp.float32 else part  66.8 us
    all_gather x1, waiting for transfers between devices, on_device(): lax.all_gather(owned_shards[10], 'fsdp', axis=1, tiled=True)  65.3 us
    unnamed x1, blocking collectives  61 us
    unnamed x130, local copies, waits for them, and re-layouts  60.8 us
    another operation x34, local copies, waits for them, and re-layouts  50.1 us
    ppermute x4, waiting for transfers between devices, from_behind(): lax.ppermute(value, axis, [(source, source + steps) for source in range(i...  42.5 us
  transfers between devices with their start and end apart: 28, of which 20 were waited for; matrix products, arithmetic and copies ran while one was open for 21% of the time, Pallas kernels for 0%

commit v1 on v0

v1 whole, which is shorter than its diff:
```python
import functools

import jax
import jax.numpy as jnp
from jax import lax
from jax.experimental import pallas as pl
from jax.experimental.pallas import tpu as pltpu
from jax.sharding import PartitionSpec as P

epsilon = 1e-06
rope_base = 1000000.0
low = jnp.bfloat16
f32 = jnp.float32
MODEL = 1024
HEAD = 128
ROOT = HEAD ** (-0.5)


def swap_core(value):
    return lax.ppermute(value, "fsdp", [(i, i ^ 1) for i in range(16)])


def swap_z(value):
    return lax.ppermute(value, "fsdp", [(i, i ^ 8) for i in range(16)])


def move_y(value, step):
    pairs = [(i, (i & 8) | ((((i >> 1) + step) & 3) << 1) | (i & 1)) for i in range(16)]
    return lax.ppermute(value, "fsdp", pairs)


def move_x(value, step):
    return lax.ppermute(value, "dp", [(i, (i + step) % 4) for i in range(4)])


def move_section(value, step):
    return lax.ppermute(value, "section", [(0, 1)] if step > 0 else [(1, 0)])


def pick(value, *where):
    start = list(where) + [0] * (value.ndim - len(where))
    size = [1] * len(where) + list(value.shape[len(where) :])
    return lax.dynamic_slice(value, start, size).reshape(value.shape[len(where) :])


def half_of(value, index, axis):
    width = value.shape[axis] // 2
    return lax.dynamic_slice_in_dim(value, index * width, width, axis)


def in_order(own, other, core, axis):
    first = jnp.where(core == 0, own, other)
    second = jnp.where(core == 0, other, own)
    return jnp.concatenate([first, second], axis=axis)


def placing_kernel(counts, rows, offsets, *refs):
    sources, out, sems = refs[: len(counts)], refs[len(counts)], refs[len(counts) + 1]
    copies, k = [], 0
    for source, count in zip(sources, counts):
        for i in range(count):
            at = pl.multiple_of(offsets[k], 16)
            copies.append(pltpu.make_async_copy(source.at[i], out.at[pl.ds(at, rows)], sems.at[k]))
            k += 1
    for copy in copies:
        copy.start()
    for copy in copies:
        copy.wait()


def place(pieces, offsets, total):
    counts = tuple(p.shape[0] for p in pieces)
    rows, width = pieces[0].shape[1:]
    return pl.pallas_call(
        functools.partial(placing_kernel, counts, rows),
        out_shape=jax.ShapeDtypeStruct((total, width), pieces[0].dtype),
        in_specs=[pl.BlockSpec(memory_space=pltpu.SMEM)]
        + [pl.BlockSpec(memory_space=pl.ANY)] * len(pieces),
        out_specs=pl.BlockSpec(memory_space=pl.ANY),
        scratch_shapes=[pltpu.SemaphoreType.DMA((sum(counts),))],
        compiler_params=pltpu.CompilerParams(vmem_limit_bytes=2**20),
        cost_estimate=pl.CostEstimate(
            flops=0, bytes_accessed=4 * total * width, transcendentals=0
        ),
    )(jnp.stack(offsets).astype(jnp.int32), *pieces)


def gather_chip_rows(block, spot, by_x, flip):
    x, z, y = spot
    rows = block.shape[0]
    part = rows // 4 if by_x else rows
    piece = lax.dynamic_slice_in_dim(block, x * part, part, 0) if by_x else block
    across = swap_z(piece)
    pair = jnp.stack([piece, across])
    behind, ahead = move_y(pair, 1), move_y(pair, -1)
    far_own, far_across = move_y(behind[0], 1), move_y(ahead[1], -1)
    origin = [(0, 0), (1, 0), (0, 1), (1, 1), (0, 3), (1, 3), (0, 2), (1, 2)]
    bases = [((z ^ dz ^ flip) * 4 + ((y - dy) & 3)) * rows for dz, dy in origin]
    if not by_x:
        pieces = (pair, behind, ahead, far_own[None], far_across[None])
        return place(pieces, bases, 8 * rows)
    whole = jnp.concatenate([pair, behind, ahead, far_own[None], far_across[None]])
    x_behind, x_ahead = move_x(whole, 1), move_x(whole, -1)
    x_far_a, x_far_b = move_x(x_behind[:4], 1), move_x(x_ahead[4:], -1)
    pieces = (whole, x_behind, x_ahead, x_far_a, x_far_b)
    offsets = []
    for dx, kept in ((0, bases), (1, bases), (3, bases), (2, bases)):
        offsets += [base + ((x - dx) & 3) * part for base in kept]
    return place(pieces, offsets, 8 * rows)


def added(left, right):
    return (left.astype(f32) + right.astype(f32)).astype(low)


def reduce_x(values, x):
    cut = values.shape[1] // 2
    far = pick(values, (x + 2) & 3)
    up, down = move_x(far[:cut], 1), move_x(far[cut:], -1)
    after, before = pick(values, (x + 1) & 3), pick(values, (x - 1) & 3)
    after = jnp.concatenate([added(after[:cut], up), after[cut:]])
    before = jnp.concatenate([before[:cut], added(before[cut:], down)])
    from_behind, from_ahead = move_x(after, 1), move_x(before, -1)
    own = pick(values, x)
    return (own.astype(f32) + from_behind.astype(f32) + from_ahead.astype(f32)).astype(low)


def reduce_chips(values, z, y):
    other = 1 - z
    up = move_y(pick(values, z, (y + 2) & 3), 1)
    down = move_y(pick(values, other, (y + 2) & 3), -1)
    y_after, y_before = (y + 1) & 3, (y - 1) & 3
    after = jnp.stack([added(pick(values, z, y_after), up), pick(values, other, y_after)])
    before = jnp.stack([pick(values, z, y_before), added(pick(values, other, y_before), down)])
    from_behind, from_ahead = move_y(after, 1), move_y(before, -1)

    def total(k, zi):
        own = pick(values, zi, y)
        return (own.astype(f32) + from_behind[k].astype(f32) + from_ahead[k].astype(f32)).astype(low)

    return added(total(0, z), swap_z(total(1, other)))


def scatter_rows(gradient, spot, by_x, flip):
    x, z, y = spot
    z = z ^ flip
    rows, width = gradient.shape[0] // 8, gradient.shape[1]
    part = rows // 4
    if by_x:
        values = gradient.reshape(8, 4, part, width).transpose(1, 0, 2, 3)
        mine = reduce_x(values, x)
        return reduce_chips(mine.reshape(2, 4, part, width), z, y)
    mine = reduce_chips(gradient.reshape(2, 4, rows, width), z, y)
    return reduce_x(mine.reshape(4, part, width), x)


def gather_x(value, x):
    cut = value.shape[0] // 2
    behind, ahead = move_x(value, 1), move_x(value, -1)
    far = jnp.concatenate([move_x(behind[:cut], 1), move_x(ahead[cut:], -1)])
    ring = jnp.stack([value, ahead, far, behind, value, ahead, far, behind])
    return lax.dynamic_slice_in_dim(ring, (4 - x) & 3, 4, 0)


def packed(value):
    return jnp.concatenate([value[:, k : k + 512] for k in range(0, value.shape[1], 512)])


def unpacked(rows, part, width):
    blocks = [rows[:, k * part : (k + 1) * part] for k in range(width // 512)]
    return jnp.concatenate(blocks, axis=2).reshape(4 * part, width)


def finish(values, x, core):
    sizes = [v.shape for v in values]
    together = gather_x(jnp.concatenate([packed(v) for v in values]), x)
    chips, at = [], 0
    for part, width in sizes:
        n = part * width // 512
        chips.append(unpacked(together[:, at : at + n], part, width))
        at += n
    mine = [half_of(chip, core, 0) for chip in chips]
    theirs = [half_of(chip, 1 - core, 0) for chip in chips]
    arrived = swap_core(jnp.concatenate([packed(t) for t in theirs]))
    outs, at = [], 0
    for (part, width), own in zip(sizes, mine):
        n = 2 * part * width // 512
        rows = arrived[at : at + n]
        at += n
        other = jnp.concatenate(
            [rows[k * 2 * part : (k + 1) * 2 * part] for k in range(width // 512)], axis=1
        )
        outs.append((own.astype(f32), other.astype(f32)))
    return outs


def row_scale(values):
    return lax.rsqrt(jnp.mean(values * values, axis=-1, keepdims=True) + epsilon)


def rotation_tables(length):
    half_size = HEAD // 2
    places = jnp.arange(length, dtype=f32)
    frequencies = rope_base ** (-jnp.arange(half_size, dtype=f32) * 2.0 / HEAD)
    angles = places[:, None] * frequencies[None, :]
    return (jnp.cos(angles)[:, None, :], jnp.sin(angles)[:, None, :])


def rotate_heads(values, tables, sign):
    cosine, sine = tables
    first, second = values[..., : HEAD // 2], values[..., HEAD // 2 :]
    sine = sine * sign
    return jnp.concatenate(
        [first * cosine - second * sine, second * cosine + first * sine], axis=-1
    )


def norm_backward(upstream, normed, scaling, gain_vector):
    gain_part = jnp.sum(upstream * normed, axis=tuple(range(upstream.ndim - 1)))
    scaled = upstream * gain_vector
    return (
        scaling * (scaled - normed * jnp.mean(scaled * normed, axis=-1, keepdims=True)),
        gain_part,
    )


def dot(left, right):
    return jnp.dot(left, right, preferred_element_type=f32)


def dot_t(left, right):
    return lax.dot_general(left, right, (((1,), (1,)), ((), ())), preferred_element_type=f32)


def wide(left, pair):
    return jnp.stack([dot(left, w) for w in pair])


def forward(hidden, weights, gains, tables):
    w_qkv, w_out, w_gu, w_down = weights
    mixer_gain, query_gain, key_gain, dense_gain = gains
    tokens = hidden.shape[0]
    seqs = tokens // 128
    scale_one = row_scale(hidden)
    normed_one = hidden * scale_one
    a1 = (normed_one * mixer_gain).astype(low)
    qkv = wide(a1, w_qkv).reshape(2, seqs, 128, 16, HEAD)
    q, k, v = qkv[..., :8, :], qkv[..., 8:12, :], qkv[..., 12:, :].astype(low)
    q_scale, k_scale = row_scale(q), row_scale(k)
    qn, kn = q * q_scale, k * k_scale
    qr = rotate_heads(qn * query_gain, tables, 1.0).astype(low).reshape(2, seqs, 128, 4, 2, HEAD)
    kr = rotate_heads(kn * key_gain, tables, 1.0).astype(low)
    scores = jnp.einsum("hbqkgd,hbskd->hbkgqs", qr, kr, preferred_element_type=f32) * ROOT
    causal = jnp.arange(128)[:, None] >= jnp.arange(128)[None, :]
    p = jax.nn.softmax(jnp.where(causal, scores, -1e30), axis=-1)
    pb = p.astype(low)
    att = jnp.einsum("hbkgqs,hbskd->bqhkgd", pb, v, preferred_element_type=f32)
    att = att.astype(low).reshape(tokens, 2048)
    after = hidden + dot(att, w_out)
    scale_two = row_scale(after)
    normed_two = after * scale_two
    a2 = (normed_two * dense_gain).astype(low)
    gu = wide(a2, w_gu)
    gate, up = gu[..., :1536], gu[..., 1536:]
    z = (jax.nn.silu(gate) * up).astype(low)
    z = jnp.concatenate([z[0], z[1]], axis=-1)
    out = after + dot(z, w_down)
    saved = (
        (scale_one, normed_one, a1, q_scale, qn, k_scale, kn, qr, kr, v, p, pb, att)
        + (scale_two, normed_two, a2, gate, up, z)
    )
    return out, saved


def backward(cotangent, saved, weights, gains, tables):
    w_qkv, w_out, w_gu, w_down = weights
    mixer_gain, query_gain, key_gain, dense_gain = gains
    (scale_one, normed_one, a1, q_scale, qn, k_scale, kn, qr, kr, v, p, pb, att) = saved[:13]
    scale_two, normed_two, a2, gate, up, z = saved[13:]
    tokens = cotangent.shape[0]
    seqs = tokens // 128
    dm = cotangent.astype(low)
    dz = dot_t(dm, w_down)
    dz = jnp.stack([dz[:, :1536], dz[:, 1536:]])
    sig = jax.nn.sigmoid(gate)
    dg = (dz * up * sig * (1.0 + gate * (1.0 - sig))).astype(low)
    du = (dz * (gate * sig)).astype(low)
    dgu = jnp.concatenate([dg, du], axis=-1)
    da2 = dot_t(dgu[0], w_gu[0]) + dot_t(dgu[1], w_gu[1])
    part, dense_gain_grad = norm_backward(da2, normed_two, scale_two, dense_gain)
    dh2 = cotangent + part
    dr = dh2.astype(low)
    datt = dot_t(dr, w_out).astype(low).reshape(seqs, 128, 2, 4, 2, HEAD)
    dp = jnp.einsum("bqhkgd,hbskd->hbkgqs", datt, v, preferred_element_type=f32)
    dv = jnp.einsum("hbkgqs,bqhkgd->hbskd", pb, datt, preferred_element_type=f32).astype(low)
    ds = (p * (dp - jnp.sum(dp * p, axis=-1, keepdims=True))).astype(low)
    dqr = jnp.einsum("hbkgqs,hbskd->hbqkgd", ds, kr, preferred_element_type=f32)
    dqr = dqr.reshape(2, seqs, 128, 8, HEAD) * ROOT
    dkr = jnp.einsum("hbkgqs,hbqkgd->hbskd", ds, qr, preferred_element_type=f32) * ROOT
    dq, q_gain_grad = norm_backward(rotate_heads(dqr, tables, -1.0), qn, q_scale, query_gain)
    dk, k_gain_grad = norm_backward(rotate_heads(dkr, tables, -1.0), kn, k_scale, key_gain)
    dqkv = jnp.concatenate([dq.astype(low), dk.astype(low), dv], axis=3).reshape(2, tokens, 2048)
    da1 = dot_t(dqkv[0], w_qkv[0]) + dot_t(dqkv[1], w_qkv[1])
    part, mixer_gain_grad = norm_backward(da1, normed_one, scale_one, mixer_gain)
    dh = dh2 + part
    return dh, (dm, dgu, dr, dqkv), (mixer_gain_grad, dense_gain_grad, q_gain_grad, k_gain_grad)


def swapped_halves(value):
    cut = value.shape[1] // 2
    return jnp.concatenate([value[:, cut:], value[:, :cut]], axis=1)


def product(left, left_other, right, right_other):
    both_left = jnp.concatenate([left, left_other])
    both_right = jnp.concatenate([right, right_other])
    dims = (((0,), (0,)), ((), ()))
    return lax.dot_general(both_left, both_right, dims, preferred_element_type=f32).astype(low)


def on_device(
    boundary,
    mixer_gain,
    query_weight,
    key_weight,
    value_weight,
    output_weight,
    query_gain,
    key_gain,
    dense_gain,
    gate_weight,
    up_weight,
    down_weight,
):
    first_section = lax.axis_index("section") == 0
    x = lax.axis_index("dp")
    place_at = lax.axis_index("fsdp")
    core, y, z = place_at & 1, (place_at >> 1) & 3, place_at >> 3
    spot = (x, z, y)
    local = boundary[0, :, 0].astype(f32).reshape(256, MODEL)

    tile = jnp.stack(
        [
            mixer_gain[0],
            dense_gain[0],
            jnp.pad(query_gain[0], (0, 56)),
            jnp.pad(key_gain[0], (0, 56)),
        ]
    )
    tiles = lax.all_gather(tile, "fsdp", axis=0, tiled=False).astype(f32)
    gains = (
        tiles[:, 0].reshape(MODEL),
        tiles[:, 2, :8].reshape(HEAD),
        tiles[:, 3, :8].reshape(HEAD),
        tiles[:, 1].reshape(MODEL),
    )

    def column_half(index):
        def cat(*parts):
            return jnp.concatenate([half_of(p[0], index, 1) for p in parts], axis=1)

        return (
            cat(query_weight, key_weight, value_weight),
            cat(output_weight),
            cat(gate_weight, up_weight),
            cat(down_weight),
        )

    kept, sent = column_half(core), column_half(1 - core)
    came = [swap_core(s) for s in sent]
    chips = [in_order(k, c, core, 0) for k, c in zip(kept, came)]
    zero = jnp.zeros_like(z)
    own_qkv = gather_chip_rows(chips[0], spot, False, zero)
    own_gu = gather_chip_rows(chips[2], spot, True, zero)
    own_out = gather_chip_rows(chips[1], spot, False, core)
    own_down = gather_chip_rows(chips[3], spot, True, core)
    w_qkv = (own_qkv, swap_core(own_qkv))
    w_gu = (own_gu, swap_core(own_gu))

    def columns(own):
        other = swap_core(own)
        cut = own.shape[0] // 2
        return in_order(own, jnp.concatenate([other[cut:], other[:cut]]), core, 1)

    w_out, w_down = columns(own_out), columns(own_down)
    weights = (w_qkv, w_out, w_gu, w_down)

    tables = rotation_tables(128)
    early, _ = forward(local, weights, gains, tables)
    arrived = move_section(early.astype(low), 1).astype(f32)
    out, saved = forward(jnp.where(first_section, local, arrived), weights, gains, tables)
    a1, att, a2, z_low = saved[2], saved[12], saved[15], saved[18]
    early_dh, _, _ = backward(local, saved, weights, gains, tables)
    returned = move_section(early_dh.astype(low), -1).astype(f32)
    cotangent = jnp.where(first_section, returned, local)
    dh, (dm, dgu, dr, dqkv), gain_grads = backward(cotangent, saved, weights, gains, tables)
    endpoints = jnp.where(first_section, dh, out).reshape(1, 2, 1, 128, MODEL)

    a1_o, att_o, a2_o, z_o = [swap_core(v) for v in (a1, att, a2, z_low)]
    att_o, z_o = swapped_halves(att_o), swapped_halves(z_o)
    dm_mine, dr_mine = half_of(dm, core, 1), half_of(dr, core, 1)
    g_down = product(z_low, z_o, dm_mine, swap_core(half_of(dm, 1 - core, 1)))
    g_gu = product(a2, a2_o, dgu[0], swap_core(dgu[1]))
    g_out = product(att, att_o, dr_mine, swap_core(half_of(dr, 1 - core, 1)))
    g_qkv = product(a1, a1_o, dqkv[0], swap_core(dqkv[1]))
    s_gu = scatter_rows(g_gu, spot, True, zero)
    s_down = scatter_rows(g_down, spot, False, core)
    s_out = scatter_rows(g_out, spot, False, core)
    s_qkv = scatter_rows(g_qkv, spot, False, zero)
    (gu, down), (out_w, qkv) = finish((s_gu, s_down), x, core), finish((s_out, s_qkv), x, core)

    def both(pair, start, width):
        return in_order(*(p[:, start : start + width] for p in pair), core, 1)[None]

    sums = lax.psum(jnp.concatenate(gain_grads).reshape(18, 128), ("dp", "fsdp")).reshape(-1)

    def gain_rows(start, width):
        return lax.dynamic_slice_in_dim(sums, start + place_at * width, width, 0)[None]

    return (
        endpoints,
        gain_rows(0, 64),
        both(qkv, 0, 1024),
        both(qkv, 1024, 512),
        both(qkv, 1536, 512),
        both(out_w, 0, 512),
        gain_rows(2048, 8),
        gain_rows(2176, 8),
        gain_rows(1024, 64),
        both(gu, 0, 1536),
        both(gu, 1536, 1536),
        both(down, 0, 512),
    )


def solution(mesh):
    placed = (
        P("section", None, ("dp", "fsdp"), None, None),
        P("section", "fsdp"),
        P("section", "fsdp", None),
        P("section", "fsdp", None),
        P("section", "fsdp", None),
        P("section", "fsdp", None),
        P("section", "fsdp"),
        P("section", "fsdp"),
        P("section", "fsdp"),
        P("section", "fsdp", None),
        P("section", "fsdp", None),
        P("section", "fsdp", None),
    )
    return jax.shard_map(
        on_device,
        mesh=mesh,
        in_specs=placed,
        out_specs=(
            P("section", None, ("dp", "fsdp"), None, None),
            P("section", "fsdp"),
            P("section", "fsdp", None),
            P("section", "fsdp", None),
            P("section", "fsdp", None),
            P("section", "fsdp", None),
            P("section", "fsdp"),
            P("section", "fsdp"),
            P("section", "fsdp"),
            P("section", "fsdp", None),
            P("section", "fsdp", None),
            P("section", "fsdp", None),
        ),
        check_vma=False,
    )
```

time: 2040 us -> 1210 us (0.59)
  waiting for transfers between devices: 1300 us -> 182 us
  blocking collectives: 130 us -> 351 us
  Pallas kernels: 0 us -> 217 us
  starting transfers between devices: 6.13 us -> 131 us
  local copies, waits for them, and re-layouts: 224 us -> 110 us
  other arithmetic: 166 us -> 58 us
    reduce_scatter x14 -> x0, waiting for transfers between devices: 1030 us -> none  [on_device(): lax.psum_scatter(shortened(gradients), 'fsdp', scatter_dimension=0, tiled...]
    psum x1, blocking collectives: 8.7 us -> 322 us  [on_device(): lax.psum(jnp.concatenate(gain_grads).reshape(18, 128), ('dp', 'fsdp'))]
    pallas_call x0 -> x4, Pallas kernels: none -> 217 us  [place(): pl.pallas_call(functools.partial(placing_kernel, counts, rows), out_shape...]
    all_gather x9 -> x0, waiting for transfers between devices: 217 us -> none  [the longest x2 84.7 us: sent_together(): whole = lax.all_gather(both, axis, axis=dim, tiled=True)]
    ppermute x4 -> x92, waiting for transfers between devices: 42.5 us -> 182 us  [the longest x32 74.9 us: move_y(): return lax.ppermute(value, 'fsdp', pairs)]
    ppermute x4 -> x92, starting transfers between devices: 5.18 us -> 131 us  [the longest x18 40.2 us: swap_core(): return lax.ppermute(value, 'fsdp', [(i, i ^ 1) for i in range(16)])]
    another operation x72 -> x11, local copies, waits for them, and re-layouts: 91.1 us -> 7.45 us  [the longest x2 4.89 us: wide(): return jnp.stack([dot(left, w) for w in pair])]
    unnamed x1 -> x0, blocking collectives: 61 us -> none
  transfers between devices with their start and end apart: 28 -> 92, of which waited for: 20 -> 37; matrix products, arithmetic and copies ran while one was open for 21% -> 15% of each run, Pallas kernels for 0% -> 18%
where the time goes in v1:
time: 1210 us; the launch traced here: 1200 us
  blocking collectives  351 us (29%)
  Pallas kernels  217 us (18%)
  waiting for transfers between devices  182 us (15%)
  matrix products  147 us (12%)
  starting transfers between devices  131 us (11%)
  local copies, waits for them, and re-layouts  110 us (9%)
  other arithmetic  58 us (5%)
    psum x1, blocking collectives, on_device(): lax.psum(jnp.concatenate(gain_grads).reshape(18, 128), ('dp', 'fsdp'))  322 us
    pallas_call x4, Pallas kernels, place(): pl.pallas_call(functools.partial(placing_kernel, counts, rows), out_shape...  217 us
    ppermute x32, waiting for transfers between devices, move_y(): return lax.ppermute(value, 'fsdp', pairs)  74.9 us
    ppermute x32, waiting for transfers between devices, move_x(): return lax.ppermute(value, 'dp', [(i, (i + step) % 4) for i in range(4)])  55.1 us
    dot_general x12, matrix products, dot(): return jnp.dot(left, right, preferred_element_type=f32)  49.5 us
    dot_general x12, matrix products, dot_t(): lax.dot_general(left, right, (((1,), (1,)), ((), ())), preferred_element_...  48.1 us
    ppermute x18, starting transfers between devices, swap_core(): return lax.ppermute(value, 'fsdp', [(i, i ^ 1) for i in range(16)])  40.2 us
    ppermute x32, starting transfers between devices, move_y(): return lax.ppermute(value, 'fsdp', pairs)  38.4 us
  transfers between devices with their start and end apart: 92, of which 37 were waited for; matrix products, arithmetic and copies ran while one was open for 15% of the time, Pallas kernels for 18%

profile of v1, /device:TPU:1, one launch (start us, length us, event | category | flops | bytes accessed | tf_op | source)
XLA Modules:
  0.0 1200.8 jit_solution(14442438337305844722)
XLA Ops:
  6.8 3.8 collective-permute-start.8
  15.0 4.3 collective-permute-done.26
  45.5 4.3 collective-permute-done.16
  53.0 23.5 %collective-permute-done.18 = bf16[32,3072]{1,0:T(8,128)(2,1)S(1)} collective-permute-done((bf16[32,3072]{1,0:T(8,128)(2,1)S(1)}, bf16[32,3072]{1,0:T(8,128)(2,1)S(1)}, u32[]{:S(2)}, u32[]{:S(2)}) %collective-permute-start.18) | collective-permute-done | bytes 196640 | tf_op jit(solution)/shard_map/ppermute | solution.py:29
  92.4 4.3 collective-permute-start.13
  96.8 5.4 shard_map.214
  108.4 29.3 %all-gather.1 = bf16[16,4,64]{2,1,0:T(4,128)(2,1)S(1)} all-gather(bf16[1,4,64]{2,1,0:T(4,128)(2,1)S(1)} %maximum_bitcast_fusion.23), channel_id=2, replica_groups=mesh['section'=2,'dp'=4,'fsdp'=16] {'fsdp'}, dimensions={0}, use_global_device_ids=true | all-gather | bytes 8704 | tf_op jit(solution)/shard_map/all_gather | solution.py:350
  142.6 17.6 %shard_map.211 = bf16[1024,2048]{1,0:T(8,128)(2,1)} custom-call(s32[8]{0:T(128)S(1)} %stack.444.offsets, bf16[2,128,2048]{2,1,0:T(8,128)(2,1)S(1)} %copy-done.1, bf16[2,128,2048]{2,1,0:T(8,128)(2,1)S(1)} %copy-done.3, bf16[2,128,2048]{2,1,0:T(8,128)(2,1)S(1)} %copy-done.5, bf16[1,128,2048]{2,1,0:T(8,128)(2,1)S(1)} %bitcast.776, ...), custom_call_target="tpu_custom_call" | custom-call | bytes 8388608 | tf_op jit(solution)/shard_map/pallas_call | solution.py:74
  169.9 6.4 copy.147
  176.3 5.1 convolution_bitcast_fusion.8
  185.9 192.5 %shard_map.213 = bf16[1024,3072]{1,0:T(8,128)(2,1)} custom-call(s32[32]{0:T(128)S(1)} %stack.493.offsets, bf16[8,32,3072]{2,1,0:T(8,128)(2,1)} %bitcast_dynamic-update-slice_fusion.12.refs_0_, bf16[8,32,3072]{2,1,0:T(8,128)(2,1)} %collective-permute-done.20.refs_1_, bf16[8,32,3072]{2,1,0:T(8,128)(2,1)} %collective-permute-done.21.refs_2_, ...), custom_call_target="tpu_custom_call" | custom-call | bytes 12582912 | tf_op jit(solution)/shard_map/pallas_call | solution.py:74
  380.0 4.3 broadcast_select_fusion.3
  391.8 6.5 copy.148
  411.1 4.1 fusion.212
  425.4 4.6 convolution_bitcast_fusion.4
  430.1 4.6 convolution_bitcast_fusion.3
  444.1 9.4 collective-permute-done.36
  454.1 4.9 convolution_bitcast_fusion.6
  466.2 4.1 copy.163
  484.1 4.2 fusion.215
  500.2 4.1 multiply_reduce_fusion.14
  504.5 5.0 convolution_bitcast_fusion.1
  509.5 5.7 convolution_bitcast_fusion
  517.7 4.7 fusion.43
  522.4 4.9 multiply_reduce_fusion.13
  555.5 3.9 fusion.84
  566.6 12.8 %collective-permute-done.37 = bf16[256,1024]{1,0:T(8,128)(2,1)} collective-permute-done((bf16[256,1024]{1,0:T(8,128)(2,1)}, bf16[256,1024]{1,0:T(8,128)(2,1)}, u32[]{:S(2)}, u32[]{:S(2)}) %collective-permute-start.37) | collective-permute-done | bytes 524320 | tf_op jit(solution)/shard_map/ppermute | solution.py:37
  580.8 4.2 fusion.199
  592.5 5.7 fusion.216
  598.2 5.5 multiply_reduce_fusion.6
  637.2 3.9 multiply_reduce_fusion.7
  650.5 321.6 %psum.7 = f32[2304]{0:T(1024)S(1)} all-reduce(f32[2304]{0:T(1024)S(1)} %pad_maximum_fusion.47), channel_id=1, replica_groups=mesh['section'=2,'dp'=4,'fsdp'=16] {'dp','fsdp'}, use_global_device_ids=true, to_apply=%region_26.27 | all-reduce | flops 2304 | bytes 18432 | tf_op jit(solution)/shard_map/psum | solution.py:415
  977.4 4.4 collective-permute-done.43
  981.8 9.2 collective-permute-start.65
  994.0 3.8 convolution_convert_fusion.2
  998.1 4.9 collective-permute-done.44
  1006.9 5.1 convolution_convert_fusion
  1015.7 12.5 %convolution_convert_fusion.1 = bf16[3072,512]{1,0:T(8,128)(2,1)S(1)} fusion(bf16[256,1536]{1,0:T(8,128)(2,1)S(1)} %get-tuple-element.131, bf16[256,1536]{1,0:T(8,128)(2,1)S(1)} %get-tuple-element.130, bf16[256,1536]{1,0:T(8,128)(2,1)S(1)} %get-tuple-element.145, bf16[256,1536]{1,0:T(8,128)(2,1)S(1)} %get-tuple-element.144, ...), kind=kOutput, calls=%fused_computation.16 | convolution fusion | flops 1625817088 | bytes 6815744 | tf_op jit(solution)/shard_map/dot_general | solution.py:318
  1041.4 13.2 %collective-permute-done.67 = bf16[4,32,3072]{2,1,0:T(8,128)(2,1)S(1)} collective-permute-done((bf16[4,32,3072]{2,1,0:T(8,128)(2,1)S(1)}, bf16[4,32,3072]{2,1,0:T(8,128)(2,1)S(1)}, u32[]{:S(2)}, u32[]{:S(2)}) %collective-permute-start.67) | collective-permute-done | bytes 786464 | tf_op jit(solution)/shard_map/ppermute | solution.py:33
  1055.0 21.5 %collective-permute-done.81 = bf16[2,384,512]{2,1,0:T(8,128)(2,1)S(1)} collective-permute-done((bf16[2,384,512]{2,1,0:T(8,128)(2,1)S(1)}, bf16[2,384,512]{2,1,0:T(8,128)(2,1)S(1)}, u32[]{:S(2)}, u32[]{:S(2)}) %collective-permute-start.81) | collective-permute-done | bytes 786464 | tf_op jit(solution)/shard_map/ppermute | solution.py:29
  1087.9 8.2 collective-permute-done.55
  1099.2 14.6 %collective-permute-done.83 = bf16[48,512]{1,0:T(8,128)(2,1)S(1)} collective-permute-done((bf16[48,512]{1,0:T(8,128)(2,1)S(1)}, bf16[48,512]{1,0:T(8,128)(2,1)S(1)}, u32[]{:S(2)}, u32[]{:S(2)}) %collective-permute-start.83) | collective-permute-done | bytes 49184 | tf_op jit(solution)/shard_map/ppermute | solution.py:33
  1125.1 4.1 collective-permute-done.60
  1134.7 11.8 collective-permute-start.64
  1152.2 5.0 collective-permute-done.71
  1161.6 5.9 collective-permute-done.74
  1171.3 5.6 collective-permute-done.75
  1190.0 5.5 collective-permute-start.91
  (628 shorter events, 335.9 us)
Async XLA Ops:
  5.5 16.8 %collective-permute-start.14 = (bf16[64,3072]{1,0:T(8,128)(2,1)S(1)}, bf16[64,3072]{1,0:T(8,128)(2,1)}, u32[]{:S(2)}, u32[]{:S(2)}) collective-permute-start(bf16[64,3072]{1,0:T(8,128)(2,1)S(1)} %pad_maximum_fusion.31), channel_id=1, source_target_pairs={{0,1},{1,0},{2,3},{3,2},{4,5},{5,4},{6,7},{7,6},{8,9},{9,8},{10,11... | collective-permute-start | bytes 1179656 | tf_op jit(solution)/shard_map/ppermute | solution.py:20
  12.8 29.6 %collective-permute-start.1 = (bf16[128,2048]{1,0:T(8,128)(2,1)S(1)}, bf16[128,2048]{1,0:T(8,128)(2,1)S(1)}, u32[]{:S(2)}, u32[]{:S(2)}) collective-permute-start(bf16[128,2048]{1,0:T(8,128)(2,1)S(1)} %get-tuple-element.184), channel_id=1, source_target_pairs={{0,8},{1,9},{2,10},{3,11},{4,12},{5,13},{6,14},{7,15},{8,0},{9,1},... | collective-permute-start | bytes 1572872 | tf_op jit(solution)/shard_map/ppermute | solution.py:24
  22.2 21.6 %collective-permute-start.9 = (bf16[2,256,512]{2,1,0:T(8,128)(2,1)S(1)}, bf16[2,256,512]{2,1,0:T(8,128)(2,1)S(1)}, u32[]{:S(2)}, u32[]{:S(2)}) collective-permute-start(bf16[2,256,512]{2,1,0:T(8,128)(2,1)S(1)} %pad_maximum_fusion.26.refs_0_), channel_id=1, source_target_pairs={{0,2},{1,3},{2,4},{3,5},{4,6},{5,7},{6,0},{7,1},{8,10},{9,11},{10,... | collective-permute-start | bytes 1572872 | tf_op jit(solution)/shard_map/ppermute | solution.py:29
  22.3 23.0 %collective-permute-start.10 = (bf16[2,256,512]{2,1,0:T(8,128)(2,1)S(1)}, bf16[2,256,512]{2,1,0:T(8,128)(2,1)S(1)}, u32[]{:S(2)}, u32[]{:S(2)}) collective-permute-start(bf16[2,256,512]{2,1,0:T(8,128)(2,1)S(1)} %pad_maximum_fusion.26.refs_0_), channel_id=1, source_target_pairs={{0,6},{1,7},{2,0},{3,1},{4,2},{5,3},{6,4},{7,5},{8,14},{9,15},{10,... | collective-permute-start | bytes 1572872 | tf_op jit(solution)/shard_map/ppermute | solution.py:29
  42.4 34.8 %collective-permute-start.31 = (bf16[8,96,512]{2,1,0:T(8,128)(2,1)S(1)}, bf16[8,96,512]{2,1,0:T(8,128)(2,1)S(1)}, u32[]{:S(2)}, u32[]{:S(2)}) collective-permute-start(bf16[8,96,512]{2,1,0:T(8,128)(2,1)S(1)} %constant_dynamic-update-slice_fusion.4.refs_0_), channel_id=1, source_target_pairs={{0,16},{16,32},{32,48},{48,0},{1,17},{17,33},{33,49},{49,1},{2,18}... | collective-permute-start | bytes 2359304 | tf_op jit(solution)/shard_map/ppermute | solution.py:33
  43.8 36.1 %collective-permute-start.32 = (bf16[8,96,512]{2,1,0:T(8,128)(2,1)S(1)}, bf16[8,96,512]{2,1,0:T(8,128)(2,1)S(1)}, u32[]{:S(2)}, u32[]{:S(2)}) collective-permute-start(bf16[8,96,512]{2,1,0:T(8,128)(2,1)S(1)} %constant_dynamic-update-slice_fusion.4.refs_0_), channel_id=1, source_target_pairs={{0,48},{16,0},{32,16},{48,32},{1,49},{17,1},{33,17},{49,33},{2,50}... | collective-permute-start | bytes 2359304 | tf_op jit(solution)/shard_map/ppermute | solution.py:33
  45.4 34.7 %collective-permute-start.2 = (bf16[2,128,2048]{2,1,0:T(8,128)(2,1)S(1)}, bf16[2,128,2048]{2,1,0:T(8,128)(2,1)S(1)}, u32[]{:S(2)}, u32[]{:S(2)}) collective-permute-start(bf16[2,128,2048]{2,1,0:T(8,128)(2,1)S(1)} %pad_maximum_fusion.18.refs_0_), channel_id=1, source_target_pairs={{0,2},{1,3},{2,4},{3,5},{4,6},{5,7},{6,0},{7,1},{8,10},{9,11},{10,... | collective-permute-start | bytes 3145736 | tf_op jit(solution)/shard_map/ppermute | solution.py:29
  49.8 52.4 %collective-permute-start.3 = (bf16[2,128,2048]{2,1,0:T(8,128)(2,1)S(1)}, bf16[2,128,2048]{2,1,0:T(8,128)(2,1)S(1)}, u32[]{:S(2)}, u32[]{:S(2)}) collective-permute-start(bf16[2,128,2048]{2,1,0:T(8,128)(2,1)S(1)} %pad_maximum_fusion.18.refs_0_), channel_id=1, source_target_pairs={{0,6},{1,7},{2,0},{3,1},{4,2},{5,3},{6,4},{7,5},{8,14},{9,15},{10,... | collective-permute-start | bytes 3145736 | tf_op jit(solution)/shard_map/ppermute | solution.py:29
  49.8 26.7 %collective-permute-start.18 = (bf16[32,3072]{1,0:T(8,128)(2,1)S(1)}, bf16[32,3072]{1,0:T(8,128)(2,1)S(1)}, u32[]{:S(2)}, u32[]{:S(2)}) collective-permute-start(bf16[32,3072]{1,0:T(8,128)(2,1)S(1)} %slice_bitcast_fusion.35), channel_id=1, source_target_pairs={{0,2},{1,3},{2,4},{3,5},{4,6},{5,7},{6,0},{7,1},{8,10},{9,11},{10,... | collective-permute-start | bytes 589832 | tf_op jit(solution)/shard_map/ppermute | solution.py:29
  86.8 17.3 %collective-permute-start.4 = (bf16[128,2048]{1,0:T(8,128)(2,1)S(1)}, bf16[128,2048]{1,0:T(8,128)(2,1)S(1)}, u32[]{:S(2)}, u32[]{:S(2)}) collective-permute-start(bf16[128,2048]{1,0:T(8,128)(2,1)S(1)} %slice_bitcast_fusion.19), channel_id=1, source_target_pairs={{0,2},{1,3},{2,4},{3,5},{4,6},{5,7},{6,0},{7,1},{8,10},{9,11},{10,... | collective-permute-start | bytes 1572872 | tf_op jit(solution)/shard_map/ppermute | solution.py:29
  87.5 75.0 %collective-permute-start.20 = (bf16[8,32,3072]{2,1,0:T(8,128)(2,1)}, bf16[8,32,3072]{2,1,0:T(8,128)(2,1)}, u32[]{:S(2)}, u32[]{:S(2)}) collective-permute-start(bf16[8,32,3072]{2,1,0:T(8,128)(2,1)} %bitcast_dynamic-update-slice_fusion.12.refs_0_), channel_id=1, source_target_pairs={{0,16},{16,32},{32,48},{48,0},{1,17},{17,33},{33,49},{49,1},{2,18}... | collective-permute-start | bytes 4718600 | tf_op jit(solution)/shard_map/ppermute | solution.py:33
  90.7 73.8 %collective-permute-start.21 = (bf16[8,32,3072]{2,1,0:T(8,128)(2,1)}, bf16[8,32,3072]{2,1,0:T(8,128)(2,1)}, u32[]{:S(2)}, u32[]{:S(2)}) collective-permute-start(bf16[8,32,3072]{2,1,0:T(8,128)(2,1)} %bitcast_dynamic-update-slice_fusion.12.refs_0_), channel_id=1, source_target_pairs={{0,48},{16,0},{32,16},{48,32},{1,49},{17,1},{33,17},{49,33},{2,50}... | collective-permute-start | bytes 4718600 | tf_op jit(solution)/shard_map/ppermute | solution.py:33
  92.4 88.9 %collective-permute-start.13 = (bf16[2048,512]{1,0:T(8,128)(2,1)}, bf16[2048,512]{1,0:T(8,128)(2,1)}, u32[]{:S(2)}, u32[]{:S(2)}) collective-permute-start(bf16[2048,512]{1,0:T(8,128)(2,1)} %shard_map.212), channel_id=1, source_target_pairs={{0,1},{1,0},{2,3},{3,2},{4,5},{5,4},{6,7},{7,6},{8,9},{9,8},{10,11... | collective-permute-start | bytes 6291464 | tf_op jit(solution)/shard_map/ppermute | solution.py:20
  102.2 282.1 %collective-permute-start.35 = (bf16[3072,512]{1,0:T(8,128)(2,1)S(1)}, bf16[3072,512]{1,0:T(8,128)(2,1)}, u32[]{:S(2)}, u32[]{:S(2)}) collective-permute-start(bf16[3072,512]{1,0:T(8,128)(2,1)S(1)} %shard_map.214), channel_id=1, source_target_pairs={{0,1},{1,0},{2,3},{3,2},{4,5},{5,4},{6,7},{7,6},{8,9},{9,8},{10,11... | collective-permute-start | bytes 9437192 | tf_op jit(solution)/shard_map/ppermute | solution.py:20
  104.9 33.0 %collective-permute-start.5 = (bf16[128,2048]{1,0:T(8,128)(2,1)}, bf16[128,2048]{1,0:T(8,128)(2,1)}, u32[]{:S(2)}, u32[]{:S(2)}) collective-permute-start(bf16[128,2048]{1,0:T(8,128)(2,1)} %slice_bitcast_fusion.18), channel_id=1, source_target_pairs={{0,6},{1,7},{2,0},{3,1},{4,2},{5,3},{6,4},{7,5},{8,14},{9,15},{10,... | collective-permute-start | bytes 1572872 | tf_op jit(solution)/shard_map/ppermute | solution.py:29
  160.2 231.6 %collective-permute-start.6 = (bf16[1024,2048]{1,0:T(8,128)(2,1)}, bf16[1024,2048]{1,0:T(8,128)(2,1)}, u32[]{:S(2)}, u32[]{:S(2)}) collective-permute-start(bf16[1024,2048]{1,0:T(8,128)(2,1)} %shard_map.211), channel_id=1, source_target_pairs={{0,1},{1,0},{2,3},{3,2},{4,5},{5,4},{6,7},{7,6},{8,9},{9,8},{10,11... | collective-permute-start | bytes 12582920 | tf_op jit(solution)/shard_map/ppermute | solution.py:20
  164.5 20.3 %collective-permute-start.22 = (bf16[4,32,3072]{2,1,0:T(8,128)(2,1)}, bf16[4,32,3072]{2,1,0:T(8,128)(2,1)}, u32[]{:S(2)}, u32[]{:S(2)}) collective-permute-start(bf16[4,32,3072]{2,1,0:T(8,128)(2,1)} %slice.782), channel_id=1, source_target_pairs={{0,16},{16,32},{32,48},{48,0},{1,17},{17,33},{33,49},{49,1},{2,18}... | collective-permute-start | bytes 2359304 | tf_op jit(solution)/shard_map/ppermute | solution.py:33
  166.6 19.3 %collective-permute-start.23 = (bf16[4,32,3072]{2,1,0:T(8,128)(2,1)}, bf16[4,32,3072]{2,1,0:T(8,128)(2,1)}, u32[]{:S(2)}, u32[]{:S(2)}) collective-permute-start(bf16[4,32,3072]{2,1,0:T(8,128)(2,1)} %slice.783), channel_id=1, source_target_pairs={{0,48},{16,0},{32,16},{48,32},{1,49},{17,1},{33,17},{49,33},{2,50}... | collective-permute-start | bytes 2359304 | tf_op jit(solution)/shard_map/ppermute | solution.py:33
  378.4 51.6 %collective-permute-start.24 = (bf16[1024,3072]{1,0:T(8,128)(2,1)}, bf16[1024,3072]{1,0:T(8,128)(2,1)}, u32[]{:S(2)}, u32[]{:S(2)}) collective-permute-start(bf16[1024,3072]{1,0:T(8,128)(2,1)} %shard_map.213), channel_id=1, source_target_pairs={{0,1},{1,0},{2,3},{3,2},{4,5},{5,4},{6,7},{7,6},{8,9},{9,8},{10,11... | collective-permute-start | bytes 18874376 | tf_op jit(solution)/shard_map/ppermute | solution.py:20
  565.6 75.6 %collective-permute-start.38 = (bf16[256,2048]{1,0:T(8,128)(2,1)}, bf16[256,2048]{1,0:T(8,128)(2,1)}, u32[]{:S(2)}, u32[]{:S(2)}) collective-permute-start(bf16[256,2048]{1,0:T(8,128)(2,1)} %reshape.531), channel_id=1, source_target_pairs={{0,1},{1,0},{2,3},{3,2},{4,5},{5,4},{6,7},{7,6},{8,9},{9,8},{10,11... | collective-permute-start | bytes 3145736 | tf_op jit(solution)/shard_map/ppermute | solution.py:20
  566.5 427.3 %collective-permute-start.49 = (bf16[256,1024]{1,0:T(8,128)(2,1)}, bf16[256,1024]{1,0:T(8,128)(2,1)}, u32[]{:S(2)}, u32[]{:S(2)}) collective-permute-start(bf16[256,1024]{1,0:T(8,128)(2,1)} %copy-done.68), channel_id=1, source_target_pairs={{0,1},{1,0},{2,3},{3,2},{4,5},{5,4},{6,7},{7,6},{8,9},{9,8},{10,11... | collective-permute-start | bytes 1572872 | tf_op jit(solution)/shard_map/ppermute | solution.py:20
  625.1 381.8 %collective-permute-start.66 = (bf16[256,3072]{1,0:T(8,128)(2,1)}, bf16[256,3072]{1,0:T(8,128)(2,1)}, u32[]{:S(2)}, u32[]{:S(2)}) collective-permute-start(bf16[256,3072]{1,0:T(8,128)(2,1)} %get-tuple-element.99), channel_id=1, source_target_pairs={{0,1},{1,0},{2,3},{3,2},{4,5},{5,4},{6,7},{7,6},{8,9},{9,8},{10,11... | collective-permute-start | bytes 4718600 | tf_op jit(solution)/shard_map/ppermute | solution.py:20
  633.2 360.7 %collective-permute-start.50 = (bf16[256,2048]{1,0:T(8,128)(2,1)}, bf16[256,2048]{1,0:T(8,128)(2,1)}, u32[]{:S(2)}, u32[]{:S(2)}) collective-permute-start(bf16[256,2048]{1,0:T(8,128)(2,1)} %bitcast.774), channel_id=1, source_target_pairs={{0,1},{1,0},{2,3},{3,2},{4,5},{5,4},{6,7},{7,6},{8,9},{9,8},{10,11... | collective-permute-start | bytes 3145736 | tf_op jit(solution)/shard_map/ppermute | solution.py:20
  645.0 327.3 %collective-permute-start.40 = (bf16[256,512]{1,0:T(8,128)(2,1)}, bf16[256,512]{1,0:T(8,128)(2,1)}, u32[]{:S(2)}, u32[]{:S(2)}) collective-permute-start(bf16[256,512]{1,0:T(8,128)(2,1)} %get-tuple-element.116), channel_id=1, source_target_pairs={{0,2},{1,3},{2,4},{3,5},{4,6},{5,7},{6,0},{7,1},{8,10},{9,11},{10,... | collective-permute-start | bytes 786440 | tf_op jit(solution)/shard_map/ppermute | solution.py:29
  645.0 327.3 %collective-permute-start.42 = (bf16[256,512]{1,0:T(8,128)(2,1)}, bf16[256,512]{1,0:T(8,128)(2,1)}, u32[]{:S(2)}, u32[]{:S(2)}) collective-permute-start(bf16[256,512]{1,0:T(8,128)(2,1)} %get-tuple-element.117), channel_id=1, source_target_pairs={{0,6},{1,7},{2,0},{3,1},{4,2},{5,3},{6,4},{7,5},{8,14},{9,15},{10,... | collective-permute-start | bytes 786440 | tf_op jit(solution)/shard_map/ppermute | solution.py:29
  973.8 17.2 %collective-permute-start.41 = (bf16[2,256,512]{2,1,0:T(8,128)(2,1)S(1)}, bf16[2,256,512]{2,1,0:T(8,128)(2,1)S(1)}, u32[]{:S(2)}, u32[]{:S(2)}) collective-permute-start(bf16[2,256,512]{2,1,0:T(8,128)(2,1)S(1)} %pad_maximum_fusion.27), channel_id=1, source_target_pairs={{0,2},{1,3},{2,4},{3,5},{4,6},{5,7},{6,0},{7,1},{8,10},{9,11},{10,... | collective-permute-start | bytes 1572872 | tf_op jit(solution)/shard_map/ppermute | solution.py:29
  981.8 22.8 %collective-permute-start.65 = (bf16[256,1024]{1,0:T(8,128)(2,1)S(1)}, bf16[256,1024]{1,0:T(8,128)(2,1)S(1)}, u32[]{:S(2)}, u32[]{:S(2)}) collective-permute-start(bf16[256,1024]{1,0:T(8,128)(2,1)S(1)} %copy-done.71), channel_id=1, source_target_pairs={{0,1},{1,0},{2,3},{3,2},{4,5},{5,4},{6,7},{7,6},{8,9},{9,8},{10,11... | collective-permute-start | bytes 1572872 | tf_op jit(solution)/shard_map/ppermute | solution.py:20
  991.0 21.6 %collective-permute-start.76 = (bf16[256,3072]{1,0:T(8,128)(2,1)S(1)}, bf16[256,3072]{1,0:T(8,128)(2,1)S(1)}, u32[]{:S(2)}, u32[]{:S(2)}) collective-permute-start(bf16[256,3072]{1,0:T(8,128)(2,1)S(1)} %pad_maximum_fusion.15), channel_id=1, source_target_pairs={{0,1},{1,0},{2,3},{3,2},{4,5},{5,4},{6,7},{7,6},{8,9},{9,8},{10,11... | collective-permute-start | bytes 4718600 | tf_op jit(solution)/shard_map/ppermute | solution.py:20
  993.8 21.6 %collective-permute-start.77 = (bf16[256,512]{1,0:T(8,128)(2,1)S(1)}, bf16[256,512]{1,0:T(8,128)(2,1)S(1)}, u32[]{:S(2)}, u32[]{:S(2)}) collective-permute-start(bf16[256,512]{1,0:T(8,128)(2,1)S(1)} %get-tuple-element.172), channel_id=1, source_target_pairs={{0,1},{1,0},{2,3},{3,2},{4,5},{5,4},{6,7},{7,6},{8,9},{9,8},{10,11... | collective-permute-start | bytes 786440 | tf_op jit(solution)/shard_map/ppermute | solution.py:20
  1003.0 25.4 %collective-permute-start.51 = (bf16[128,2048]{1,0:T(8,128)(2,1)S(1)}, bf16[128,2048]{1,0:T(8,128)(2,1)S(1)}, u32[]{:S(2)}, u32[]{:S(2)}) collective-permute-start(bf16[128,2048]{1,0:T(8,128)(2,1)S(1)} %get-tuple-element.86), channel_id=1, source_target_pairs={{0,2},{1,3},{2,4},{3,5},{4,6},{5,7},{6,0},{7,1},{8,10},{9,11},{10,... | collective-permute-start | bytes 1572872 | tf_op jit(solution)/shard_map/ppermute | solution.py:29
  1004.6 23.9 %collective-permute-start.53 = (bf16[128,2048]{1,0:T(8,128)(2,1)S(1)}, bf16[128,2048]{1,0:T(8,128)(2,1)S(1)}, u32[]{:S(2)}, u32[]{:S(2)}) collective-permute-start(bf16[128,2048]{1,0:T(8,128)(2,1)S(1)} %get-tuple-element.87), channel_id=1, source_target_pairs={{0,6},{1,7},{2,0},{3,1},{4,2},{5,3},{6,4},{7,5},{8,14},{9,15},{10,... | collective-permute-start | bytes 1572872 | tf_op jit(solution)/shard_map/ppermute | solution.py:29
  1006.8 24.8 %collective-permute-start.45 = (bf16[32,512]{1,0:T(8,128)(2,1)S(1)}, bf16[32,512]{1,0:T(8,128)(2,1)S(1)}, u32[]{:S(2)}, u32[]{:S(2)}) collective-permute-start(bf16[32,512]{1,0:T(8,128)(2,1)S(1)} %get-tuple-element.205), channel_id=1, source_target_pairs={{0,16},{16,32},{32,48},{48,0},{1,17},{17,33},{33,49},{49,1},{2,18}... | collective-permute-start | bytes 98312 | tf_op jit(solution)/shard_map/ppermute | solution.py:33
  1012.6 19.1 %collective-permute-start.47 = (bf16[32,512]{1,0:T(8,128)(2,1)S(1)}, bf16[32,512]{1,0:T(8,128)(2,1)S(1)}, u32[]{:S(2)}, u32[]{:S(2)}) collective-permute-start(bf16[32,512]{1,0:T(8,128)(2,1)S(1)} %get-tuple-element.207), channel_id=1, source_target_pairs={{0,48},{16,0},{32,16},{48,32},{1,49},{17,1},{33,17},{49,33},{2,50}... | collective-permute-start | bytes 98312 | tf_op jit(solution)/shard_map/ppermute | solution.py:33
  1015.5 25.4 %collective-permute-start.69 = (bf16[4,32,3072]{2,1,0:T(8,128)(2,1)S(1)}, bf16[4,32,3072]{2,1,0:T(8,128)(2,1)S(1)}, u32[]{:S(2)}, u32[]{:S(2)}) collective-permute-start(bf16[4,32,3072]{2,1,0:T(8,128)(2,1)S(1)} %get-tuple-element.139), channel_id=1, source_target_pairs={{0,48},{16,0},{32,16},{48,32},{1,49},{17,1},{33,17},{49,33},{2,50}... | collective-permute-start | bytes 2359304 | tf_op jit(solution)/shard_map/ppermute | solution.py:33
  1036.0 41.5 %collective-permute-start.54 = (bf16[2,128,2048]{2,1,0:T(8,128)(2,1)S(1)}, bf16[2,128,2048]{2,1,0:T(8,128)(2,1)S(1)}, u32[]{:S(2)}, u32[]{:S(2)}) collective-permute-start(bf16[2,128,2048]{2,1,0:T(8,128)(2,1)S(1)} %pad_maximum_fusion.22), channel_id=1, source_target_pairs={{0,6},{1,7},{2,0},{3,1},{4,2},{5,3},{6,4},{7,5},{8,14},{9,15},{10,... | collective-permute-start | bytes 3145736 | tf_op jit(solution)/shard_map/ppermute | solution.py:29
  1036.5 40.9 %collective-permute-start.52 = (bf16[2,128,2048]{2,1,0:T(8,128)(2,1)S(1)}, bf16[2,128,2048]{2,1,0:T(8,128)(2,1)S(1)}, u32[]{:S(2)}, u32[]{:S(2)}) collective-permute-start(bf16[2,128,2048]{2,1,0:T(8,128)(2,1)S(1)} %pad_maximum_fusion.21), channel_id=1, source_target_pairs={{0,2},{1,3},{2,4},{3,5},{4,6},{5,7},{6,0},{7,1},{8,10},{9,11},{10,... | collective-permute-start | bytes 3145736 | tf_op jit(solution)/shard_map/ppermute | solution.py:29
  1038.0 16.6 %collective-permute-start.67 = (bf16[4,32,3072]{2,1,0:T(8,128)(2,1)S(1)}, bf16[4,32,3072]{2,1,0:T(8,128)(2,1)S(1)}, u32[]{:S(2)}, u32[]{:S(2)}) collective-permute-start(bf16[4,32,3072]{2,1,0:T(8,128)(2,1)S(1)} %get-tuple-element.138), channel_id=1, source_target_pairs={{0,16},{16,32},{32,48},{48,0},{1,17},{17,33},{33,49},{49,1},{2,18}... | collective-permute-start | bytes 2359304 | tf_op jit(solution)/shard_map/ppermute | solution.py:33
  1039.4 37.1 %collective-permute-start.81 = (bf16[2,384,512]{2,1,0:T(8,128)(2,1)S(1)}, bf16[2,384,512]{2,1,0:T(8,128)(2,1)S(1)}, u32[]{:S(2)}, u32[]{:S(2)}) collective-permute-start(bf16[2,384,512]{2,1,0:T(8,128)(2,1)S(1)} %pad_maximum_fusion.24), channel_id=1, source_target_pairs={{0,6},{1,7},{2,0},{3,1},{4,2},{5,3},{6,4},{7,5},{8,14},{9,15},{10,... | collective-permute-start | bytes 2359304 | tf_op jit(solution)/shard_map/ppermute | solution.py:29
  1040.9 35.7 %collective-permute-start.79 = (bf16[2,384,512]{2,1,0:T(8,128)(2,1)S(1)}, bf16[2,384,512]{2,1,0:T(8,128)(2,1)S(1)}, u32[]{:S(2)}, u32[]{:S(2)}) collective-permute-start(bf16[2,384,512]{2,1,0:T(8,128)(2,1)S(1)} %pad_maximum_fusion.23), channel_id=1, source_target_pairs={{0,2},{1,3},{2,4},{3,5},{4,6},{5,7},{6,0},{7,1},{8,10},{9,11},{10,... | collective-permute-start | bytes 2359304 | tf_op jit(solution)/shard_map/ppermute | solution.py:29
  1054.6 92.0 %collective-permute-start.70 = (bf16[8,32,3072]{2,1,0:T(8,128)(2,1)S(1)}, bf16[8,32,3072]{2,1,0:T(8,128)(2,1)S(1)}, u32[]{:S(2)}, u32[]{:S(2)}) collective-permute-start(bf16[8,32,3072]{2,1,0:T(8,128)(2,1)S(1)} %pad_maximum_fusion.17), channel_id=1, source_target_pairs={{0,48},{16,0},{32,16},{48,32},{1,49},{17,1},{33,17},{49,33},{2,50}... | collective-permute-start | bytes 4718600 | tf_op jit(solution)/shard_map/ppermute | solution.py:33
  1077.7 18.4 %collective-permute-start.55 = (bf16[128,2048]{1,0:T(8,128)(2,1)S(1)}, bf16[128,2048]{1,0:T(8,128)(2,1)S(1)}, u32[]{:S(2)}, u32[]{:S(2)}) collective-permute-start(bf16[128,2048]{1,0:T(8,128)(2,1)S(1)} %fusion.99), channel_id=1, source_target_pairs={{0,8},{1,9},{2,10},{3,11},{4,12},{5,13},{6,14},{7,15},{8,0},{9,1},... | collective-permute-start | bytes 1572872 | tf_op jit(solution)/shard_map/ppermute | solution.py:24
  1080.2 66.4 %collective-permute-start.68 = (bf16[8,32,3072]{2,1,0:T(8,128)(2,1)S(1)}, bf16[8,32,3072]{2,1,0:T(8,128)(2,1)S(1)}, u32[]{:S(2)}, u32[]{:S(2)}) collective-permute-start(bf16[8,32,3072]{2,1,0:T(8,128)(2,1)S(1)} %pad_maximum_fusion.16), channel_id=1, source_target_pairs={{0,16},{16,32},{32,48},{48,0},{1,17},{17,33},{33,49},{49,1},{2,18}... | collective-permute-start | bytes 4718600 | tf_op jit(solution)/shard_map/ppermute | solution.py:33
  1085.2 28.7 %collective-permute-start.83 = (bf16[48,512]{1,0:T(8,128)(2,1)S(1)}, bf16[48,512]{1,0:T(8,128)(2,1)S(1)}, u32[]{:S(2)}, u32[]{:S(2)}) collective-permute-start(bf16[48,512]{1,0:T(8,128)(2,1)S(1)} %get-tuple-element.189), channel_id=1, source_target_pairs={{0,16},{16,32},{32,48},{48,0},{1,17},{17,33},{33,49},{49,1},{2,18}... | collective-permute-start | bytes 147464 | tf_op jit(solution)/shard_map/ppermute | solution.py:33
  1087.9 26.0 %collective-permute-start.85 = (bf16[48,512]{1,0:T(8,128)(2,1)S(1)}, bf16[48,512]{1,0:T(8,128)(2,1)S(1)}, u32[]{:S(2)}, u32[]{:S(2)}) collective-permute-start(bf16[48,512]{1,0:T(8,128)(2,1)S(1)} %get-tuple-element.191), channel_id=1, source_target_pairs={{0,48},{16,0},{32,16},{48,32},{1,49},{17,1},{33,17},{49,33},{2,50}... | collective-permute-start | bytes 147464 | tf_op jit(solution)/shard_map/ppermute | solution.py:33
  1096.5 18.8 %collective-permute-start.56 = (bf16[16,2048]{1,0:T(8,128)(2,1)S(1)}, bf16[16,2048]{1,0:T(8,128)(2,1)S(1)}, u32[]{:S(2)}, u32[]{:S(2)}) collective-permute-start(bf16[16,2048]{1,0:T(8,128)(2,1)S(1)} %get-tuple-element.177), channel_id=1, source_target_pairs={{0,16},{16,32},{32,48},{48,0},{1,17},{17,33},{33,49},{49,1},{2,18}... | collective-permute-start | bytes 196616 | tf_op jit(solution)/shard_map/ppermute | solution.py:33
  1119.0 58.2 %collective-permute-start.86 = (bf16[96,512]{1,0:T(8,128)(2,1)S(1)}, bf16[96,512]{1,0:T(8,128)(2,1)S(1)}, u32[]{:S(2)}, u32[]{:S(2)}) collective-permute-start(bf16[96,512]{1,0:T(8,128)(2,1)S(1)} %pad_maximum_fusion.42), channel_id=1, source_target_pairs={{0,48},{16,0},{32,16},{48,32},{1,49},{17,1},{33,17},{49,33},{2,50}... | collective-permute-start | bytes 294920 | tf_op jit(solution)/shard_map/ppermute | solution.py:33
  1132.7 44.4 %collective-permute-start.84 = (bf16[96,512]{1,0:T(8,128)(2,1)S(1)}, bf16[96,512]{1,0:T(8,128)(2,1)S(1)}, u32[]{:S(2)}, u32[]{:S(2)}) collective-permute-start(bf16[96,512]{1,0:T(8,128)(2,1)S(1)} %pad_maximum_fusion.41), channel_id=1, source_target_pairs={{0,16},{16,32},{32,48},{48,0},{1,17},{17,33},{33,49},{49,1},{2,18}... | collective-permute-start | bytes 294920 | tf_op jit(solution)/shard_map/ppermute | solution.py:33
  1134.7 17.2 %collective-permute-start.64 = (bf16[384,512]{1,0:T(8,128)(2,1)S(1)}, bf16[384,512]{1,0:T(8,128)(2,1)S(1)}, u32[]{:S(2)}, u32[]{:S(2)}) collective-permute-start(bf16[384,512]{1,0:T(8,128)(2,1)S(1)} %constant_dynamic-update-slice_fusion.17), channel_id=1, source_target_pairs={{0,1},{1,0},{2,3},{3,2},{4,5},{5,4},{6,7},{7,6},{8,9},{9,8},{10,11... | collective-permute-start | bytes 1179656 | tf_op jit(solution)/shard_map/ppermute | solution.py:20
  (127 other events, 1069.7 us)

commit v2 on v1

--- a/solution.py
+++ b/solution.py
@@ -16,6 +16,10 @@
 ROOT = HEAD ** (-0.5)
 
 
+def after(value, *others):
+    return lax.optimization_barrier((value, *others))[0]
+
+
 def swap_core(value):
     return lax.ppermute(value, "fsdp", [(i, i ^ 1) for i in range(16)])
 
@@ -35,6 +39,23 @@
 
 def move_section(value, step):
     return lax.ppermute(value, "section", [(0, 1)] if step > 0 else [(1, 0)])
+
+
+def doubled(value, core, y, z):
+    both = in_order(value[None], swap_core(value[None]), core, 0)
+    pair = [(i, i ^ 2) for i in range(16)]
+    both = in_order(both, lax.ppermute(both, "fsdp", pair), y & 1, 0)
+    pair = [(i, i ^ 4) for i in range(16)]
+    both = in_order(both, lax.ppermute(both, "fsdp", pair), y >> 1, 0)
+    return in_order(both, swap_z(both), z, 0)
+
+
+def summed(value):
+    for step in (1, 2, 4, 8):
+        value = value + lax.ppermute(value, "fsdp", [(i, i ^ step) for i in range(16)])
+    for step in (1, 2):
+        value = value + lax.ppermute(value, "dp", [(i, i ^ step) for i in range(4)])
+    return value
 
 
 def pick(value, *where):
@@ -76,82 +97,105 @@
         out_shape=jax.ShapeDtypeStruct((total, width), pieces[0].dtype),
         in_specs=[pl.BlockSpec(memory_space=pltpu.SMEM)]
         + [pl.BlockSpec(memory_space=pl.ANY)] * len(pieces),
-        out_specs=pl.BlockSpec(memory_space=pl.ANY),
+        out_specs=pl.BlockSpec(memory_space=pltpu.VMEM),
         scratch_shapes=[pltpu.SemaphoreType.DMA((sum(counts),))],
-        compiler_params=pltpu.CompilerParams(vmem_limit_bytes=2**20),
+        compiler_params=pltpu.CompilerParams(vmem_limit_bytes=16 * 2**20),
         cost_estimate=pl.CostEstimate(
             flops=0, bytes_accessed=4 * total * width, transcendentals=0
         ),
     )(jnp.stack(offsets).astype(jnp.int32), *pieces)
 
 
-def gather_chip_rows(block, spot, by_x, flip):
-    x, z, y = spot
-    rows = block.shape[0]
-    part = rows // 4 if by_x else rows
-    piece = lax.dynamic_slice_in_dim(block, x * part, part, 0) if by_x else block
-    across = swap_z(piece)
-    pair = jnp.stack([piece, across])
-    behind, ahead = move_y(pair, 1), move_y(pair, -1)
-    far_own, far_across = move_y(behind[0], 1), move_y(ahead[1], -1)
-    origin = [(0, 0), (1, 0), (0, 1), (1, 1), (0, 3), (1, 3), (0, 2), (1, 2)]
-    bases = [((z ^ dz ^ flip) * 4 + ((y - dy) & 3)) * rows for dz, dy in origin]
-    if not by_x:
-        pieces = (pair, behind, ahead, far_own[None], far_across[None])
-        return place(pieces, bases, 8 * rows)
-    whole = jnp.concatenate([pair, behind, ahead, far_own[None], far_across[None]])
-    x_behind, x_ahead = move_x(whole, 1), move_x(whole, -1)
-    x_far_a, x_far_b = move_x(x_behind[:4], 1), move_x(x_ahead[4:], -1)
-    pieces = (whole, x_behind, x_ahead, x_far_a, x_far_b)
+origins = [(0, 0), (1, 0), (0, 1), (1, 1), (0, 3), (1, 3), (0, 2), (1, 2)]
+
+
+def chip_bases(rows, z, y, flip):
+    return [((z ^ dz ^ flip) * 4 + ((y - dy) & 3)) * rows for dz, dy in origins]
+
+
+def near_y(pair):
+    return move_y(pair, 1), move_y(pair, -1)
+
+
+def far_y(behind, ahead):
+    return move_y(behind[0], 1)[None], move_y(ahead[1], -1)[None]
+
+
+def near_x(whole):
+    return move_x(whole, 1), move_x(whole, -1)
+
+
+def far_x(behind, ahead):
+    return move_x(behind[:4], 1), move_x(ahead[4:], -1)
+
+
+def place_x(pieces, bases, part, x):
     offsets = []
-    for dx, kept in ((0, bases), (1, bases), (3, bases), (2, bases)):
-        offsets += [base + ((x - dx) & 3) * part for base in kept]
-    return place(pieces, offsets, 8 * rows)
+    for dx in (0, 1, 3, 2):
+        offsets += [base + ((x - dx) & 3) * part for base in bases]
+    return place(pieces, offsets, 32 * part)
 
 
 def added(left, right):
     return (left.astype(f32) + right.astype(f32)).astype(low)
 
 
-def reduce_x(values, x):
+def reduce_x_first(values, x):
     cut = values.shape[1] // 2
     far = pick(values, (x + 2) & 3)
-    up, down = move_x(far[:cut], 1), move_x(far[cut:], -1)
-    after, before = pick(values, (x + 1) & 3), pick(values, (x - 1) & 3)
-    after = jnp.concatenate([added(after[:cut], up), after[cut:]])
+    return move_x(far[:cut], 1), move_x(far[cut:], -1)
+
+
+def reduce_x_second(values, x, first):
+    cut = values.shape[1] // 2
+    up, down = first
+    after_it, before = pick(values, (x + 1) & 3), pick(values, (x - 1) & 3)
+    after_it = jnp.concatenate([added(after_it[:cut], up), after_it[cut:]])
     before = jnp.concatenate([before[:cut], added(before[cut:], down)])
-    from_behind, from_ahead = move_x(after, 1), move_x(before, -1)
+    return move_x(after_it, 1), move_x(before, -1)
+
+
+def reduce_x_third(values, x, second):
     own = pick(values, x)
-    return (own.astype(f32) + from_behind.astype(f32) + from_ahead.astype(f32)).astype(low)
-
-
-def reduce_chips(values, z, y):
-    other = 1 - z
-    up = move_y(pick(values, z, (y + 2) & 3), 1)
-    down = move_y(pick(values, other, (y + 2) & 3), -1)
-    y_after, y_before = (y + 1) & 3, (y - 1) & 3
-    after = jnp.stack([added(pick(values, z, y_after), up), pick(values, other, y_after)])
+    return (own.astype(f32) + second[0].astype(f32) + second[1].astype(f32)).astype(low)
+
+
+def reduce_x(values, x):
+    return reduce_x_third(values, x, reduce_x_second(values, x, reduce_x_first(values, x)))
+
+
+def reduce_y_first(values, z, y):
+    far = (y + 2) & 3
+    return move_y(pick(values, z, far), 1), move_y(pick(values, 1 - z, far), -1)
+
+
+def reduce_y_second(values, z, y, first):
+    up, down = first
+    other, y_after, y_before = 1 - z, (y + 1) & 3, (y - 1) & 3
+    after_it = jnp.stack([added(pick(values, z, y_after), up), pick(values, other, y_after)])
     before = jnp.stack([pick(values, z, y_before), added(pick(values, other, y_before), down)])
-    from_behind, from_ahead = move_y(after, 1), move_y(before, -1)
-
+    return move_y(after_it, 1), move_y(before, -1)
+
+
+def reduce_z(values, z, y, second):
     def total(k, zi):
         own = pick(values, zi, y)
-        return (own.astype(f32) + from_behind[k].astype(f32) + from_ahead[k].astype(f32)).astype(low)
-
-    return added(total(0, z), swap_z(total(1, other)))
-
-
-def scatter_rows(gradient, spot, by_x, flip):
-    x, z, y = spot
-    z = z ^ flip
-    rows, width = gradient.shape[0] // 8, gradient.shape[1]
-    part = rows // 4
-    if by_x:
-        values = gradient.reshape(8, 4, part, width).transpose(1, 0, 2, 3)
-        mine = reduce_x(values, x)
-        return reduce_chips(mine.reshape(2, 4, part, width), z, y)
-    mine = reduce_chips(gradient.reshape(2, 4, rows, width), z, y)
-    return reduce_x(mine.reshape(4, part, width), x)
+        return (own.astype(f32) + second[0][k].astype(f32) + second[1][k].astype(f32)).astype(low)
+
+    return added(total(0, z), swap_z(total(1, 1 - z)))
+
+
+def by_chip(gradient):
+    return gradient.reshape(2, 4, gradient.shape[0] // 8, gradient.shape[1])
+
+
+def by_x(gradient):
+    part = gradient.shape[0] // 32
+    return gradient.reshape(8, 4, part, gradient.shape[1]).transpose(1, 0, 2, 3)
+
+
+def quarters(value):
+    return value.reshape(4, value.shape[0] // 4, value.shape[1])
 
 
 def gather_x(value, x):
@@ -272,7 +316,7 @@
     return out, saved
 
 
-def backward(cotangent, saved, weights, gains, tables):
+def backward(cotangent, saved, weights, gains, tables, between=None):
     w_qkv, w_out, w_gu, w_down = weights
     mixer_gain, query_gain, key_gain, dense_gain = gains
     (scale_one, normed_one, a1, q_scale, qn, k_scale, kn, qr, kr, v, p, pb, att) = saved[:13]
@@ -286,10 +330,14 @@
     dg = (dz * up * sig * (1.0 + gate * (1.0 - sig))).astype(low)
     du = (dz * (gate * sig)).astype(low)
     dgu = jnp.concatenate([dg, du], axis=-1)
+    if between is not None:
+        dgu = between[0](dm, dgu)
     da2 = dot_t(dgu[0], w_gu[0]) + dot_t(dgu[1], w_gu[1])
     part, dense_gain_grad = norm_backward(da2, normed_two, scale_two, dense_gain)
     dh2 = cotangent + part
     dr = dh2.astype(low)
+    if between is not None:
+        dr, g_out = between[1](dr)
     datt = dot_t(dr, w_out).astype(low).reshape(seqs, 128, 2, 4, 2, HEAD)
     dp = jnp.einsum("bqhkgd,hbskd->hbkgqs", datt, v, preferred_element_type=f32)
     dv = jnp.einsum("hbkgqs,bqhkgd->hbskd", pb, datt, preferred_element_type=f32).astype(low)
@@ -300,10 +348,12 @@
     dq, q_gain_grad = norm_backward(rotate_heads(dqr, tables, -1.0), qn, q_scale, query_gain)
     dk, k_gain_grad = norm_backward(rotate_heads(dkr, tables, -1.0), kn, k_scale, key_gain)
     dqkv = jnp.concatenate([dq.astype(low), dk.astype(low), dv], axis=3).reshape(2, tokens, 2048)
+    if between is not None:
+        dqkv = between[2](dqkv, g_out)
     da1 = dot_t(dqkv[0], w_qkv[0]) + dot_t(dqkv[1], w_qkv[1])
     part, mixer_gain_grad = norm_backward(da1, normed_one, scale_one, mixer_gain)
     dh = dh2 + part
-    return dh, (dm, dgu, dr, dqkv), (mixer_gain_grad, dense_gain_grad, q_gain_grad, k_gain_grad)
+    return dh, (mixer_gain_grad, dense_gain_grad, q_gain_grad, k_gain_grad)
 
 
 def swapped_halves(value):
@@ -347,7 +397,7 @@
             jnp.pad(key_gain[0], (0, 56)),
         ]
     )
-    tiles = lax.all_gather(tile, "fsdp", axis=0, tiled=False).astype(f32)
+    tiles = doubled(tile, core, y, z).astype(f32)
     gains = (
         tiles[:, 0].reshape(MODEL),
         tiles[:, 2, :8].reshape(HEAD),
@@ -367,13 +417,49 @@
         )
 
     kept, sent = column_half(core), column_half(1 - core)
-    came = [swap_core(s) for s in sent]
-    chips = [in_order(k, c, core, 0) for k, c in zip(kept, came)]
     zero = jnp.zeros_like(z)
-    own_qkv = gather_chip_rows(chips[0], spot, False, zero)
-    own_gu = gather_chip_rows(chips[2], spot, True, zero)
-    own_out = gather_chip_rows(chips[1], spot, False, core)
-    own_down = gather_chip_rows(chips[3], spot, True, core)
+
+    def quarter(chip):
+        part = chip.shape[0] // 4
+        return lax.dynamic_slice_in_dim(chip, x * part, part, 0)
+
+    with jax.named_scope("ag_gu"):
+        gu_0 = quarter(in_order(kept[2], swap_core(sent[2]), core, 0))
+        gu_z = swap_z(gu_0)
+        gu_pair = jnp.stack([gu_0, gu_z])
+        gu_near = near_y(gu_pair)
+        gu_far = far_y(*gu_near)
+        gu_all = jnp.concatenate([gu_pair, *gu_near, *gu_far])
+        gu_x = near_x(gu_all)
+    with jax.named_scope("ag_qkv"):
+        qkv_0 = in_order(kept[0], swap_core(after(sent[0], gu_0)), core, 0)
+        qkv_z = swap_z(after(qkv_0, gu_z))
+        qkv_pair = jnp.stack([qkv_0, qkv_z])
+        qkv_near = near_y(after(qkv_pair, *gu_far))
+    with jax.named_scope("ag_down"):
+        down_0 = quarter(in_order(kept[3], swap_core(after(sent[3], gu_0)), core, 0))
+        down_z = swap_z(after(down_0, qkv_z))
+        down_pair = jnp.stack([down_0, down_z])
+        down_near = near_y(after(down_pair, *gu_far))
+        down_far = far_y(*down_near)
+        down_all = jnp.concatenate([down_pair, *down_near, *down_far])
+    with jax.named_scope("ag_qkv"):
+        qkv_far = far_y(*qkv_near)
+        own_qkv = place((qkv_pair, *qkv_near, *qkv_far), chip_bases(128, z, y, 0), MODEL)
+    with jax.named_scope("ag_out"):
+        out_0 = in_order(kept[1], swap_core(after(sent[1], gu_0)), core, 0)
+        out_z = swap_z(after(out_0, down_z))
+        out_pair = jnp.stack([out_0, out_z])
+        out_near = near_y(after(out_pair, *qkv_near))
+        out_far = far_y(*after(out_near, *qkv_far))
+        own_out = place((out_pair, *out_near, *out_far), chip_bases(256, z, y, core), 2048)
+    with jax.named_scope("ag_gu"):
+        gu_x_far = far_x(*gu_x)
+        own_gu = place_x((gu_all, *gu_x, *gu_x_far), chip_bases(128, z, y, 0), 32, x)
+    with jax.named_scope("ag_down"):
+        down_x = near_x(after(down_all, *gu_x))
+        down_x_far = far_x(*down_x)
+        own_down = place_x((down_all, *down_x, *down_x_far), chip_bases(384, z, y, core), 96, x)
     w_qkv = (own_qkv, swap_core(own_qkv))
     w_gu = (own_gu, swap_core(own_gu))
 
@@ -386,33 +472,91 @@
     weights = (w_qkv, w_out, w_gu, w_down)
 
     tables = rotation_tables(128)
-    early, _ = forward(local, weights, gains, tables)
+    with jax.named_scope("f1"):
+        early, _ = forward(local, weights, gains, tables)
     arrived = move_section(early.astype(low), 1).astype(f32)
-    out, saved = forward(jnp.where(first_section, local, arrived), weights, gains, tables)
+    with jax.named_scope("f2"):
+        out, saved = forward(jnp.where(first_section, local, arrived), weights, gains, tables)
     a1, att, a2, z_low = saved[2], saved[12], saved[15], saved[18]
-    early_dh, _, _ = backward(local, saved, weights, gains, tables)
+    with jax.named_scope("b1"):
+        early_dh, _ = backward(local, saved, weights, gains, tables)
     returned = move_section(early_dh.astype(low), -1).astype(f32)
     cotangent = jnp.where(first_section, returned, local)
-    dh, (dm, dgu, dr, dqkv), gain_grads = backward(cotangent, saved, weights, gains, tables)
-    endpoints = jnp.where(first_section, dh, out).reshape(1, 2, 1, 128, MODEL)
 
     a1_o, att_o, a2_o, z_o = [swap_core(v) for v in (a1, att, a2, z_low)]
     att_o, z_o = swapped_halves(att_o), swapped_halves(z_o)
-    dm_mine, dr_mine = half_of(dm, core, 1), half_of(dr, core, 1)
-    g_down = product(z_low, z_o, dm_mine, swap_core(half_of(dm, 1 - core, 1)))
-    g_gu = product(a2, a2_o, dgu[0], swap_core(dgu[1]))
-    g_out = product(att, att_o, dr_mine, swap_core(half_of(dr, 1 - core, 1)))
-    g_qkv = product(a1, a1_o, dqkv[0], swap_core(dqkv[1]))
-    s_gu = scatter_rows(g_gu, spot, True, zero)
-    s_down = scatter_rows(g_down, spot, False, core)
-    s_out = scatter_rows(g_out, spot, False, core)
-    s_qkv = scatter_rows(g_qkv, spot, False, zero)
-    (gu, down), (out_w, qkv) = finish((s_gu, s_down), x, core), finish((s_out, s_qkv), x, core)
+    cot_mine, cot_theirs = half_of(cotangent, core, 1), half_of(cotangent, 1 - core, 1)
+    z_flip = z ^ core
+    done = {}
+
+    def after_dgu(dm, dgu):
+        with jax.named_scope("g_gu"):
+            g_gu = by_x(product(a2, a2_o, dgu[0], swap_core(dgu[1])))
+            done["gu"] = (g_gu, reduce_x_first(g_gu, x))
+        with jax.named_scope("g_down"):
+            dm_o = swap_core(cot_theirs.astype(low))
+            g_down = by_chip(product(z_low, z_o, cot_mine.astype(low), dm_o))
+            done["down"] = (g_down, reduce_y_first(g_down, z_flip, y))
+        return after(dgu, g_gu, g_down)
+
+    def after_dr(dr):
+        with jax.named_scope("rs_gu"):
+            g_gu, first = done["gu"]
+            first = after(first, dr)
+            done["gu2"] = reduce_x_second(g_gu, x, first)
+        with jax.named_scope("rs_down"):
+            g_down, first = done["down"]
+            first = after(first, dr)
+            done["down2"] = reduce_y_second(g_down, z_flip, y, first)
+        with jax.named_scope("g_out"):
+            dr_o = swap_core(half_of(dr, 1 - core, 1))
+            g_out = by_chip(product(att, att_o, half_of(dr, core, 1), dr_o))
+        return after(dr, g_out, *done["gu"][1], *done["down"][1]), g_out
+
+    def after_attention(dqkv, g_out):
+        with jax.named_scope("rs_down"):
+            second = after(done["down2"], dqkv)
+            done["s_down"] = quarters(reduce_z(done["down"][0], z_flip, y, second))
+        with jax.named_scope("rs_out"):
+            first = reduce_y_first(after(g_out, *second), z_flip, y)
+            done["out"] = (g_out, reduce_y_second(g_out, z_flip, y, first))
+        with jax.named_scope("rs_gu"):
+            second_gu = after(done["gu2"], dqkv)
+            mine = by_chip(
+                reduce_x_third(done["gu"][0], x, second_gu).reshape(8 * 32, 3072)
+            )
+            done["gu3"] = (mine, reduce_y_first(mine, z, y))
+        with jax.named_scope("g_qkv"):
+            g_qkv = by_chip(product(a1, a1_o, dqkv[0], swap_core(dqkv[1])))
+            done["qkv"] = (g_qkv, reduce_y_first(after(g_qkv, *done["gu3"][1]), z, y))
+        return after(dqkv, g_qkv, *second_gu)
+
+    with jax.named_scope("b2"):
+        dh, gain_grads = backward(
+            cotangent, saved, weights, gains, tables, (after_dgu, after_dr, after_attention)
+        )
+    endpoints = jnp.where(first_section, dh, out).reshape(1, 2, 1, 128, MODEL)
+    with jax.named_scope("rs_gu"):
+        mine, first = done["gu3"]
+        gu_y = reduce_y_second(mine, z, y, first)
+        s_gu = reduce_z(mine, z, y, gu_y)
+    with jax.named_scope("rs_qkv"):
+        g_qkv, first = done["qkv"]
+        qkv_y = reduce_y_second(g_qkv, z, y, first)
+        s_qkv = reduce_x(quarters(reduce_z(g_qkv, z, y, qkv_y)), x)
+    with jax.named_scope("rs_down"):
+        s_down = reduce_x(done["s_down"], x)
+    with jax.named_scope("rs_out"):
+        s_out = reduce_x(quarters(reduce_z(done["out"][0], z_flip, y, done["out"][1])), x)
+    with jax.named_scope("fin_a"):
+        gu, down = finish((s_gu, s_down), x, core)
+    with jax.named_scope("fin_b"):
+        out_w, qkv = finish((s_out, s_qkv), x, core)
 
     def both(pair, start, width):
         return in_order(*(p[:, start : start + width] for p in pair), core, 1)[None]
 
-    sums = lax.psum(jnp.concatenate(gain_grads).reshape(18, 128), ("dp", "fsdp")).reshape(-1)
+    sums = summed(jnp.concatenate(gain_grads).reshape(18, 128)).reshape(-1)
 
     def gain_rows(start, width):
         return lax.dynamic_slice_in_dim(sums, start + place_at * width, width, 0)[None]

time: 1210 us -> 685 us (0.57)
  blocking collectives: 351 us -> 0 us
  Pallas kernels: 217 us -> 19.2 us
  starting transfers between devices: 131 us -> 160 us
  waiting for transfers between devices: 182 us -> 167 us
    psum x1 -> x0, blocking collectives: 322 us -> none  [on_device(): lax.psum(jnp.concatenate(gain_grads).reshape(18, 128), ('dp', 'fsdp'))]
    pallas_call x4, Pallas kernels: 217 us -> 19.2 us  [place(): pl.pallas_call(functools.partial(placing_kernel, counts, rows), out_shape...]
    all_gather x1 -> x0, blocking collectives: 29.3 us -> none  [on_device(): tiles = lax.all_gather(tile, 'fsdp', axis=0, tiled=False).astype(f32)]
    ppermute x32, waiting for transfers between devices: 74.9 us -> 46.1 us  [move_y(): return lax.ppermute(value, 'fsdp', pairs)]
    ppermute x18 -> x19, starting transfers between devices: 40.2 us -> 53.8 us  [swap_core(): return lax.ppermute(value, 'fsdp', [(i, i ^ 1) for i in range(16)])]
    unnamed x217 -> x247, local copies, waits for them, and re-layouts: 30.8 us -> 21.6 us
    ppermute x8 -> x9, waiting for transfers between devices: 28.8 us -> 27.7 us  [swap_z(): return lax.ppermute(value, 'fsdp', [(i, i ^ 8) for i in range(16)])]
  transfers between devices with their start and end apart: 92 -> 102, of which waited for: 37 -> 38; matrix products, arithmetic and copies ran while one was open for 15% -> 28% of each run, Pallas kernels for 18% -> 3%
where the time goes in v2:
time: 685 us; the launch traced here: 674 us
  waiting for transfers between devices  167 us (24%)
  starting transfers between devices  160 us (23%)
  matrix products  140 us (20%)
  local copies, waits for them, and re-layouts  116 us (17%)
  other arithmetic  67.2 us (10%)
  Pallas kernels  19.2 us (3%)
    ppermute x32, waiting for transfers between devices, move_x(): return lax.ppermute(value, 'dp', [(i, (i + step) % 4) for i in range(4)])  64.7 us
    ppermute x19, starting transfers between devices, swap_core(): return lax.ppermute(value, 'fsdp', [(i, i ^ 1) for i in range(16)])  53.8 us
    dot_general x12, matrix products, dot(): return jnp.dot(left, right, preferred_element_type=f32)  48.8 us
    ppermute x32, waiting for transfers between devices, move_y(): return lax.ppermute(value, 'fsdp', pairs)  46.1 us
    dot_general x12, matrix products, dot_t(): lax.dot_general(left, right, (((1,), (1,)), ((), ())), preferred_element_...  44.1 us
    ppermute x32, starting transfers between devices, move_y(): return lax.ppermute(value, 'fsdp', pairs)  38 us
    ppermute x32, starting transfers between devices, move_x(): return lax.ppermute(value, 'dp', [(i, (i + step) % 4) for i in range(4)])  35.5 us
    ppermute x9, waiting for transfers between devices, swap_z(): return lax.ppermute(value, 'fsdp', [(i, i ^ 8) for i in range(16)])  27.7 us
  transfers between devices with their start and end apart: 102, of which 38 were waited for; matrix products, arithmetic and copies ran while one was open for 28% of the time, Pallas kernels for 3%

profile of v2, /device:TPU:1, one launch (start us, length us, event | category | flops | bytes accessed | tf_op | source)
XLA Modules:
  0.0 674.1 jit_solution(16116650130767726433)
XLA Ops:
  6.8 3.8 collective-permute-start.6
  11.2 4.6 collective-permute-done.6
  22.6 4.6 collective-permute-done.8
  39.4 18.5 %collective-permute-done.12.refs_1_ = bf16[2,128,2048]{2,1,0:T(8,128)(2,1)S(1)} collective-permute-done((bf16[2,128,2048]{2,1,0:T(8,128)(2,1)S(1)}, bf16[2,128,2048]{2,1,0:T(8,128)(2,1)S(1)}, u32[]{:S(2)}, u32[]{:S(2)}) %collective-permute-start.12) | collective-permute-done | bytes 1048608 | tf_op jit(solution)/shard_map/ag_qkv/ppermute | solution.py:33
  77.9 7.0 %collective-permute-start.16 = (bf16[1024,2048]{1,0:T(8,128)(2,1)}, bf16[1024,2048]{1,0:T(8,128)(2,1)}, u32[]{:S(2)}, u32[]{:S(2)}) collective-permute-start(bf16[1024,2048]{1,0:T(8,128)(2,1)} %ag_qkv.1), channel_id=1, source_target_pairs={{0,1},{1,0},{2,3},{3,2},{4,5},{5,4},{6,7},{7,6},{8,9},{9,8},{10,11... | collective-permute-start | bytes 12582920 | tf_op jit(solution)/shard_map/ppermute | solution.py:24
  85.9 4.8 collective-permute-done.33
  98.4 6.5 collective-permute-start.25
  117.9 6.2 collective-permute-done.35.refs_1_
  124.6 6.4 copy.112
  134.6 6.4 collective-permute-done.28.refs_3_
  141.0 5.1 convolution_bitcast_fusion.8
  147.8 11.5 %ag_gu.1 = bf16[1024,3072]{1,0:T(8,128)(2,1)} custom-call(s32[32]{0:T(128)S(1)} %stack.496.offsets, bf16[8,32,3072]{2,1,0:T(8,128)(2,1)S(1)} %copy-done.1, bf16[8,32,3072]{2,1,0:T(8,128)(2,1)S(1)} %collective-permute-done.26.refs_1_, bf16[8,32,3072]{2,1,0:T(8,128)(2,1)S(1)} %collective-permute-done.27.refs_2_, ...), custom_call_target="tpu_custom_call" | custom-call | bytes 12582912 | tf_op jit(solution)/shard_map/ag_gu/pallas_call | solution.py:95
  159.3 6.1 collective-permute-start.30
  169.7 4.5 broadcast_select_fusion.3
  174.2 6.8 %copy.113 = bf16[2048,1024]{1,0:T(8,128)(2,1)} copy(bf16[2048,1024]{0,1:T(8,128)(2,1)} %bitcast.45) | data formatting | bytes 8388608 | tf_op jit(solution)/shard_map/f1/dot_general | solution.py:272
  181.0 3.9 convolution_bitcast_fusion.7
  196.2 4.8 fusion.227
  204.3 3.7 copy.59
  210.6 4.0 multiply_reduce_fusion.17
  214.6 4.6 convolution_bitcast_fusion.4
  224.9 4.6 convolution_bitcast_fusion.3
  237.2 8.9 %collective-permute-done.40 = bf16[256,1024]{1,0:T(8,128)(2,1)S(1)} collective-permute-done((bf16[256,1024]{1,0:T(8,128)(2,1)S(1)}, bf16[256,1024]{1,0:T(8,128)(2,1)S(1)}, u32[]{:S(2)}, u32[]{:S(2)}) %collective-permute-start.40) | collective-permute-done | bytes 524320 | tf_op jit(solution)/shard_map/ppermute | solution.py:41
  268.8 4.2 fusion.230
  278.4 3.7 copy.67
  284.7 4.1 multiply_reduce_fusion.14
  289.0 5.0 convolution_bitcast_fusion.1
  294.0 5.7 convolution_bitcast_fusion
  302.0 4.7 fusion.44
  306.8 4.9 multiply_reduce_fusion.13
  318.5 3.7 copy.74
  339.6 3.9 fusion.94
  343.6 3.8 multiply_reduce_fusion.11
  349.2 12.9 %collective-permute-done.41 = bf16[256,1024]{1,0:T(8,128)(2,1)S(1)} collective-permute-done((bf16[256,1024]{1,0:T(8,128)(2,1)S(1)}, bf16[256,1024]{1,0:T(8,128)(2,1)S(1)}, u32[]{:S(2)}, u32[]{:S(2)}) %collective-permute-start.41) | collective-permute-done | bytes 524320 | tf_op jit(solution)/shard_map/ppermute | solution.py:41
  384.2 12.6 %convolution_convert_fusion.1 = bf16[3072,512]{1,0:T(8,128)(2,1)S(1)} fusion(bf16[256,1536]{1,0:T(8,128)(2,1)S(1)} %get-tuple-element.181, bf16[256,1536]{1,0:T(8,128)(2,1)S(1)} %get-tuple-element.180, bf16[256,1536]{1,0:T(8,128)(2,1)S(1)} %copy-done.62, bf16[256,1536]{1,0:T(8,128)(2,1)S(1)} %copy-done.59, ...), kind=kOutput, calls=%fused_computation.16 | convolution fusion | flops 1625817088 | bytes 6815744 | tf_op jit(solution)/shard_map/b2/g_down/dot_general | solution.py:368
  396.8 5.9 fusion.53
  402.8 4.8 multiply_reduce_fusion.6
  410.5 3.9 convolution_convert_fusion
  432.5 5.3 collective-permute-done.48
  443.1 3.7 copy.83
  463.7 4.2 reshape.565
  516.5 25.7 %collective-permute-done.69 = bf16[32,512]{1,0:T(8,128)(2,1)S(1)} collective-permute-done((bf16[32,512]{1,0:T(8,128)(2,1)S(1)}, bf16[32,512]{1,0:T(8,128)(2,1)S(1)}, u32[]{:S(2)}, u32[]{:S(2)}) %collective-permute-start.69) | collective-permute-done | bytes 32800 | tf_op jit(solution)/shard_map/rs_out/ppermute | solution.py:37
  547.4 4.0 multiply_reduce_fusion.7
  579.1 3.7 collective-permute-done.89
  584.2 9.1 %collective-permute-done.75 = bf16[128,2048]{1,0:T(8,128)(2,1)S(1)} collective-permute-done((bf16[128,2048]{1,0:T(8,128)(2,1)S(1)}, bf16[128,2048]{1,0:T(8,128)(2,1)S(1)}, u32[]{:S(2)}, u32[]{:S(2)}) %collective-permute-start.75) | collective-permute-done | bytes 524320 | tf_op jit(solution)/shard_map/b2/g_qkv/ppermute | solution.py:33
  608.0 14.3 %collective-permute-start.101 = (bf16[576,512]{1,0:T(8,128)(2,1)S(1)}, bf16[576,512]{1,0:T(8,128)(2,1)S(1)}, u32[]{:S(2)}, u32[]{:S(2)}) collective-permute-start(bf16[576,512]{1,0:T(8,128)(2,1)S(1)} %dynamic-slice_dynamic-update-slice_fusion), channel_id=1, source_target_pairs={{0,1},{1,0},{2,3},{3,2},{4,5},{5,4},{6,7},{7,6},{8,9},{9,8},{10,11... | collective-permute-start | bytes 1769480 | tf_op jit(solution)/shard_map/fin_a/ppermute | solution.py:24
  624.3 11.2 %collective-permute-done.79 = bf16[128,2048]{1,0:T(8,128)(2,1)S(1)} collective-permute-done((bf16[128,2048]{1,0:T(8,128)(2,1)S(1)}, bf16[128,2048]{1,0:T(8,128)(2,1)S(1)}, u32[]{:S(2)}, u32[]{:S(2)}) %collective-permute-start.79) | collective-permute-done | bytes 524320 | tf_op jit(solution)/shard_map/rs_qkv/ppermute | solution.py:28
  648.4 5.7 collective-permute-done.85
  660.0 8.9 %collective-permute-start.88 = (bf16[384,512]{1,0:T(8,128)(2,1)S(1)}, bf16[384,512]{1,0:T(8,128)(2,1)S(1)}, u32[]{:S(2)}, u32[]{:S(2)}) collective-permute-start(bf16[384,512]{1,0:T(8,128)(2,1)S(1)} %constant_dynamic-update-slice_fusion.19), channel_id=1, source_target_pairs={{0,1},{1,0},{2,3},{3,2},{4,5},{5,4},{6,7},{7,6},{8,9},{9,8},{10,11... | collective-permute-start | bytes 1179656 | tf_op jit(solution)/shard_map/fin_b/ppermute | solution.py:24
  (694 shorter events, 352.7 us)
Async XLA Ops:
  15.8 11.5 %collective-permute-start.8 = (bf16[2,32,3072]{2,1,0:T(8,128)(2,1)S(1)}, bf16[2,32,3072]{2,1,0:T(8,128)(2,1)S(1)}, u32[]{:S(2)}, u32[]{:S(2)}) collective-permute-start(bf16[2,32,3072]{2,1,0:T(8,128)(2,1)S(1)} %pad_maximum_fusion.32), channel_id=1, source_target_pairs={{0,2},{1,3},{2,4},{3,5},{4,6},{5,7},{6,0},{7,1},{8,10},{9,11},{10,... | collective-permute-start | bytes 1179656 | tf_op jit(solution)/shard_map/ag_gu/ppermute | solution.py:33
  19.8 14.0 %collective-permute-start.7 = (bf16[128,2048]{1,0:T(8,128)(2,1)S(1)}, bf16[128,2048]{1,0:T(8,128)(2,1)S(1)}, u32[]{:S(2)}, u32[]{:S(2)}) collective-permute-start(bf16[128,2048]{1,0:T(8,128)(2,1)S(1)} %get-tuple-element.38), channel_id=1, source_target_pairs={{0,8},{1,9},{2,10},{3,11},{4,12},{5,13},{6,14},{7,15},{8,0},{9,1},... | collective-permute-start | bytes 1572872 | tf_op jit(solution)/shard_map/ag_qkv/ppermute | solution.py:28
  33.9 24.0 %collective-permute-start.12 = (bf16[2,128,2048]{2,1,0:T(8,128)(2,1)S(1)}, bf16[2,128,2048]{2,1,0:T(8,128)(2,1)S(1)}, u32[]{:S(2)}, u32[]{:S(2)}) collective-permute-start(bf16[2,128,2048]{2,1,0:T(8,128)(2,1)S(1)} %pad_maximum_fusion.18.refs_0_), channel_id=1, source_target_pairs={{0,2},{1,3},{2,4},{3,5},{4,6},{5,7},{6,0},{7,1},{8,10},{9,11},{10,... | collective-permute-start | bytes 3145736 | tf_op jit(solution)/shard_map/ag_qkv/ppermute | solution.py:33
  34.1 28.6 %collective-permute-start.19 = (bf16[96,512]{1,0:T(8,128)(2,1)S(1)}, bf16[96,512]{1,0:T(8,128)(2,1)S(1)}, u32[]{:S(2)}, u32[]{:S(2)}) collective-permute-start(bf16[96,512]{1,0:T(8,128)(2,1)S(1)} %get-tuple-element.42), channel_id=1, source_target_pairs={{0,8},{1,9},{2,10},{3,11},{4,12},{5,13},{6,14},{7,15},{8,0},{9,1},... | collective-permute-start | bytes 294920 | tf_op jit(solution)/shard_map/ag_down/ppermute | solution.py:28
  36.7 22.4 %collective-permute-start.13 = (bf16[2,128,2048]{2,1,0:T(8,128)(2,1)S(1)}, bf16[2,128,2048]{2,1,0:T(8,128)(2,1)S(1)}, u32[]{:S(2)}, u32[]{:S(2)}) collective-permute-start(bf16[2,128,2048]{2,1,0:T(8,128)(2,1)S(1)} %pad_maximum_fusion.18.refs_0_), channel_id=1, source_target_pairs={{0,6},{1,7},{2,0},{3,1},{4,2},{5,3},{6,4},{7,5},{8,14},{9,15},{10,... | collective-permute-start | bytes 3145736 | tf_op jit(solution)/shard_map/ag_qkv/ppermute | solution.py:33
  57.9 12.8 %collective-permute-start.14 = (bf16[128,2048]{1,0:T(8,128)(2,1)S(1)}, bf16[128,2048]{1,0:T(8,128)(2,1)S(1)}, u32[]{:S(2)}, u32[]{:S(2)}) collective-permute-start(bf16[128,2048]{1,0:T(8,128)(2,1)S(1)} %slice_bitcast_fusion.19), channel_id=1, source_target_pairs={{0,2},{1,3},{2,4},{3,5},{4,6},{5,7},{6,0},{7,1},{8,10},{9,11},{10,... | collective-permute-start | bytes 1572872 | tf_op jit(solution)/shard_map/ag_qkv/ppermute | solution.py:33
  59.1 13.1 %collective-permute-start.15 = (bf16[128,2048]{1,0:T(8,128)(2,1)S(1)}, bf16[128,2048]{1,0:T(8,128)(2,1)S(1)}, u32[]{:S(2)}, u32[]{:S(2)}) collective-permute-start(bf16[128,2048]{1,0:T(8,128)(2,1)S(1)} %slice_bitcast_fusion.18), channel_id=1, source_target_pairs={{0,6},{1,7},{2,0},{3,1},{4,2},{5,3},{6,4},{7,5},{8,14},{9,15},{10,... | collective-permute-start | bytes 1572872 | tf_op jit(solution)/shard_map/ag_qkv/ppermute | solution.py:33
  63.4 11.8 %collective-permute-start.31 = (bf16[2,96,512]{2,1,0:T(8,128)(2,1)S(1)}, bf16[2,96,512]{2,1,0:T(8,128)(2,1)S(1)}, u32[]{:S(2)}, u32[]{:S(2)}) collective-permute-start(bf16[2,96,512]{2,1,0:T(8,128)(2,1)S(1)} %pad_maximum_fusion.38), channel_id=1, source_target_pairs={{0,2},{1,3},{2,4},{3,5},{4,6},{5,7},{6,0},{7,1},{8,10},{9,11},{10,... | collective-permute-start | bytes 589832 | tf_op jit(solution)/shard_map/ag_down/ppermute | solution.py:33
  63.4 14.5 %collective-permute-start.32 = (bf16[2,96,512]{2,1,0:T(8,128)(2,1)S(1)}, bf16[2,96,512]{2,1,0:T(8,128)(2,1)S(1)}, u32[]{:S(2)}, u32[]{:S(2)}) collective-permute-start(bf16[2,96,512]{2,1,0:T(8,128)(2,1)S(1)} %pad_maximum_fusion.38), channel_id=1, source_target_pairs={{0,6},{1,7},{2,0},{3,1},{4,2},{5,3},{6,4},{7,5},{8,14},{9,15},{10,... | collective-permute-start | bytes 589832 | tf_op jit(solution)/shard_map/ag_down/ppermute | solution.py:33
  69.4 36.1 %collective-permute-start.26 = (bf16[8,32,3072]{2,1,0:T(8,128)(2,1)S(1)}, bf16[8,32,3072]{2,1,0:T(8,128)(2,1)S(1)}, u32[]{:S(2)}, u32[]{:S(2)}) collective-permute-start(bf16[8,32,3072]{2,1,0:T(8,128)(2,1)S(1)} %constant_dynamic-update-slice_fusion.refs_0_), channel_id=1, source_target_pairs={{0,16},{16,32},{32,48},{48,0},{1,17},{17,33},{33,49},{49,1},{2,18}... | collective-permute-start | bytes 4718600 | tf_op jit(solution)/shard_map/ag_gu/ppermute | solution.py:37
  70.7 34.9 %collective-permute-start.27 = (bf16[8,32,3072]{2,1,0:T(8,128)(2,1)S(1)}, bf16[8,32,3072]{2,1,0:T(8,128)(2,1)S(1)}, u32[]{:S(2)}, u32[]{:S(2)}) collective-permute-start(bf16[8,32,3072]{2,1,0:T(8,128)(2,1)S(1)} %constant_dynamic-update-slice_fusion.refs_0_), channel_id=1, source_target_pairs={{0,48},{16,0},{32,16},{48,32},{1,49},{17,1},{33,17},{49,33},{2,50}... | collective-permute-start | bytes 4718600 | tf_op jit(solution)/shard_map/ag_gu/ppermute | solution.py:37
  72.3 13.4 %collective-permute-start.21 = (bf16[2,256,512]{2,1,0:T(8,128)(2,1)S(1)}, bf16[2,256,512]{2,1,0:T(8,128)(2,1)S(1)}, u32[]{:S(2)}, u32[]{:S(2)}) collective-permute-start(bf16[2,256,512]{2,1,0:T(8,128)(2,1)S(1)} %pad_maximum_fusion.26.refs_0_), channel_id=1, source_target_pairs={{0,2},{1,3},{2,4},{3,5},{4,6},{5,7},{6,0},{7,1},{8,10},{9,11},{10,... | collective-permute-start | bytes 1572872 | tf_op jit(solution)/shard_map/ag_out/ppermute | solution.py:33
  77.9 96.2 %collective-permute-start.16 = (bf16[1024,2048]{1,0:T(8,128)(2,1)}, bf16[1024,2048]{1,0:T(8,128)(2,1)}, u32[]{:S(2)}, u32[]{:S(2)}) collective-permute-start(bf16[1024,2048]{1,0:T(8,128)(2,1)} %ag_qkv.1), channel_id=1, source_target_pairs={{0,1},{1,0},{2,3},{3,2},{4,5},{5,4},{6,7},{7,6},{8,9},{9,8},{10,11... | collective-permute-start | bytes 12582920 | tf_op jit(solution)/shard_map/ppermute | solution.py:24
  98.4 69.6 %collective-permute-start.25 = (bf16[2048,512]{1,0:T(8,128)(2,1)}, bf16[2048,512]{1,0:T(8,128)(2,1)}, u32[]{:S(2)}, u32[]{:S(2)}) collective-permute-start(bf16[2048,512]{1,0:T(8,128)(2,1)} %ag_out.1), channel_id=1, source_target_pairs={{0,1},{1,0},{2,3},{3,2},{4,5},{5,4},{6,7},{7,6},{8,9},{9,8},{10,11... | collective-permute-start | bytes 6291464 | tf_op jit(solution)/shard_map/ppermute | solution.py:24
  105.6 18.5 %collective-permute-start.35 = (bf16[8,96,512]{2,1,0:T(8,128)(2,1)}, bf16[8,96,512]{2,1,0:T(8,128)(2,1)}, u32[]{:S(2)}, u32[]{:S(2)}) collective-permute-start(bf16[8,96,512]{2,1,0:T(8,128)(2,1)} %constant_dynamic-update-slice_fusion.6.refs_0_), channel_id=1, source_target_pairs={{0,16},{16,32},{32,48},{48,0},{1,17},{17,33},{33,49},{49,1},{2,18}... | collective-permute-start | bytes 2359304 | tf_op jit(solution)/shard_map/ag_down/ppermute | solution.py:37
  113.3 18.7 %collective-permute-start.36 = (bf16[8,96,512]{2,1,0:T(8,128)(2,1)}, bf16[8,96,512]{2,1,0:T(8,128)(2,1)}, u32[]{:S(2)}, u32[]{:S(2)}) collective-permute-start(bf16[8,96,512]{2,1,0:T(8,128)(2,1)} %constant_dynamic-update-slice_fusion.6.refs_0_), channel_id=1, source_target_pairs={{0,48},{16,0},{32,16},{48,32},{1,49},{17,1},{33,17},{49,33},{2,50}... | collective-permute-start | bytes 2359304 | tf_op jit(solution)/shard_map/ag_down/ppermute | solution.py:37
  117.0 24.0 %collective-permute-start.28 = (bf16[4,32,3072]{2,1,0:T(8,128)(2,1)}, bf16[4,32,3072]{2,1,0:T(8,128)(2,1)}, u32[]{:S(2)}, u32[]{:S(2)}) collective-permute-start(bf16[4,32,3072]{2,1,0:T(8,128)(2,1)} %slice.792), channel_id=1, source_target_pairs={{0,16},{16,32},{32,48},{48,0},{1,17},{17,33},{33,49},{49,1},{2,18}... | collective-permute-start | bytes 2359304 | tf_op jit(solution)/shard_map/ag_gu/ppermute | solution.py:37
  124.1 23.6 %collective-permute-start.29 = (bf16[4,32,3072]{2,1,0:T(8,128)(2,1)}, bf16[4,32,3072]{2,1,0:T(8,128)(2,1)}, u32[]{:S(2)}, u32[]{:S(2)}) collective-permute-start(bf16[4,32,3072]{2,1,0:T(8,128)(2,1)} %slice.793), channel_id=1, source_target_pairs={{0,48},{16,0},{32,16},{48,32},{1,49},{17,1},{33,17},{49,33},{2,50}... | collective-permute-start | bytes 2359304 | tf_op jit(solution)/shard_map/ag_gu/ppermute | solution.py:37
  132.1 33.3 %collective-permute-start.37 = (bf16[4,96,512]{2,1,0:T(8,128)(2,1)S(1)}, bf16[4,96,512]{2,1,0:T(8,128)(2,1)S(1)}, u32[]{:S(2)}, u32[]{:S(2)}) collective-permute-start(bf16[4,96,512]{2,1,0:T(8,128)(2,1)S(1)} %slice.800), channel_id=1, source_target_pairs={{0,16},{16,32},{32,48},{48,0},{1,17},{17,33},{33,49},{49,1},{2,18}... | collective-permute-start | bytes 1179656 | tf_op jit(solution)/shard_map/ag_down/ppermute | solution.py:37
  141.0 24.4 %collective-permute-start.38 = (bf16[4,96,512]{2,1,0:T(8,128)(2,1)S(1)}, bf16[4,96,512]{2,1,0:T(8,128)(2,1)S(1)}, u32[]{:S(2)}, u32[]{:S(2)}) collective-permute-start(bf16[4,96,512]{2,1,0:T(8,128)(2,1)S(1)} %slice.801), channel_id=1, source_target_pairs={{0,48},{16,0},{32,16},{48,32},{1,49},{17,1},{33,17},{49,33},{2,50}... | collective-permute-start | bytes 1179656 | tf_op jit(solution)/shard_map/ag_down/ppermute | solution.py:37
  159.3 65.6 %collective-permute-start.30 = (bf16[1024,3072]{1,0:T(8,128)(2,1)}, bf16[1024,3072]{1,0:T(8,128)(2,1)}, u32[]{:S(2)}, u32[]{:S(2)}) collective-permute-start(bf16[1024,3072]{1,0:T(8,128)(2,1)} %ag_gu.1), channel_id=1, source_target_pairs={{0,1},{1,0},{2,3},{3,2},{4,5},{5,4},{6,7},{7,6},{8,9},{9,8},{10,11... | collective-permute-start | bytes 18874376 | tf_op jit(solution)/shard_map/ppermute | solution.py:24
  167.9 51.3 %collective-permute-start.39 = (bf16[3072,512]{1,0:T(8,128)(2,1)S(1)}, bf16[3072,512]{1,0:T(8,128)(2,1)}, u32[]{:S(2)}, u32[]{:S(2)}) collective-permute-start(bf16[3072,512]{1,0:T(8,128)(2,1)S(1)} %ag_down.1), channel_id=1, source_target_pairs={{0,1},{1,0},{2,3},{3,2},{4,5},{5,4},{6,7},{7,6},{8,9},{9,8},{10,11... | collective-permute-start | bytes 9437192 | tf_op jit(solution)/shard_map/ppermute | solution.py:24
  232.6 13.4 %collective-permute-start.40 = (bf16[256,1024]{1,0:T(8,128)(2,1)S(1)}, bf16[256,1024]{1,0:T(8,128)(2,1)S(1)}, u32[]{:S(2)}, u32[]{:S(2)}) collective-permute-start(bf16[256,1024]{1,0:T(8,128)(2,1)S(1)} %fusion.80), channel_id=1, source_target_pairs={{0,64},{1,65},{2,66},{3,67},{4,68},{5,69},{6,70},{7,71},{8,72},{9,... | collective-permute-start | bytes 1572872 | tf_op jit(solution)/shard_map/ppermute | solution.py:41
  347.8 14.4 %collective-permute-start.41 = (bf16[256,1024]{1,0:T(8,128)(2,1)S(1)}, bf16[256,1024]{1,0:T(8,128)(2,1)S(1)}, u32[]{:S(2)}, u32[]{:S(2)}) collective-permute-start(bf16[256,1024]{1,0:T(8,128)(2,1)S(1)} %add_convert_fusion.1), channel_id=1, source_target_pairs={{64,0},{65,1},{66,2},{67,3},{68,4},{69,5},{70,6},{71,7},{72,8},{73... | collective-permute-start | bytes 1572872 | tf_op jit(solution)/shard_map/ppermute | solution.py:41
  375.0 35.5 %collective-permute-start.46 = (bf16[256,1024]{1,0:T(8,128)(2,1)}, bf16[256,1024]{1,0:T(8,128)(2,1)S(1)}, u32[]{:S(2)}, u32[]{:S(2)}) collective-permute-start(bf16[256,1024]{1,0:T(8,128)(2,1)} %copy-done.80), channel_id=1, source_target_pairs={{0,1},{1,0},{2,3},{3,2},{4,5},{5,4},{6,7},{7,6},{8,9},{9,8},{10,11... | collective-permute-start | bytes 1572872 | tf_op jit(solution)/shard_map/ppermute | solution.py:24
  379.1 31.4 %collective-permute-start.47 = (bf16[256,3072]{1,0:T(8,128)(2,1)S(1)}, bf16[256,3072]{1,0:T(8,128)(2,1)S(1)}, u32[]{:S(2)}, u32[]{:S(2)}) collective-permute-start(bf16[256,3072]{1,0:T(8,128)(2,1)S(1)} %get-tuple-element.137), channel_id=1, source_target_pairs={{0,1},{1,0},{2,3},{3,2},{4,5},{5,4},{6,7},{7,6},{8,9},{9,8},{10,11... | collective-permute-start | bytes 4718600 | tf_op jit(solution)/shard_map/b2/g_gu/ppermute | solution.py:24
  407.8 21.0 %collective-permute-start.50 = (bf16[384,512]{1,0:T(8,128)(2,1)S(1)}, bf16[384,512]{1,0:T(8,128)(2,1)S(1)}, u32[]{:S(2)}, u32[]{:S(2)}) collective-permute-start(bf16[384,512]{1,0:T(8,128)(2,1)S(1)} %get-tuple-element.133), channel_id=1, source_target_pairs={{0,2},{1,3},{2,4},{3,5},{4,6},{5,7},{6,0},{7,1},{8,10},{9,11},{10,... | collective-permute-start | bytes 1179656 | tf_op jit(solution)/shard_map/b2/g_down/ppermute | solution.py:33
  409.0 19.8 %collective-permute-start.51 = (bf16[384,512]{1,0:T(8,128)(2,1)S(1)}, bf16[384,512]{1,0:T(8,128)(2,1)S(1)}, u32[]{:S(2)}, u32[]{:S(2)}) collective-permute-start(bf16[384,512]{1,0:T(8,128)(2,1)S(1)} %get-tuple-element.132), channel_id=1, source_target_pairs={{0,6},{1,7},{2,0},{3,1},{4,2},{5,3},{6,4},{7,5},{8,14},{9,15},{10,... | collective-permute-start | bytes 1179656 | tf_op jit(solution)/shard_map/b2/g_down/ppermute | solution.py:33
  417.3 20.5 %collective-permute-start.48 = (bf16[4,32,3072]{2,1,0:T(8,128)(2,1)S(1)}, bf16[4,32,3072]{2,1,0:T(8,128)(2,1)}, u32[]{:S(2)}, u32[]{:S(2)}) collective-permute-start(bf16[4,32,3072]{2,1,0:T(8,128)(2,1)S(1)} %get-tuple-element.179), channel_id=1, source_target_pairs={{0,16},{16,32},{32,48},{48,0},{1,17},{17,33},{33,49},{49,1},{2,18}... | collective-permute-start | bytes 2359304 | tf_op jit(solution)/shard_map/b2/g_gu/ppermute | solution.py:37
  418.9 18.9 %collective-permute-start.49 = (bf16[4,32,3072]{2,1,0:T(8,128)(2,1)S(1)}, bf16[4,32,3072]{2,1,0:T(8,128)(2,1)}, u32[]{:S(2)}, u32[]{:S(2)}) collective-permute-start(bf16[4,32,3072]{2,1,0:T(8,128)(2,1)S(1)} %get-tuple-element.178), channel_id=1, source_target_pairs={{0,48},{16,0},{32,16},{48,32},{1,49},{17,1},{33,17},{49,33},{2,50}... | collective-permute-start | bytes 2359304 | tf_op jit(solution)/shard_map/b2/g_gu/ppermute | solution.py:37
  430.0 44.0 %collective-permute-start.63 = (bf16[2,384,512]{2,1,0:T(8,128)(2,1)}, bf16[2,384,512]{2,1,0:T(8,128)(2,1)}, u32[]{:S(2)}, u32[]{:S(2)}) collective-permute-start(bf16[2,384,512]{2,1,0:T(8,128)(2,1)} %pad_maximum_fusion.24), channel_id=1, source_target_pairs={{0,6},{1,7},{2,0},{3,1},{4,2},{5,3},{6,4},{7,5},{8,14},{9,15},{10,... | collective-permute-start | bytes 2359304 | tf_op jit(solution)/shard_map/b2/rs_down/ppermute | solution.py:33
  431.8 42.2 %collective-permute-start.62 = (bf16[2,384,512]{2,1,0:T(8,128)(2,1)}, bf16[2,384,512]{2,1,0:T(8,128)(2,1)}, u32[]{:S(2)}, u32[]{:S(2)}) collective-permute-start(bf16[2,384,512]{2,1,0:T(8,128)(2,1)} %pad_maximum_fusion.23), channel_id=1, source_target_pairs={{0,2},{1,3},{2,4},{3,5},{4,6},{5,7},{6,0},{7,1},{8,10},{9,11},{10,... | collective-permute-start | bytes 2359304 | tf_op jit(solution)/shard_map/b2/rs_down/ppermute | solution.py:33
  471.2 35.5 %collective-permute-start.53 = (bf16[256,2048]{1,0:T(8,128)(2,1)}, bf16[256,2048]{1,0:T(8,128)(2,1)}, u32[]{:S(2)}, u32[]{:S(2)}) collective-permute-start(bf16[256,2048]{1,0:T(8,128)(2,1)} %bitcast.787), channel_id=1, source_target_pairs={{0,1},{1,0},{2,3},{3,2},{4,5},{5,4},{6,7},{7,6},{8,9},{9,8},{10,11... | collective-permute-start | bytes 3145736 | tf_op jit(solution)/shard_map/b2/g_qkv/ppermute | solution.py:24
  479.6 11.6 %collective-permute-start.92 = (bf16[384,512]{1,0:T(8,128)(2,1)S(1)}, bf16[384,512]{1,0:T(8,128)(2,1)S(1)}, u32[]{:S(2)}, u32[]{:S(2)}) collective-permute-start(bf16[384,512]{1,0:T(8,128)(2,1)S(1)} %fusion.127), channel_id=1, source_target_pairs={{0,8},{1,9},{2,10},{3,11},{4,12},{5,13},{6,14},{7,15},{8,0},{9,1},... | collective-permute-start | bytes 1179656 | tf_op jit(solution)/shard_map/b2/rs_down/ppermute | solution.py:28
  484.3 19.1 %collective-permute-start.65 = (bf16[2,256,512]{2,1,0:T(8,128)(2,1)}, bf16[2,256,512]{2,1,0:T(8,128)(2,1)S(1)}, u32[]{:S(2)}, u32[]{:S(2)}) collective-permute-start(bf16[2,256,512]{2,1,0:T(8,128)(2,1)} %pad_maximum_fusion.27), channel_id=1, source_target_pairs={{0,2},{1,3},{2,4},{3,5},{4,6},{5,7},{6,0},{7,1},{8,10},{9,11},{10,... | collective-permute-start | bytes 1572872 | tf_op jit(solution)/shard_map/b2/rs_out/ppermute | solution.py:33
  485.2 18.4 %collective-permute-start.67 = (bf16[2,256,512]{2,1,0:T(8,128)(2,1)}, bf16[2,256,512]{2,1,0:T(8,128)(2,1)}, u32[]{:S(2)}, u32[]{:S(2)}) collective-permute-start(bf16[2,256,512]{2,1,0:T(8,128)(2,1)} %pad_maximum_fusion.28), channel_id=1, source_target_pairs={{0,6},{1,7},{2,0},{3,1},{4,2},{5,3},{6,4},{7,5},{8,14},{9,15},{10,... | collective-permute-start | bytes 1572872 | tf_op jit(solution)/shard_map/b2/rs_out/ppermute | solution.py:33
  501.0 42.9 %collective-permute-start.55 = (bf16[8,32,3072]{2,1,0:T(8,128)(2,1)S(1)}, bf16[8,32,3072]{2,1,0:T(8,128)(2,1)S(1)}, u32[]{:S(2)}, u32[]{:S(2)}) collective-permute-start(bf16[8,32,3072]{2,1,0:T(8,128)(2,1)S(1)} %copy-done.73), channel_id=1, source_target_pairs={{0,48},{16,0},{32,16},{48,32},{1,49},{17,1},{33,17},{49,33},{2,50}... | collective-permute-start | bytes 4718600 | tf_op jit(solution)/shard_map/b2/rs_gu/ppermute | solution.py:37
  503.4 40.5 %collective-permute-start.54 = (bf16[8,32,3072]{2,1,0:T(8,128)(2,1)}, bf16[8,32,3072]{2,1,0:T(8,128)(2,1)S(1)}, u32[]{:S(2)}, u32[]{:S(2)}) collective-permute-start(bf16[8,32,3072]{2,1,0:T(8,128)(2,1)} %pad_maximum_fusion.16), channel_id=1, source_target_pairs={{0,16},{16,32},{32,48},{48,0},{1,17},{17,33},{33,49},{49,1},{2,18}... | collective-permute-start | bytes 4718600 | tf_op jit(solution)/shard_map/b2/rs_gu/ppermute | solution.py:37
  503.5 90.5 %collective-permute-start.94 = (bf16[96,512]{1,0:T(8,128)(2,1)S(1)}, bf16[96,512]{1,0:T(8,128)(2,1)S(1)}, u32[]{:S(2)}, u32[]{:S(2)}) collective-permute-start(bf16[96,512]{1,0:T(8,128)(2,1)S(1)} %pad_maximum_fusion.41), channel_id=1, source_target_pairs={{0,16},{16,32},{32,48},{48,0},{1,17},{17,33},{33,49},{49,1},{2,18}... | collective-permute-start | bytes 294920 | tf_op jit(solution)/shard_map/rs_down/ppermute | solution.py:37
  513.6 28.7 %collective-permute-start.69 = (bf16[32,512]{1,0:T(8,128)(2,1)S(1)}, bf16[32,512]{1,0:T(8,128)(2,1)S(1)}, u32[]{:S(2)}, u32[]{:S(2)}) collective-permute-start(bf16[32,512]{1,0:T(8,128)(2,1)S(1)} %get-tuple-element.243), channel_id=1, source_target_pairs={{0,16},{16,32},{32,48},{48,0},{1,17},{17,33},{33,49},{49,1},{2,18}... | collective-permute-start | bytes 98312 | tf_op jit(solution)/shard_map/rs_out/ppermute | solution.py:37
  514.4 27.9 %collective-permute-start.71 = (bf16[32,512]{1,0:T(8,128)(2,1)S(1)}, bf16[32,512]{1,0:T(8,128)(2,1)S(1)}, u32[]{:S(2)}, u32[]{:S(2)}) collective-permute-start(bf16[32,512]{1,0:T(8,128)(2,1)S(1)} %get-tuple-element.245), channel_id=1, source_target_pairs={{0,48},{16,0},{32,16},{48,32},{1,49},{17,1},{33,17},{49,33},{2,50}... | collective-permute-start | bytes 98312 | tf_op jit(solution)/shard_map/rs_out/ppermute | solution.py:37
  542.3 51.8 %collective-permute-start.96 = (bf16[96,512]{1,0:T(8,128)(2,1)S(1)}, bf16[96,512]{1,0:T(8,128)(2,1)S(1)}, u32[]{:S(2)}, u32[]{:S(2)}) collective-permute-start(bf16[96,512]{1,0:T(8,128)(2,1)S(1)} %pad_maximum_fusion.42), channel_id=1, source_target_pairs={{0,48},{16,0},{32,16},{48,32},{1,49},{17,1},{33,17},{49,33},{2,50}... | collective-permute-start | bytes 294920 | tf_op jit(solution)/shard_map/rs_down/ppermute | solution.py:37
  542.3 13.1 %collective-permute-start.70 = (bf16[64,512]{1,0:T(8,128)(2,1)S(1)}, bf16[64,512]{1,0:T(8,128)(2,1)S(1)}, u32[]{:S(2)}, u32[]{:S(2)}) collective-permute-start(bf16[64,512]{1,0:T(8,128)(2,1)S(1)} %pad_maximum_fusion.45), channel_id=1, source_target_pairs={{0,16},{16,32},{32,48},{48,0},{1,17},{17,33},{33,49},{49,1},{2,18}... | collective-permute-start | bytes 196616 | tf_op jit(solution)/shard_map/rs_out/ppermute | solution.py:37
  579.0 14.2 %collective-permute-start.75 = (bf16[128,2048]{1,0:T(8,128)(2,1)S(1)}, bf16[128,2048]{1,0:T(8,128)(2,1)S(1)}, u32[]{:S(2)}, u32[]{:S(2)}) collective-permute-start(bf16[128,2048]{1,0:T(8,128)(2,1)S(1)} %get-tuple-element.124), channel_id=1, source_target_pairs={{0,2},{1,3},{2,4},{3,5},{4,6},{5,7},{6,0},{7,1},{8,10},{9,11},{10,... | collective-permute-start | bytes 1572872 | tf_op jit(solution)/shard_map/b2/g_qkv/ppermute | solution.py:33
  593.8 28.6 %collective-permute-start.76 = (bf16[2,128,2048]{2,1,0:T(8,128)(2,1)S(1)}, bf16[2,128,2048]{2,1,0:T(8,128)(2,1)S(1)}, u32[]{:S(2)}, u32[]{:S(2)}) collective-permute-start(bf16[2,128,2048]{2,1,0:T(8,128)(2,1)S(1)} %pad_maximum_fusion.21), channel_id=1, source_target_pairs={{0,2},{1,3},{2,4},{3,5},{4,6},{5,7},{6,0},{7,1},{8,10},{9,11},{10,... | collective-permute-start | bytes 3145736 | tf_op jit(solution)/shard_map/rs_qkv/ppermute | solution.py:33
  595.8 26.7 %collective-permute-start.78 = (bf16[2,128,2048]{2,1,0:T(8,128)(2,1)S(1)}, bf16[2,128,2048]{2,1,0:T(8,128)(2,1)S(1)}, u32[]{:S(2)}, u32[]{:S(2)}) collective-permute-start(bf16[2,128,2048]{2,1,0:T(8,128)(2,1)S(1)} %pad_maximum_fusion.22), channel_id=1, source_target_pairs={{0,6},{1,7},{2,0},{3,1},{4,2},{5,3},{6,4},{7,5},{8,14},{9,15},{10,... | collective-permute-start | bytes 3145736 | tf_op jit(solution)/shard_map/rs_qkv/ppermute | solution.py:33
  608.0 16.0 %collective-permute-start.101 = (bf16[576,512]{1,0:T(8,128)(2,1)S(1)}, bf16[576,512]{1,0:T(8,128)(2,1)S(1)}, u32[]{:S(2)}, u32[]{:S(2)}) collective-permute-start(bf16[576,512]{1,0:T(8,128)(2,1)S(1)} %dynamic-slice_dynamic-update-slice_fusion), channel_id=1, source_target_pairs={{0,1},{1,0},{2,3},{3,2},{4,5},{5,4},{6,7},{7,6},{8,9},{9,8},{10,11... | collective-permute-start | bytes 1769480 | tf_op jit(solution)/shard_map/fin_a/ppermute | solution.py:24
  622.7 12.8 %collective-permute-start.79 = (bf16[128,2048]{1,0:T(8,128)(2,1)S(1)}, bf16[128,2048]{1,0:T(8,128)(2,1)S(1)}, u32[]{:S(2)}, u32[]{:S(2)}) collective-permute-start(bf16[128,2048]{1,0:T(8,128)(2,1)S(1)} %fusion.109), channel_id=1, source_target_pairs={{0,8},{1,9},{2,10},{3,11},{4,12},{5,13},{6,14},{7,15},{8,0},{9,1},... | collective-permute-start | bytes 1572872 | tf_op jit(solution)/shard_map/rs_qkv/ppermute | solution.py:28
  (152 other events, 1011.8 us)

commit v3 on v2

v3 whole, which is shorter than its diff:
```python
import functools

import jax
import jax.numpy as jnp
from jax import lax
from jax.experimental import pallas as pl
from jax.experimental.pallas import tpu as pltpu
from jax.sharding import PartitionSpec as P

epsilon = 1e-06
rope_base = 1000000.0
low = jnp.bfloat16
f32 = jnp.float32
MODEL = 1024
HEAD = 128
ROOT = HEAD ** (-0.5)


def tied(*values):
    return lax.optimization_barrier(values)


def swap_core(value):
    return lax.ppermute(value, "fsdp", [(i, i ^ 1) for i in range(16)])


def swap_z(value):
    return lax.ppermute(value, "fsdp", [(i, i ^ 8) for i in range(16)])


def move_y(value, step):
    pairs = [(i, (i & 8) | ((((i >> 1) + step) & 3) << 1) | (i & 1)) for i in range(16)]
    return lax.ppermute(value, "fsdp", pairs)


def move_x(value, step):
    return lax.ppermute(value, "dp", [(i, (i + step) % 4) for i in range(4)])


def move_section(value, step):
    return lax.ppermute(value, "section", [(0, 1)] if step > 0 else [(1, 0)])


def summed(value):
    for step in (1, 2, 4, 8):
        value = value + lax.ppermute(value, "fsdp", [(i, i ^ step) for i in range(16)])
    for step in (1, 2):
        value = value + lax.ppermute(value, "dp", [(i, i ^ step) for i in range(4)])
    return value


def pick(value, *where):
    start = list(where) + [0] * (value.ndim - len(where))
    size = [1] * len(where) + list(value.shape[len(where) :])
    return lax.dynamic_slice(value, start, size).reshape(value.shape[len(where) :])


def half_of(value, index, axis):
    width = value.shape[axis] // 2
    return lax.dynamic_slice_in_dim(value, index * width, width, axis)


def in_order(own, other, core, axis):
    first = jnp.where(core == 0, own, other)
    second = jnp.where(core == 0, other, own)
    return jnp.concatenate([first, second], axis=axis)


def placing_kernel(moves, sources_count, skipped, offsets, *refs):
    sources, outs, sems = refs[:sources_count], refs[sources_count + skipped : -1], refs[-1]
    copies = []
    for n, (source, index, row, column, rows, width, out) in enumerate(moves):
        block = sources[source].at[index, pl.ds(row, rows), pl.ds(column, width)]
        at = pl.multiple_of(offsets[n], 16)
        copies.append(pltpu.make_async_copy(block, outs[out].at[pl.ds(at, rows)], sems.at[n]))
    for copy in copies:
        copy.start()
    for copy in copies:
        copy.wait()


def place(pieces, moves, offsets, shapes, waits=()):
    return pl.pallas_call(
        functools.partial(placing_kernel, tuple(moves), len(pieces), len(waits)),
        out_shape=[jax.ShapeDtypeStruct(shape, low) for shape in shapes],
        in_specs=[pl.BlockSpec(memory_space=pltpu.SMEM)]
        + [pl.BlockSpec(memory_space=pl.ANY)] * (len(pieces) + len(waits)),
        out_specs=[pl.BlockSpec(memory_space=pltpu.VMEM)] * len(shapes),
        scratch_shapes=[pltpu.SemaphoreType.DMA((len(moves),))],
        compiler_params=pltpu.CompilerParams(vmem_limit_bytes=16 * 2**20),
    )(jnp.stack(offsets).astype(jnp.int32), *pieces, *waits)


def joining_kernel(core_ref, own, other, out, sems):
    rows, width = own.shape
    cut = rows // 2
    mine = pl.multiple_of(core_ref[0] * width, width)
    theirs = pl.multiple_of((1 - core_ref[0]) * width, width)
    upper, lower = pl.ds(0, cut), pl.ds(cut, cut)
    copies = (
        pltpu.make_async_copy(own, out.at[:, pl.ds(mine, width)], sems.at[0]),
        pltpu.make_async_copy(other.at[lower], out.at[upper, pl.ds(theirs, width)], sems.at[1]),
        pltpu.make_async_copy(other.at[upper], out.at[lower, pl.ds(theirs, width)], sems.at[2]),
    )
    for copy in copies:
        copy.start()
    for copy in copies:
        copy.wait()


def joined(own, core):
    rows, width = own.shape
    return pl.pallas_call(
        joining_kernel,
        out_shape=jax.ShapeDtypeStruct((rows, 2 * width), low),
        in_specs=[pl.BlockSpec(memory_space=pltpu.SMEM)] + [pl.BlockSpec(memory_space=pl.ANY)] * 2,
        out_specs=pl.BlockSpec(memory_space=pltpu.VMEM),
        scratch_shapes=[pltpu.SemaphoreType.DMA((3,))],
        compiler_params=pltpu.CompilerParams(vmem_limit_bytes=16 * 2**20),
    )(core.reshape(1).astype(jnp.int32), own, swap_core(own))


origins = [(0, 0), (1, 0), (0, 1), (1, 1), (0, 3), (1, 3), (0, 2), (1, 2)]


def near_y(pair):
    return move_y(pair, 1), move_y(pair, -1)


def far_y(behind, ahead):
    return move_y(behind[0], 1)[None], move_y(ahead[1], -1)[None]


def near_x(whole):
    return move_x(whole, 1), move_x(whole, -1)


def far_x(behind, ahead):
    return move_x(behind[:4], 1), move_x(ahead[4:], -1)


def added(left, right):
    return (left.astype(f32) + right.astype(f32)).astype(low)


def reduce_x_first(take, x):
    far = take((x + 2) & 3)
    cut = far.shape[0] // 2
    return move_x(far[:cut], 1), move_x(far[cut:], -1)


def reduce_x_ready(take, x, first):
    up, down = first
    cut = up.shape[0]
    after_it, before = take((x + 1) & 3), take((x - 1) & 3)
    after_it = jnp.concatenate([added(after_it[:cut], up), after_it[cut:]])
    before = jnp.concatenate([before[:cut], added(before[cut:], down)])
    return after_it, before


def reduce_x_third(take, x, second):
    own = take(x)
    return (own.astype(f32) + second[0].astype(f32) + second[1].astype(f32)).astype(low)


def reduce_x(values, x):
    def take(place):
        return pick(values, place)

    second = near_x_two(*reduce_x_ready(take, x, reduce_x_first(take, x)))
    return reduce_x_third(take, x, second)


def near_x_two(up, down):
    return move_x(up, 1), move_x(down, -1)


def near_y_two(up, down):
    return move_y(up, 1), move_y(down, -1)


def reduce_y_first(values, z, y):
    far = (y + 2) & 3
    return move_y(pick(values, z, far), 1), move_y(pick(values, 1 - z, far), -1)


def reduce_y_ready(values, z, y, first):
    up, down = first
    other, y_after, y_before = 1 - z, (y + 1) & 3, (y - 1) & 3
    after_it = jnp.stack([added(pick(values, z, y_after), up), pick(values, other, y_after)])
    before = jnp.stack([pick(values, z, y_before), added(pick(values, other, y_before), down)])
    return after_it, before


def reduce_y_second(values, z, y, first):
    return near_y_two(*reduce_y_ready(values, z, y, first))


def reduce_z(values, z, y, second):
    def total(k, zi):
        own = pick(values, zi, y)
        return (own.astype(f32) + second[0][k].astype(f32) + second[1][k].astype(f32)).astype(low)

    return added(total(0, z), swap_z(total(1, 1 - z)))


def by_chip(gradient):
    return gradient.reshape(2, 4, gradient.shape[0] // 8, gradient.shape[1])


def quarters(value):
    return value.reshape(4, value.shape[0] // 4, value.shape[1])


def gather_x(value, x):
    cut = value.shape[0] // 2
    behind, ahead = move_x(value, 1), move_x(value, -1)
    far = jnp.concatenate([move_x(behind[:cut], 1), move_x(ahead[cut:], -1)])
    ring = jnp.stack([value, ahead, far, behind, value, ahead, far, behind])
    return lax.dynamic_slice_in_dim(ring, (4 - x) & 3, 4, 0)


def packed(value):
    return jnp.concatenate([value[:, k : k + 512] for k in range(0, value.shape[1], 512)])


def unpacked(rows, part, width):
    blocks = [rows[:, k * part : (k + 1) * part] for k in range(width // 512)]
    return jnp.concatenate(blocks, axis=2).reshape(4 * part, width)


def finish(values, x, core):
    sizes = [v.shape for v in values]
    together = gather_x(jnp.concatenate([packed(v) for v in values]), x)
    chips, at = [], 0
    for part, width in sizes:
        n = part * width // 512
        chip = unpacked(together[:, at : at + n], part, width)
        if width == 3072:
            blocks = chip.reshape(4, part, 4, width // 4).transpose(2, 1, 0, 3)
            chip = blocks.reshape(4 * part, width)
        chips.append(chip)
        at += n
    mine = [half_of(chip, core, 0) for chip in chips]
    theirs = [half_of(chip, 1 - core, 0) for chip in chips]
    arrived = swap_core(jnp.concatenate([packed(t) for t in theirs]))
    outs, at = [], 0
    for (part, width), own in zip(sizes, mine):
        n = 2 * part * width // 512
        rows = arrived[at : at + n]
        at += n
        other = jnp.concatenate(
            [rows[k * 2 * part : (k + 1) * 2 * part] for k in range(width // 512)], axis=1
        )
        outs.append((own.astype(f32), other.astype(f32)))
    return outs


def row_scale(values):
    return lax.rsqrt(jnp.mean(values * values, axis=-1, keepdims=True) + epsilon)


def rotation_tables(length):
    half_size = HEAD // 2
    places = jnp.arange(length, dtype=f32)
    frequencies = rope_base ** (-jnp.arange(half_size, dtype=f32) * 2.0 / HEAD)
    angles = places[:, None] * frequencies[None, :]
    cosine, sine = jnp.cos(angles), jnp.sin(angles)
    return jnp.concatenate([cosine, cosine], 1), jnp.concatenate([-sine, sine], 1)


def norm_backward(upstream, normed, scaling, gain_vector):
    gain_part = jnp.sum(upstream * normed, axis=tuple(range(upstream.ndim - 1)))
    scaled = upstream * gain_vector
    return (
        scaling * (scaled - normed * jnp.mean(scaled * normed, axis=-1, keepdims=True)),
        gain_part,
    )


def dot(left, right):
    return jnp.dot(left, right, preferred_element_type=f32)


def dot_t(left, right):
    return lax.dot_general(left, right, (((1,), (1,)), ((), ())), preferred_element_type=f32)


def dot_first(left, right):
    return lax.dot_general(left, right, (((0,), (0,)), ((), ())), preferred_element_type=f32)


def turned(values, cosine, sine):
    return values * cosine + pltpu.roll(values, HEAD // 2, 1) * sine


def scaled_heads(qkv, query_gain, key_gain, cosine, sine):
    q = jnp.concatenate([qkv[:, :HEAD], qkv[:, HEAD : 2 * HEAD]])
    k, v = qkv[:, 2 * HEAD : 3 * HEAD], qkv[:, 3 * HEAD :].astype(low)
    q_scale, k_scale = row_scale(q), row_scale(k)
    qn, kn = q * q_scale, k * k_scale
    cosine_two, sine_two = jnp.concatenate([cosine] * 2), jnp.concatenate([sine] * 2)
    qr = turned(qn * query_gain, cosine_two, sine_two).astype(low)
    kr = turned(kn * key_gain, cosine, sine).astype(low)
    return qr, kr, v, qn, kn, q_scale, k_scale


def soft_scores(qr, kr):
    scores = dot_t(qr, kr) * ROOT
    query = lax.broadcasted_iota(jnp.int32, scores.shape, 0) & 127
    key = lax.broadcasted_iota(jnp.int32, scores.shape, 1)
    scores = jnp.where(query >= key, scores, -1e30)
    p = jnp.exp(scores - jnp.max(scores, axis=-1, keepdims=True))
    return p / jnp.sum(p, axis=-1, keepdims=True)


def attention_kernel(first, *refs):
    if first:
        hidden, gain, qg, kg, cosine, sine, w, wo, out, a1, qkv_out, att_out = refs
    else:
        sofar, a1, qg, kg, cosine, sine, w, wo, out, qkv_out, att_out = refs

    @pl.when(pl.program_id(0) == 0)
    def _():
        if first:
            h = hidden[...]
            a1[...] = (h * row_scale(h) * gain[...]).astype(low)
            out[...] = h
        else:
            out[...] = sofar[...]

    qkv = dot(a1[...], w[...])
    qkv_out[...] = qkv
    for s in range(2):
        rows = slice(128 * s, 128 * s + 128)
        qr, kr, v, *_ = scaled_heads(qkv[rows], qg[...], kg[...], cosine[...], sine[...])
        att = dot(soft_scores(qr, kr).astype(low), v).astype(low)
        att_out[rows, :HEAD] = att[:128]
        att_out[rows, HEAD:] = att[128:]
    out[...] += dot(att_out[...], wo[...])


def whole(shape):
    return pl.BlockSpec(shape, lambda i: (0,) * len(shape))


def columns_at(rows, width):
    return pl.BlockSpec((rows, width), lambda i: (0, i))


def rows_at(rows, width, start):
    return pl.BlockSpec((rows, width), lambda i: (start + i, 0))


def shape_of(rows, width, kind):
    return jax.ShapeDtypeStruct((rows, width), kind)


def call(kernel, steps, ins, outs, waits=()):
    specs, values = [p[0] for p in ins], [p[1] for p in ins]
    specs += [pl.BlockSpec(memory_space=pl.ANY)] * len(waits)
    values += list(waits)

    def body(*refs):
        kernel(*refs[: len(ins)], *refs[len(ins) + len(waits) :])

    return pl.pallas_call(
        body,
        grid=(steps,),
        in_specs=specs,
        out_specs=[p[0] for p in outs],
        out_shape=[p[1] for p in outs],
        compiler_params=pltpu.CompilerParams(vmem_limit_bytes=28 * 2**20),
        cost_estimate=pl.CostEstimate(flops=2**20, bytes_accessed=2**16, transcendentals=0),
    )(*values)


BLOCK = (256, MODEL)


def attention_half(half, state, w_half, w_out, gains, tables, waits=()):
    mixer_gain, query_gain, key_gain, _ = gains
    head, table = whole((1, HEAD)), whole((128, HEAD))
    ins = [(whole(BLOCK), state[0])]
    ins.append((whole((1, MODEL)), mixer_gain[None]) if half == 0 else (whole(BLOCK), state[1]))
    ins += [(head, query_gain[None]), (head, key_gain[None]), (table, tables[0]), (table, tables[1])]
    ins += [(columns_at(MODEL, 512), w_half), (rows_at(256, MODEL, 4 * half), w_out)]
    outs = [(whole(BLOCK), shape_of(*BLOCK, f32))]
    if half == 0:
        outs.append((whole(BLOCK), shape_of(*BLOCK, low)))
    outs.append((columns_at(256, 512), shape_of(256, 2048, f32)))
    outs.append((columns_at(256, 256), shape_of(256, 1024, low)))
    return call(functools.partial(attention_kernel, half == 0), 4, ins, outs, waits)


def dense_kernel(first, *refs):
    if first:
        hidden, gain, w, wd, out, a2, gu_out, z_out = refs
    else:
        sofar, a2, w, wd, out, gu_out, z_out = refs

    @pl.when(pl.program_id(0) == 0)
    def _():
        if first:
            h = hidden[...]
            a2[...] = (h * row_scale(h) * gain[...]).astype(low)
            out[...] = h
        else:
            out[...] = sofar[...]

    gu = dot(a2[...], w[...])
    gu_out[...] = gu.astype(gu_out.dtype)
    gate, up = gu[:, :512], gu[:, 512:]
    z = (gate * jax.nn.sigmoid(gate) * up).astype(low)
    z_out[...] = z
    out[...] += dot(z, wd[...])


def dense_half(half, state, w_half, w_down, gains):
    ins = [(whole(BLOCK), state[0])]
    ins.append((whole((1, MODEL)), gains[3][None]) if half == 0 else (whole(BLOCK), state[1]))
    ins += [(columns_at(MODEL, 1024), w_half), (rows_at(512, MODEL, 3 * half), w_down)]
    outs = [(whole(BLOCK), shape_of(*BLOCK, f32))]
    if half == 0:
        outs.append((whole(BLOCK), shape_of(*BLOCK, low)))
    outs.append((columns_at(256, 1024), shape_of(256, 3072, f32)))
    outs.append((columns_at(256, 512), shape_of(256, 1536, low)))
    return call(functools.partial(dense_kernel, half == 0), 3, ins, outs)


def forward_mixer(hidden, w_qkv, w_out, gains, tables, between=None):
    part, a1, qkv_0, att_0 = attention_half(0, (hidden,), w_qkv[0], w_out, gains, tables)
    waits = between(part) if between is not None else ()
    after_mixer, qkv_1, att_1 = attention_half(1, (part, a1), w_qkv[1], w_out, gains, tables, waits)
    return after_mixer, (hidden, a1, (qkv_0, qkv_1), (att_0, att_1), after_mixer)


def forward_dense(after_mixer, w_gu, w_down, gains):
    part, a2, gu_0, z_0 = dense_half(0, (after_mixer,), w_gu[0], w_down, gains)
    out, gu_1, z_1 = dense_half(1, (part, a2), w_gu[1], w_down, gains)
    return out, (a2, (gu_0, gu_1), (z_0, z_1))


def forward(hidden, weights, gains, tables):
    w_qkv, w_out, w_gu, w_down = weights
    after_mixer, saved = forward_mixer(hidden, w_qkv, w_out, gains, tables)
    out, saved_dense = forward_dense(after_mixer, w_gu, w_down, gains)
    return out, saved + saved_dense


def dense_back_kernel(first, *refs):
    sofar, refs = (None, refs) if first else (refs[0], refs[1:])
    dm, wd, gu, w, dgu_out, da2 = refs

    @pl.when(pl.program_id(0) == 0)
    def _():
        da2[...] = jnp.zeros_like(da2) if first else sofar[...]

    dz = dot_t(dm[...], wd[...])
    gate, up = gu[:, :512], gu[:, 512:]
    sig = jax.nn.sigmoid(gate)
    dg = (dz * up * sig * (1.0 + gate * (1.0 - sig))).astype(low)
    du = (dz * (gate * sig)).astype(low)
    dgu_out[:, :512] = dg
    dgu_out[:, 512:] = du
    da2[...] += dot_t(dgu_out[...], w[...])


def dense_back_half(half, sofar, dm, gu, w_half, w_down):
    ins = [] if half == 1 else [(whole(BLOCK), sofar)]
    ins += [(whole(BLOCK), dm), (rows_at(512, MODEL, 3 * half), w_down)]
    ins += [(columns_at(256, 1024), gu), (columns_at(MODEL, 1024), w_half)]
    outs = [(columns_at(256, 1024), shape_of(256, 3072, low)), (whole(BLOCK), shape_of(*BLOCK, f32))]
    kernel = functools.partial(dense_back_kernel, half == 1)
    return call(kernel, 3, ins, outs)


def normed_back(upstream, normed, scale, gain):
    gain_part = jnp.sum(upstream * normed, axis=0, keepdims=True)
    scaled = upstream * gain
    return scale * (scaled - normed * jnp.mean(scaled * normed, axis=-1, keepdims=True)), gain_part


def attention_back_kernel(first, *refs):
    sofar, refs = (None, refs) if first else (refs[:3], refs[3:])
    dr, wo, qkv, qg, kg, cosine, sine, w, dqkv_out, da1, q_grad, k_grad = refs

    @pl.when(pl.program_id(0) == 0)
    def _():
        for k, ref in enumerate((da1, q_grad, k_grad)):
            ref[...] = jnp.zeros_like(ref) if first else sofar[k][...]

    datt = dot_t(dr[...], wo[...]).astype(low)
    for s in range(2):
        rows = slice(128 * s, 128 * s + 128)
        cos, sin = cosine[...], sine[...]
        qr, kr, v, qn, kn, q_scale, k_scale = scaled_heads(qkv[rows, :], qg[...], kg[...], cos, sin)
        p = soft_scores(qr, kr)
        do = jnp.concatenate([datt[rows, :HEAD], datt[rows, HEAD:]])
        dp = dot_t(do, v)
        dv = dot_first(p.astype(low), do)
        ds = (p * (dp - jnp.sum(dp * p, axis=-1, keepdims=True))).astype(low)
        dqr, dkr = dot(ds, kr) * ROOT, dot_first(ds, qr) * ROOT
        cos_two, sin_two = jnp.concatenate([cos] * 2), jnp.concatenate([sin] * 2)
        dq, q_part = normed_back(turned(dqr, cos_two, -sin_two), qn, q_scale, qg[...])
        dk, k_part = normed_back(turned(dkr, cos, -sin), kn, k_scale, kg[...])
        q_grad[...] += q_part
        k_grad[...] += k_part
        dq = dq.astype(low)
        dqkv_out[rows, :HEAD] = dq[:128]
        dqkv_out[rows, HEAD : 2 * HEAD] = dq[128:]
        dqkv_out[rows, 2 * HEAD : 3 * HEAD] = dk.astype(low)
        dqkv_out[rows, 3 * HEAD :] = dv.astype(low)
    da1[...] += dot_t(dqkv_out[...], w[...])


def attention_back_half(half, sofar, dr, qkv, w_half, w_out, gains, tables, waits=()):
    head, table = whole((1, HEAD)), whole((128, HEAD))
    ins = [] if half == 1 else [(whole(BLOCK), sofar[0]), (head, sofar[1]), (head, sofar[2])]
    ins += [(whole(BLOCK), dr), (rows_at(256, MODEL, 4 * half), w_out), (columns_at(256, 512), qkv)]
    ins += [(head, gains[1][None]), (head, gains[2][None]), (table, tables[0]), (table, tables[1])]
    ins += [(columns_at(MODEL, 512), w_half)]
    outs = [(columns_at(256, 512), shape_of(256, 2048, low)), (whole(BLOCK), shape_of(*BLOCK, f32))]
    outs += [(head, shape_of(1, HEAD, f32))] * 2
    kernel = functools.partial(attention_back_kernel, half == 1)
    return call(kernel, 4, ins, outs, waits)


def backward(cotangent, saved, weights, gains, tables, between=None):
    w_qkv, w_out, w_gu, w_down = weights
    mixer_gain, query_gain, key_gain, dense_gain = gains
    hidden, a1, qkv, att, after_mixer, a2, gu, z = saved
    dm = cotangent.astype(low)
    dgu_1, da2 = dense_back_half(1, None, dm, gu[1], w_gu[1], w_down)
    dgu_0, da2 = dense_back_half(0, da2, dm, gu[0], w_gu[0], w_down)
    if between is not None:
        da2 = between[0]((dgu_0, dgu_1), da2)
    scale_two = row_scale(after_mixer)
    part, dense_gain_grad = norm_backward(da2, after_mixer * scale_two, scale_two, dense_gain)
    dh2 = cotangent + part
    dr = dh2.astype(low)
    g_out = None
    if between is not None:
        dr, g_out = between[1](dr)
    dqkv_1, *so_far = attention_back_half(1, None, dr, qkv[1], w_qkv[1], w_out, gains, tables)
    if between is not None:
        dr = between[3](dr, dqkv_1, g_out)
    dqkv_0, da1, q_grad, k_grad = attention_back_half(
        0, so_far, dr, qkv[0], w_qkv[0], w_out, gains, tables
    )
    if between is not None:
        da1 = between[2]((dqkv_0, dqkv_1), da1, g_out)
    scale_one = row_scale(hidden)
    part, mixer_gain_grad = norm_backward(da1, hidden * scale_one, scale_one, mixer_gain)
    dh = dh2 + part
    return dh, (mixer_gain_grad, dense_gain_grad, q_grad[0], k_grad[0])


def product(left, left_other, right, right_other):
    both_left = jnp.concatenate([left, left_other])
    both_right = jnp.concatenate([right, right_other])
    dims = (((0,), (0,)), ((), ()))
    return lax.dot_general(both_left, both_right, dims, preferred_element_type=f32).astype(low)


def on_device(
    boundary,
    mixer_gain,
    query_weight,
    key_weight,
    value_weight,
    output_weight,
    query_gain,
    key_gain,
    dense_gain,
    gate_weight,
    up_weight,
    down_weight,
):
    first_section = lax.axis_index("section") == 0
    x = lax.axis_index("dp")
    place_at = lax.axis_index("fsdp")
    core, y, z = place_at & 1, (place_at >> 1) & 3, place_at >> 3
    spot = (x, z, y)
    local = boundary[0, :, 0].astype(f32).reshape(256, MODEL)

    gain_tile = jnp.stack(
        [mixer_gain[0], dense_gain[0], jnp.pad(query_gain[0], (0, 56)), jnp.pad(key_gain[0], (0, 56))],
        axis=1,
    )
    gain_tile = jnp.pad(gain_tile, ((0, 0), (0, 124)))

    def column_half(index):
        def cut(value):
            return half_of(value[0], index, 1)

        def mixed(parts, widths):
            halves = [cut(p) for p in parts]
            blocks = range(halves[0].shape[1] // widths[0])
            return [h[:, b * w : (b + 1) * w] for b in blocks for h, w in zip(halves, widths)]

        def rows_beside(value):
            half = cut(value)
            return [half[k : k + 64] for k in range(0, half.shape[0], 64)]

        pieces = mixed((query_weight, key_weight, value_weight), (256, 128, 128)) + [gain_tile]
        pieces += rows_beside(output_weight)
        pieces += mixed((gate_weight, up_weight), (512, 512)) + rows_beside(down_weight)
        return jnp.concatenate(pieces, axis=1)

    chip = in_order(column_half(core), swap_core(column_half(1 - core)), core, 0)
    zero = jnp.zeros_like(z)
    z_own = z ^ core

    with jax.named_scope("ag_dense"):
        d_0 = lax.dynamic_slice(chip, (x * 32, zero + 3200), (32, 4608))
        d_z = swap_z(d_0)
        d_pair = jnp.stack([d_0, d_z])
        d_near = near_y(d_pair)
        m_0 = chip[:, :3200]
        m_z = swap_z(m_0)
        d_near, m_z = tied(d_near, m_z)
        d_far = far_y(*d_near)
        d_all = jnp.concatenate([d_pair, *d_near, *d_far])
        d_x = near_x(d_all)
    with jax.named_scope("ag_mixer"):
        m_pair = jnp.stack([m_0, m_z])
        m_near = near_y(m_pair)
        m_near, d_x = tied(m_near, d_x)
        m_far = far_y(*m_near)
        moves, offsets = [], []
        spots = [(0, 0), (0, 1), (1, 0), (1, 1), (2, 0), (2, 1), (3, 0), (4, 0)]
        for (piece, index), (dz, dy) in zip(spots, origins):
            moves.append((piece, index, 0, 0, 128, 2176, 0))
            offsets.append(((z ^ dz) * 4 + ((y - dy) & 3)) * 128)
            block = ((z_own ^ dz) * 4 + ((y - dy) & 3)) * 256
            for k in range(2):
                for m in range(2):
                    moves.append((piece, index, 64 * k, 2176 + 512 * m, 64, 512, 1))
                    offsets.append(block + 128 * k + 64 * m)
        own_qkv, own_out = place(
            (m_pair, *m_near, *m_far), moves, offsets, ((MODEL, 2176), (2048, 512))
        )
        w_qkv = (own_qkv, swap_core(own_qkv))
        w_out = joined(own_out, core)
    tile = own_qkv[:, 2048:2052].astype(f32)
    gains = (
        tile[:, 0],
        tile[:, 2].reshape(16, 64)[:, :8].reshape(HEAD),
        tile[:, 3].reshape(16, 64)[:, :8].reshape(HEAD),
        tile[:, 1],
    )
    tables = rotation_tables(128)
    d_x_far = far_x(*d_x)

    def place_dense(part):
        moves, offsets = [], []
        for piece, dx in enumerate((0, 1, 3, 2, 2)):
            turn = (x - dx) & 3
            kept = range(4) if piece == 3 else range(4, 8) if piece == 4 else range(8)
            for index, n in enumerate(kept):
                dz, dy = origins[n]
                moves.append((piece, index, 0, 0, 32, 3072, 0))
                offsets.append(((z ^ dz) * 4 + ((y - dy) & 3)) * 128 + turn * 32)
                block = ((z_own ^ dz) * 4 + ((y - dy) & 3)) * 384 + (turn >> 1) * 192
                for m in range(3):
                    moves.append((piece, index, 0, 3072 + 512 * m, 32, 512, 1))
                    offsets.append(block + 64 * m + (turn & 1) * 32)
        return place((d_all, *d_x, *d_x_far), moves, offsets, ((MODEL, 3072), (3072, 512)), (part,))

    own_dense = []

    def between_halves(part):
        own_dense.extend(place_dense(part))
        return (own_dense[0],)

    with jax.named_scope("f1"):
        early_mixer, _ = forward_mixer(local, w_qkv, w_out, gains, tables, between_halves)
    with jax.named_scope("ag_dense"):
        own_gu, own_down = own_dense
        w_gu = (own_gu, swap_core(own_gu))
        w_down = joined(own_down, core)
    weights = (w_qkv, w_out, w_gu, w_down)
    with jax.named_scope("f1"):
        early, _ = forward_dense(early_mixer, w_gu, w_down, gains)
    arrived = move_section(early.astype(low), 1).astype(f32)
    with jax.named_scope("f2"):
        out, saved = forward(jnp.where(first_section, local, arrived), weights, gains, tables)
    _, a1, _, att, _, a2, _, z_low = saved
    with jax.named_scope("b1"):
        early_dh, _ = backward(local, saved, weights, gains, tables)
    returned = move_section(early_dh.astype(low), -1).astype(f32)
    cotangent = jnp.where(first_section, returned, local)

    acts = jnp.concatenate([a1, att[1], att[0], a2, z_low[1], z_low[0]], axis=1)
    acts = swap_core(acts)
    a1_o, att_o = acts[:, :1024], (acts[:, 1024:2048], acts[:, 2048:3072])
    a2_o, z_o = acts[:, 3072:4096], (acts[:, 4096:5632], acts[:, 5632:])

    def by_halves(left, left_other, right, right_other):
        parts = [product(a, b, right, right_other) for a, b in zip(left, left_other)]
        return by_chip(jnp.concatenate(parts))

    cot_mine, cot_theirs = half_of(cotangent, core, 1), half_of(cotangent, 1 - core, 1)
    z_flip = z ^ core
    done = {}

    def after_dgu(dgu, da2):
        with jax.named_scope("g_gu"):
            g_gu = product(a2, a2_o, dgu[0], swap_core(dgu[1])).reshape(8, 128, 3072)
            da2, g_gu = tied(da2, g_gu)

            def columns_of(place):
                return lax.dynamic_slice_in_dim(g_gu, place * 768, 768, 2)

            done["gu"] = (columns_of, reduce_x_first(columns_of, x))
        with jax.named_scope("g_down"):
            dm_o = swap_core(cot_theirs.astype(low))
            g_down = by_halves(z_low, z_o, cot_mine.astype(low), dm_o)
            da2, g_down = tied(da2, g_down)
            done["down"] = g_down
        return da2

    def after_dr(dr):
        with jax.named_scope("g_out"):
            dr_o = swap_core(half_of(dr, 1 - core, 1))
            g_out = by_halves(att, att_o, half_of(dr, core, 1), dr_o)
            g_do = jnp.concatenate([done["down"], g_out], axis=2)
        with jax.named_scope("rs_do"):
            done["do"] = reduce_y_first(g_do, z_flip, y)
        with jax.named_scope("rs_gu"):
            columns_of, first = done["gu"]
            ready = reduce_x_ready(columns_of, x, first)
            dr, ready, g_do = tied(dr, ready, g_do)
            done["gu2"] = near_x_two(*ready)
        return dr, g_do

    def between_heads(dr, dqkv_1, g_do):
        with jax.named_scope("g_qkv"):
            done["dqkv_o"] = swap_core(dqkv_1)
        with jax.named_scope("rs_do"):
            first, dqkv_1 = tied(done["do"], dqkv_1)
            ready = reduce_y_ready(g_do, z_flip, y, first)
            dr, ready = tied(dr, ready)
            done["do2"] = near_y_two(*ready)
        return dr

    def after_attention(dqkv, da1, g_do):
        own, second_gu, second = tied(dqkv[0], done["gu2"], done["do2"])
        with jax.named_scope("g_qkv"):
            g_qkv = by_chip(product(a1, a1_o, own, done["dqkv_o"]))
        with jax.named_scope("rs_qg"):
            mine = reduce_x_third(done["gu"][0], x, second_gu).reshape(2, 4, 128, 768)
            both_parts = jnp.concatenate([g_qkv, mine], axis=3)
            da1, both_parts = tied(da1, both_parts)
            done["qg"] = (both_parts, reduce_y_first(both_parts, z, y))
        with jax.named_scope("rs_do"):
            done["s_do"] = reduce_z(g_do, z_flip, y, second)
        return da1

    with jax.named_scope("b2"):
        dh, gain_grads = backward(
            cotangent, saved, weights, gains, tables, (after_dgu, after_dr, after_attention, between_heads)
        )
    endpoints = jnp.where(first_section, dh, out).reshape(1, 2, 1, 128, MODEL)
    with jax.named_scope("rs_qg"):
        g_qg, first = done["qg"]
        s_qg = reduce_z(g_qg, z, y, reduce_y_second(g_qg, z, y, first))
    with jax.named_scope("rs_x"):
        s_do, s_qkv = quarters(done["s_do"][:384]), quarters(s_qg[:, :2048])
        s_o = quarters(done["s_do"][384:])
        blocks = [s_qkv[:, :, k : k + 512] for k in range(0, 2048, 512)] + [s_do, s_o]
        mine = reduce_x(jnp.concatenate(blocks, axis=1), x)
        m_qkv = jnp.concatenate([mine[k : k + 32] for k in range(0, 128, 32)], axis=1)
        m_gu = jnp.concatenate([s_qg[k : k + 32, 2048:] for k in range(0, 128, 32)], axis=1)
    with jax.named_scope("fin"):
        parts = (m_qkv, m_gu, mine[128:224], mine[224:])
        qkv, gu, down, out_w = finish(parts, x, core)

    def both(pair, start, width, block=None):
        block = block or pair[0].shape[1]

        def part(value):
            starts = range(start, value.shape[1], block)
            return jnp.concatenate([value[:, k : k + width] for k in starts], axis=1)

        return in_order(*(part(p) for p in pair), core, 1)[None]

    sums = summed(jnp.concatenate(gain_grads).reshape(18, 128)).reshape(-1)

    def gain_rows(start, width):
        return lax.dynamic_slice_in_dim(sums, start + place_at * width, width, 0)[None]

    return (
        endpoints,
        gain_rows(0, 64),
        both(qkv, 0, 256, 512),
        both(qkv, 256, 128, 512),
        both(qkv, 384, 128, 512),
        both(out_w, 0, 512),
        gain_rows(2048, 8),
        gain_rows(2176, 8),
        gain_rows(1024, 64),
        both(gu, 0, 512, 1024),
        both(gu, 512, 512, 1024),
        both(down, 0, 512),
    )


def solution(mesh):
    placed = (
        P("section", None, ("dp", "fsdp"), None, None),
        P("section", "fsdp"),
        P("section", "fsdp", None),
        P("section", "fsdp", None),
        P("section", "fsdp", None),
        P("section", "fsdp", None),
        P("section", "fsdp"),
        P("section", "fsdp"),
        P("section", "fsdp"),
        P("section", "fsdp", None),
        P("section", "fsdp", None),
        P("section", "fsdp", None),
    )
    return jax.shard_map(
        on_device,
        mesh=mesh,
        in_specs=placed,
        out_specs=(
            P("section", None, ("dp", "fsdp"), None, None),
            P("section", "fsdp"),
            P("section", "fsdp", None),
            P("section", "fsdp", None),
            P("section", "fsdp", None),
            P("section", "fsdp", None),
            P("section", "fsdp"),
            P("section", "fsdp"),
            P("section", "fsdp"),
            P("section", "fsdp", None),
            P("section", "fsdp", None),
            P("section", "fsdp", None),
        ),
        check_vma=False,
    )
```

time: 685 us -> 592 us (0.86)
  matrix products: 140 us -> 12.8 us
  Pallas kernels: 19.2 us -> 124 us
  starting transfers between devices: 160 us -> 88.8 us
  waiting for transfers between devices: 167 us -> 234 us
  local copies, waits for them, and re-layouts: 116 us -> 77.9 us
  other arithmetic: 67.2 us -> 44.4 us
    dot_general x34 -> x0, matrix products: 108 us -> none  [the longest x12 48.8 us: dot(): return jnp.dot(left, right, preferred_element_type=f32)]
    pallas_call x4 -> x20, Pallas kernels: 19.2 us -> 124 us  [the longest x16 111 us: call(): pl.pallas_call(body, grid=(steps,), in_specs=specs, out_specs=[p[0] for p...]
    ppermute x32 -> x16, waiting for transfers between devices: 46.1 us -> 98.7 us  [move_y(): return lax.ppermute(value, 'fsdp', pairs)]
    ppermute x19 -> x11, starting transfers between devices: 53.8 us -> 23.9 us  [swap_core(): return lax.ppermute(value, 'fsdp', [(i, i ^ 1) for i in range(16)])]
    unnamed x247 -> x251, local copies, waits for them, and re-layouts: 21.6 us -> 51.3 us
    reshape x11 -> x2, local copies, waits for them, and re-layouts: 23.4 us -> 0.67 us  [the longest x1 0.57 us: finish(): blocks = chip.reshape(4, part, 4, width // 4).transpose(2, 1, 0, 3)]
    ppermute x19 -> x11, waiting for transfers between devices: 1.58 us -> 19.9 us  [swap_core(): return lax.ppermute(value, 'fsdp', [(i, i ^ 1) for i in range(16)])]
    ppermute x32 -> x16, starting transfers between devices: 38 us -> 22.8 us  [move_y(): return lax.ppermute(value, 'fsdp', pairs)]
  transfers between devices with their start and end apart: 102 -> 55, of which waited for: 38 -> 28; matrix products, arithmetic and copies ran while one was open for 28% -> 9% of each run, Pallas kernels for 3% -> 14%
where the time goes in v3:
time: 592 us; the launch traced here: 585 us
  waiting for transfers between devices  234 us (40%)
  Pallas kernels  124 us (21%)
  starting transfers between devices  88.8 us (15%)
  local copies, waits for them, and re-layouts  77.9 us (13%)
  other arithmetic  44.4 us (8%)
  matrix products  12.8 us (2%)
    pallas_call x16, Pallas kernels, call(): pl.pallas_call(body, grid=(steps,), in_specs=specs, out_specs=[p[0] for p...  111 us
    ppermute x16, waiting for transfers between devices, move_y(): return lax.ppermute(value, 'fsdp', pairs)  98.7 us
    ppermute x16, waiting for transfers between devices, move_x(): return lax.ppermute(value, 'dp', [(i, (i + step) % 4) for i in range(4)])  59.6 us
    unnamed x251, local copies, waits for them, and re-layouts  51.3 us
    ppermute x2, waiting for transfers between devices, move_section(): return lax.ppermute(value, 'section', [(0, 1)] if step > 0 else [(1, 0)])  24.6 us
    ppermute x4, waiting for transfers between devices, swap_z(): return lax.ppermute(value, 'fsdp', [(i, i ^ 8) for i in range(16)])  24.2 us
    ppermute x11, starting transfers between devices, swap_core(): return lax.ppermute(value, 'fsdp', [(i, i ^ 1) for i in range(16)])  23.9 us
    ppermute x16, starting transfers between devices, move_y(): return lax.ppermute(value, 'fsdp', pairs)  22.8 us
  transfers between devices with their start and end apart: 55, of which 28 were waited for; matrix products, arithmetic and copies ran while one was open for 9% of the time, Pallas kernels for 14%

profile of v3, /device:TPU:1, one launch (start us, length us, event | category | flops | bytes accessed | tf_op | source)
XLA Modules:
  0.0 584.9 jit_solution(2699740105498927344)
XLA Ops:
  23.3 3.8 collective-permute-start.1
  27.2 6.9 %collective-permute-done.1 = bf16[32,4608]{1,0:T(8,128)(2,1)S(1)} collective-permute-done((bf16[32,4608]{1,0:T(8,128)(2,1)S(1)}, bf16[32,4608]{1,0:T(8,128)(2,1)S(1)}, u32[]{:S(2)}, u32[]{:S(2)}) %collective-permute-start.1) | collective-permute-done | bytes 294944 | tf_op jit(solution)/shard_map/ag_dense/ppermute | solution.py:28
  37.1 14.6 %collective-permute-done.4 = bf16[128,3200]{1,0:T(8,128)(2,1)S(1)} collective-permute-done((bf16[128,3200]{1,0:T(8,128)(2,1)S(1)}, bf16[128,3200]{1,0:T(8,128)(2,1)S(1)}, u32[]{:S(2)}, u32[]{:S(2)}) %collective-permute-start.4) | collective-permute-done | bytes 819232 | tf_op jit(solution)/shard_map/ag_dense/ppermute | solution.py:28
  54.7 6.1 %collective-permute-done.7 = bf16[32,4608]{1,0:T(8,128)(2,1)S(1)} collective-permute-done((bf16[32,4608]{1,0:T(8,128)(2,1)S(1)}, bf16[32,4608]{1,0:T(8,128)(2,1)S(1)}, u32[]{:S(2)}, u32[]{:S(2)}) %collective-permute-start.7) | collective-permute-done | bytes 294944 | tf_op jit(solution)/shard_map/ag_dense/ppermute | solution.py:33
  66.5 33.6 %collective-permute-done.5.refs_1_ = bf16[2,128,3200]{2,1,0:T(8,128)(2,1)S(1)} collective-permute-done((bf16[2,128,3200]{2,1,0:T(8,128)(2,1)S(1)}, bf16[2,128,3200]{2,1,0:T(8,128)(2,1)S(1)}, u32[]{:S(2)}, u32[]{:S(2)}) %collective-permute-start.5) | collective-permute-done | bytes 1638432 | tf_op jit(solution)/shard_map/ag_mixer/ppermute | solution.py:33
  100.1 13.1 %collective-permute-done.9.refs_1_ = bf16[8,32,4608]{2,1,0:T(8,128)(2,1)} collective-permute-done((bf16[8,32,4608]{2,1,0:T(8,128)(2,1)S(1)}, bf16[8,32,4608]{2,1,0:T(8,128)(2,1)}, u32[]{:S(2)}, u32[]{:S(2)}) %collective-permute-start.9) | collective-permute-done | bytes 2359328 | tf_op jit(solution)/shard_map/ag_dense/ppermute | solution.py:37
  117.9 14.8 %collective-permute-done.11 = bf16[128,3200]{1,0:T(8,128)(2,1)} collective-permute-done((bf16[128,3200]{1,0:T(8,128)(2,1)}, bf16[128,3200]{1,0:T(8,128)(2,1)}, u32[]{:S(2)}, u32[]{:S(2)}) %collective-permute-start.11) | collective-permute-done | bytes 819232 | tf_op jit(solution)/shard_map/ag_mixer/ppermute | solution.py:33
  134.1 4.2 ag_mixer.2
  138.4 4.2 collective-permute-start.13
  157.3 6.7 %f1.5 = (f32[256,1024]{1,0:T(8,128)S(1)}, bf16[256,1024]{1,0:T(8,128)(2,1)S(1)}, f32[256,2048]{1,0:T(8,128)}, bf16[256,1024]{1,0:T(8,128)(2,1)}) custom-call(f32[256,1024]{1,0:T(8,128)S(1)} %bitcast_convert_fusion.refs_0_, f32[1,1024]{1,0:T(1,128)S(1)} %bitcast.452, f32[1,128]{1,0:T(1,128)S(1)} %broadcast_in_dim_reshape.4.refs_2_.refs_3_.refs_6_, ...), custom_call_target="tpu_custom_call" | custom-call | flops 1048576 | bytes 65536 | tf_op jit(solution)/shard_map/f1/pallas_call | solution.py:367
  164.0 9.0 %collective-permute-done.15.refs_3_ = bf16[4,32,4608]{2,1,0:T(8,128)(2,1)} collective-permute-done((bf16[4,32,4608]{2,1,0:T(8,128)(2,1)}, bf16[4,32,4608]{2,1,0:T(8,128)(2,1)}, u32[]{:S(2)}, u32[]{:S(2)}) %collective-permute-start.15) | collective-permute-done | bytes 1179680 | tf_op jit(solution)/shard_map/ppermute | solution.py:37
  175.0 5.7 f1.6
  183.5 15.5 %collective-permute-done.14.refs_6_.refs_7_ = bf16[1024,2176]{1,0:T(8,128)(2,1)S(1)} collective-permute-done((bf16[1024,2176]{1,0:T(8,128)(2,1)S(1)}, bf16[1024,2176]{1,0:T(8,128)(2,1)S(1)}, u32[]{:S(2)}, u32[]{:S(2)}) %collective-permute-start.14) | collective-permute-done | bytes 4456480 | tf_op jit(solution)/shard_map/ag_mixer/ppermute | solution.py:24
  199.0 6.6 %f1.7 = (f32[256,1024]{1,0:T(8,128)S(1)}, f32[256,2048]{1,0:T(8,128)}, bf16[256,1024]{1,0:T(8,128)(2,1)}) custom-call(f32[256,1024]{1,0:T(8,128)S(1)} %get-tuple-element.88.refs_5_.refs_0_, bf16[256,1024]{1,0:T(8,128)(2,1)S(1)} %get-tuple-element.89.refs_1_, f32[1,128]{1,0:T(1,128)S(1)} %broadcast_in_dim_reshape.4.refs_2_.refs_3_.refs_6_, ...), custom_call_target="tpu_custom_call" | custom-call | flops 1048576 | bytes 65536 | tf_op jit(solution)/shard_map/f1/pallas_call | solution.py:367
  206.5 4.9 f1.8
  211.4 6.7 %f1.9 = (f32[256,1024]{1,0:T(8,128)S(1)}, f32[256,3072]{1,0:T(8,128)}, bf16[256,1536]{1,0:T(8,128)(2,1)}) custom-call(f32[256,1024]{1,0:T(8,128)S(1)} %get-tuple-element.95.refs_0_, bf16[256,1024]{1,0:T(8,128)(2,1)S(1)} %get-tuple-element.96.refs_1_, bf16[1024,3072]{1,0:T(8,128)(2,1)} %collective-permute-done.18.refs_2_.refs_3_, ...), custom_call_target="tpu_custom_call" | custom-call | flops 1048576 | bytes 65536 | tf_op jit(solution)/shard_map/f1/pallas_call | solution.py:367
  221.9 10.5 %collective-permute-done.19 = bf16[256,1024]{1,0:T(8,128)(2,1)} collective-permute-done((bf16[256,1024]{1,0:T(8,128)(2,1)}, bf16[256,1024]{1,0:T(8,128)(2,1)}, u32[]{:S(2)}, u32[]{:S(2)}) %collective-permute-start.19) | collective-permute-done | bytes 524320 | tf_op jit(solution)/shard_map/ppermute | solution.py:41
  238.5 6.5 %f2.4 = (f32[256,1024]{1,0:T(8,128)S(1)}, bf16[256,1024]{1,0:T(8,128)(2,1)S(1)}, f32[256,2048]{1,0:T(8,128)S(1)}, bf16[256,1024]{1,0:T(8,128)(2,1)S(1)}) custom-call(f32[256,1024]{1,0:T(8,128)S(1)} %get-tuple-element.211.refs_0_, f32[1,1024]{1,0:T(1,128)S(1)} %bitcast.453, f32[1,128]{1,0:T(1,128)S(1)} %broadcast_in_dim_reshape.4.refs_2_.refs_3_.refs_6_, ...), custom_call_target="tpu_custom_call" | custom-call | flops 1048576 | bytes 65536 | tf_op jit(solution)/shard_map/f2/pallas_call | solution.py:367
  250.3 6.3 %f2.5 = (f32[256,1024]{1,0:T(8,128)S(1)}, f32[256,2048]{1,0:T(8,128)S(1)}, bf16[256,1024]{1,0:T(8,128)(2,1)S(1)}) custom-call(f32[256,1024]{1,0:T(8,128)S(1)} %get-tuple-element.98.refs_0_, bf16[256,1024]{1,0:T(8,128)(2,1)S(1)} %get-tuple-element.99.refs_1_, f32[1,128]{1,0:T(1,128)S(1)} %broadcast_in_dim_reshape.4.refs_2_.refs_3_.refs_6_, ...), custom_call_target="tpu_custom_call" | custom-call | flops 1048576 | bytes 65536 | tf_op jit(solution)/shard_map/f2/pallas_call | solution.py:367
  258.1 4.2 f2.6
  265.5 5.6 f2.7
  277.2 6.0 %b1.4 = (bf16[256,3072]{1,0:T(8,128)(2,1)}, f32[256,1024]{1,0:T(8,128)S(1)}) custom-call(bf16[256,1024]{1,0:T(8,128)(2,1)S(1)} %bitcast.448, bf16[3072,1024]{1,0:T(8,128)(2,1)S(1)} %bitcast.439, f32[256,3072]{1,0:T(8,128)S(1)} %copy-done.22, bf16[1024,3072]{1,0:T(8,128)(2,1)} %collective-permute-done.18.refs_2_.refs_3_), custom_call_target="tpu_custom_call" | custom-call | flops 1048576 | bytes 65536 | tf_op jit(solution)/shard_map/b1/pallas_call | solution.py:367
  283.2 5.0 b1.5
  292.7 10.5 %b1.6 = (bf16[256,2048]{1,0:T(8,128)(2,1)}, f32[256,1024]{1,0:T(8,128)S(1)}, f32[1,128]{1,0:T(1,128)S(1)}, f32[1,128]{1,0:T(1,128)S(1)}) custom-call(bf16[256,1024]{1,0:T(8,128)(2,1)S(1)} %fusion.68.refs_0_.refs_3_, bf16[2048,1024]{1,0:T(8,128)(2,1)S(1)} %copy-done.3, f32[256,2048]{1,0:T(8,128)S(1)} %copy-done.30, ...), custom_call_target="tpu_custom_call" | custom-call | flops 1048576 | bytes 65536 | tf_op jit(solution)/shard_map/b1/pallas_call | solution.py:367
  303.3 10.5 %b1.7 = (bf16[256,2048]{1,0:T(8,128)(2,1)}, f32[256,1024]{1,0:T(8,128)S(1)}, f32[1,128]{1,0:T(1,128)}, f32[1,128]{1,0:T(1,128)}) custom-call(f32[256,1024]{1,0:T(8,128)S(1)} %get-tuple-element.108.refs_0_, f32[1,128]{1,0:T(1,128)S(1)} %get-tuple-element.109.refs_1_, f32[1,128]{1,0:T(1,128)S(1)} %get-tuple-element.110.refs_2_, ...), custom_call_target="tpu_custom_call" | custom-call | flops 1048576 | bytes 65536 | tf_op jit(solution)/shard_map/b1/pallas_call | solution.py:367
  317.0 14.1 %collective-permute-done.20 = bf16[256,1024]{1,0:T(8,128)(2,1)S(1)} collective-permute-done((bf16[256,1024]{1,0:T(8,128)(2,1)S(1)}, bf16[256,1024]{1,0:T(8,128)(2,1)S(1)}, u32[]{:S(2)}, u32[]{:S(2)}) %collective-permute-start.20) | collective-permute-done | bytes 524320 | tf_op jit(solution)/shard_map/ppermute | solution.py:41
  331.4 6.3 %b2.4 = (bf16[256,3072]{1,0:T(8,128)(2,1)S(1)}, f32[256,1024]{1,0:T(8,128)S(1)}) custom-call(bf16[256,1024]{1,0:T(8,128)(2,1)S(1)} %get-tuple-element.208.refs_0_.refs_1_, bf16[3072,1024]{1,0:T(8,128)(2,1)S(1)} %bitcast.439, f32[256,3072]{1,0:T(8,128)S(1)} %copy-done.23, bf16[1024,3072]{1,0:T(8,128)(2,1)} %collective-permute-done.18.refs_2_.refs_3_), custom_call_target="tpu_custom_call" | custom-call | flops 1048576 | bytes 65536 | tf_op jit(solution)/shard_map/b2/pallas_call | solution.py:367
  339.1 4.4 b2.5
  347.8 5.6 convolution_convert_fusion
  360.5 3.3 constant_dynamic-slice_fusion.4
  375.3 8.7 %collective-permute-done.25 = bf16[4,128,768]{2,1,0:T(8,128)(2,1)} collective-permute-done((bf16[4,128,768]{2,1,0:T(8,128)(2,1)}, bf16[4,128,768]{2,1,0:T(8,128)(2,1)}, u32[]{:S(2)}, u32[]{:S(2)}) %collective-permute-start.25) | collective-permute-done | bytes 786464 | tf_op jit(solution)/shard_map/b2/g_gu/ppermute | solution.py:37
  384.0 3.1 collective-permute-done.24
  394.8 10.5 %b2.6 = (bf16[256,2048]{1,0:T(8,128)(2,1)}, f32[256,1024]{1,0:T(8,128)S(1)}, f32[1,128]{1,0:T(1,128)S(1)}, f32[1,128]{1,0:T(1,128)S(1)}) custom-call(bf16[256,1024]{1,0:T(8,128)(2,1)S(1)} %get-tuple-element.133.refs_0_.refs_3_, bf16[2048,1024]{1,0:T(8,128)(2,1)S(1)} %copy-done.4, f32[256,2048]{1,0:T(8,128)S(1)} %copy-done.31, ...), custom_call_target="tpu_custom_call" | custom-call | flops 1048576 | bytes 65536 | tf_op jit(solution)/shard_map/b2/pallas_call | solution.py:367
  420.4 10.0 %b2.7 = (bf16[256,2048]{1,0:T(8,128)(2,1)S(1)}, f32[256,1024]{1,0:T(8,128)S(1)}, f32[1,128]{1,0:T(1,128)S(1)}, f32[1,128]{1,0:T(1,128)S(1)}) custom-call(f32[256,1024]{1,0:T(8,128)S(1)} %copy-done.43, f32[1,128]{1,0:T(1,128)S(1)} %get-tuple-element.127.refs_1_, f32[1,128]{1,0:T(1,128)S(1)} %get-tuple-element.128.refs_2_, ...), custom_call_target="tpu_custom_call" | custom-call | flops 1048576 | bytes 65536 | tf_op jit(solution)/shard_map/b2/pallas_call | solution.py:367
  430.4 9.9 %collective-permute-done.31 = bf16[2,640,512]{2,1,0:T(8,128)(2,1)} collective-permute-done((bf16[2,640,512]{2,1,0:T(8,128)(2,1)}, bf16[2,640,512]{2,1,0:T(8,128)(2,1)}, u32[]{:S(2)}, u32[]{:S(2)}) %collective-permute-start.31) | collective-permute-done | bytes 1310752 | tf_op jit(solution)/shard_map/b2/rs_do/ppermute | solution.py:33
  443.5 3.6 convolution_convert_fusion.1
  450.6 13.8 %collective-permute-done.40 = bf16[128,2816]{1,0:T(8,128)(2,1)S(1)} collective-permute-done((bf16[128,2816]{1,0:T(8,128)(2,1)S(1)}, bf16[128,2816]{1,0:T(8,128)(2,1)S(1)}, u32[]{:S(2)}, u32[]{:S(2)}) %collective-permute-start.40) | collective-permute-done | bytes 720928 | tf_op jit(solution)/shard_map/b2/rs_qg/ppermute | solution.py:33
  470.3 3.9 collective-permute-start.34
  476.8 3.3 collective-permute-start.45
  480.1 16.0 %collective-permute-done.43 = bf16[2,128,2816]{2,1,0:T(8,128)(2,1)} collective-permute-done((bf16[2,128,2816]{2,1,0:T(8,128)(2,1)}, bf16[2,128,2816]{2,1,0:T(8,128)(2,1)}, u32[]{:S(2)}, u32[]{:S(2)}) %collective-permute-start.43) | collective-permute-done | bytes 1441824 | tf_op jit(solution)/shard_map/rs_qg/ppermute | solution.py:33
  496.1 4.5 collective-permute-done.41
  503.3 3.3 collective-permute-start.44
  509.3 4.4 collective-permute-done.36
  539.1 7.8 %collective-permute-done.50 = bf16[480,512]{1,0:T(8,128)(2,1)S(1)} collective-permute-done((bf16[480,512]{1,0:T(8,128)(2,1)S(1)}, bf16[480,512]{1,0:T(8,128)(2,1)S(1)}, u32[]{:S(2)}, u32[]{:S(2)}) %collective-permute-start.50) | collective-permute-done | bytes 491552 | tf_op jit(solution)/shard_map/fin/ppermute | solution.py:37
  546.9 3.2 collective-permute-start.53
  550.3 5.6 collective-permute-done.53
  555.8 3.6 collective-permute-done.52
  565.2 10.4 %collective-permute-start.54 = (bf16[960,512]{1,0:T(8,128)(2,1)S(1)}, bf16[960,512]{1,0:T(8,128)(2,1)S(1)}, u32[]{:S(2)}, u32[]{:S(2)}) collective-permute-start(bf16[960,512]{1,0:T(8,128)(2,1)S(1)} %constant_dynamic-update-slice_fusion.78), channel_id=1, source_target_pairs={{0,1},{1,0},{2,3},{3,2},{4,5},{5,4},{6,7},{7,6},{8,9},{9,8},{10,11... | collective-permute-start | bytes 2949128 | tf_op jit(solution)/shard_map/fin/ppermute | solution.py:24
  (481 shorter events, 201.1 us)
Async XLA Ops:
  23.3 10.8 %collective-permute-start.1 = (bf16[32,4608]{1,0:T(8,128)(2,1)S(1)}, bf16[32,4608]{1,0:T(8,128)(2,1)S(1)}, u32[]{:S(2)}, u32[]{:S(2)}) collective-permute-start(bf16[32,4608]{1,0:T(8,128)(2,1)S(1)} %get-tuple-element.213), channel_id=1, source_target_pairs={{0,8},{1,9},{2,10},{3,11},{4,12},{5,13},{6,14},{7,15},{8,0},{9,1},... | collective-permute-start | bytes 884744 | tf_op jit(solution)/shard_map/ag_dense/ppermute | solution.py:28
  27.1 24.6 %collective-permute-start.4 = (bf16[128,3200]{1,0:T(8,128)(2,1)S(1)}, bf16[128,3200]{1,0:T(8,128)(2,1)S(1)}, u32[]{:S(2)}, u32[]{:S(2)}) collective-permute-start(bf16[128,3200]{1,0:T(8,128)(2,1)S(1)} %fusion.32), channel_id=1, source_target_pairs={{0,8},{1,9},{2,10},{3,11},{4,12},{5,13},{6,14},{7,15},{8,0},{9,1},... | collective-permute-start | bytes 2457608 | tf_op jit(solution)/shard_map/ag_dense/ppermute | solution.py:28
  34.2 17.5 %collective-permute-start.2 = (bf16[2,32,4608]{2,1,0:T(8,128)(2,1)S(1)}, bf16[2,32,4608]{2,1,0:T(8,128)(2,1)S(1)}, u32[]{:S(2)}, u32[]{:S(2)}) collective-permute-start(bf16[2,32,4608]{2,1,0:T(8,128)(2,1)S(1)} %pad_maximum_fusion.11), channel_id=1, source_target_pairs={{0,2},{1,3},{2,4},{3,5},{4,6},{5,7},{6,0},{7,1},{8,10},{9,11},{10,... | collective-permute-start | bytes 1769480 | tf_op jit(solution)/shard_map/ag_dense/ppermute | solution.py:33
  35.5 16.1 %collective-permute-start.3 = (bf16[2,32,4608]{2,1,0:T(8,128)(2,1)S(1)}, bf16[2,32,4608]{2,1,0:T(8,128)(2,1)S(1)}, u32[]{:S(2)}, u32[]{:S(2)}) collective-permute-start(bf16[2,32,4608]{2,1,0:T(8,128)(2,1)S(1)} %pad_maximum_fusion.11), channel_id=1, source_target_pairs={{0,6},{1,7},{2,0},{3,1},{4,2},{5,3},{6,4},{7,5},{8,14},{9,15},{10,... | collective-permute-start | bytes 1769480 | tf_op jit(solution)/shard_map/ag_dense/ppermute | solution.py:33
  51.7 9.0 %collective-permute-start.7 = (bf16[32,4608]{1,0:T(8,128)(2,1)S(1)}, bf16[32,4608]{1,0:T(8,128)(2,1)S(1)}, u32[]{:S(2)}, u32[]{:S(2)}) collective-permute-start(bf16[32,4608]{1,0:T(8,128)(2,1)S(1)} %slice_bitcast_fusion.7), channel_id=1, source_target_pairs={{0,2},{1,3},{2,4},{3,5},{4,6},{5,7},{6,0},{7,1},{8,10},{9,11},{10,... | collective-permute-start | bytes 884744 | tf_op jit(solution)/shard_map/ag_dense/ppermute | solution.py:33
  53.1 7.7 %collective-permute-start.8 = (bf16[32,4608]{1,0:T(8,128)(2,1)S(1)}, bf16[32,4608]{1,0:T(8,128)(2,1)S(1)}, u32[]{:S(2)}, u32[]{:S(2)}) collective-permute-start(bf16[32,4608]{1,0:T(8,128)(2,1)S(1)} %slice_bitcast_fusion.6), channel_id=1, source_target_pairs={{0,6},{1,7},{2,0},{3,1},{4,2},{5,3},{6,4},{7,5},{8,14},{9,15},{10,... | collective-permute-start | bytes 884744 | tf_op jit(solution)/shard_map/ag_dense/ppermute | solution.py:33
  60.9 52.3 %collective-permute-start.9 = (bf16[8,32,4608]{2,1,0:T(8,128)(2,1)S(1)}, bf16[8,32,4608]{2,1,0:T(8,128)(2,1)}, u32[]{:S(2)}, u32[]{:S(2)}) collective-permute-start(bf16[8,32,4608]{2,1,0:T(8,128)(2,1)S(1)} %bitcast_dynamic-update-slice_fusion.6.refs_0_), channel_id=1, source_target_pairs={{0,16},{16,32},{32,48},{48,0},{1,17},{17,33},{33,49},{49,1},{2,18}... | collective-permute-start | bytes 7077896 | tf_op jit(solution)/shard_map/ag_dense/ppermute | solution.py:37
  62.1 51.1 %collective-permute-start.10 = (bf16[8,32,4608]{2,1,0:T(8,128)(2,1)S(1)}, bf16[8,32,4608]{2,1,0:T(8,128)(2,1)}, u32[]{:S(2)}, u32[]{:S(2)}) collective-permute-start(bf16[8,32,4608]{2,1,0:T(8,128)(2,1)S(1)} %bitcast_dynamic-update-slice_fusion.6.refs_0_), channel_id=1, source_target_pairs={{0,48},{16,0},{32,16},{48,32},{1,49},{17,1},{33,17},{49,33},{2,50}... | collective-permute-start | bytes 7077896 | tf_op jit(solution)/shard_map/ag_dense/ppermute | solution.py:37
  63.8 36.3 %collective-permute-start.5 = (bf16[2,128,3200]{2,1,0:T(8,128)(2,1)S(1)}, bf16[2,128,3200]{2,1,0:T(8,128)(2,1)S(1)}, u32[]{:S(2)}, u32[]{:S(2)}) collective-permute-start(bf16[2,128,3200]{2,1,0:T(8,128)(2,1)S(1)} %pad_maximum_fusion.4.refs_0_), channel_id=1, source_target_pairs={{0,2},{1,3},{2,4},{3,5},{4,6},{5,7},{6,0},{7,1},{8,10},{9,11},{10,... | collective-permute-start | bytes 4915208 | tf_op jit(solution)/shard_map/ag_mixer/ppermute | solution.py:33
  64.9 35.3 %collective-permute-start.6 = (bf16[2,128,3200]{2,1,0:T(8,128)(2,1)S(1)}, bf16[2,128,3200]{2,1,0:T(8,128)(2,1)S(1)}, u32[]{:S(2)}, u32[]{:S(2)}) collective-permute-start(bf16[2,128,3200]{2,1,0:T(8,128)(2,1)S(1)} %pad_maximum_fusion.4.refs_0_), channel_id=1, source_target_pairs={{0,6},{1,7},{2,0},{3,1},{4,2},{5,3},{6,4},{7,5},{8,14},{9,15},{10,... | collective-permute-start | bytes 4915208 | tf_op jit(solution)/shard_map/ag_mixer/ppermute | solution.py:33
  114.2 18.5 %collective-permute-start.11 = (bf16[128,3200]{1,0:T(8,128)(2,1)}, bf16[128,3200]{1,0:T(8,128)(2,1)}, u32[]{:S(2)}, u32[]{:S(2)}) collective-permute-start(bf16[128,3200]{1,0:T(8,128)(2,1)} %slice_bitcast_fusion.1), channel_id=1, source_target_pairs={{0,2},{1,3},{2,4},{3,5},{4,6},{5,7},{6,0},{7,1},{8,10},{9,11},{10,... | collective-permute-start | bytes 2457608 | tf_op jit(solution)/shard_map/ag_mixer/ppermute | solution.py:33
  115.8 16.9 %collective-permute-start.12 = (bf16[128,3200]{1,0:T(8,128)(2,1)}, bf16[128,3200]{1,0:T(8,128)(2,1)}, u32[]{:S(2)}, u32[]{:S(2)}) collective-permute-start(bf16[128,3200]{1,0:T(8,128)(2,1)} %slice_bitcast_fusion), channel_id=1, source_target_pairs={{0,6},{1,7},{2,0},{3,1},{4,2},{5,3},{6,4},{7,5},{8,14},{9,15},{10,... | collective-permute-start | bytes 2457608 | tf_op jit(solution)/shard_map/ag_mixer/ppermute | solution.py:33
  138.4 14.9 %collective-permute-start.13 = (bf16[2048,512]{1,0:T(8,128)(2,1)}, bf16[2048,512]{1,0:T(8,128)(2,1)}, u32[]{:S(2)}, u32[]{:S(2)}) collective-permute-start(bf16[2048,512]{1,0:T(8,128)(2,1)} %get-tuple-element.87.own), channel_id=1, source_target_pairs={{0,1},{1,0},{2,3},{3,2},{4,5},{5,4},{6,7},{7,6},{8,9},{9,8},{10,11... | collective-permute-start | bytes 6291464 | tf_op jit(solution)/shard_map/ag_mixer/ppermute | solution.py:24
  144.9 28.1 %collective-permute-start.15 = (bf16[4,32,4608]{2,1,0:T(8,128)(2,1)}, bf16[4,32,4608]{2,1,0:T(8,128)(2,1)}, u32[]{:S(2)}, u32[]{:S(2)}) collective-permute-start(bf16[4,32,4608]{2,1,0:T(8,128)(2,1)} %slice.678), channel_id=1, source_target_pairs={{0,16},{16,32},{32,48},{48,0},{1,17},{17,33},{33,49},{49,1},{2,18}... | collective-permute-start | bytes 3538952 | tf_op jit(solution)/shard_map/ppermute | solution.py:37
  148.2 26.8 %collective-permute-start.16 = (bf16[4,32,4608]{2,1,0:T(8,128)(2,1)}, bf16[4,32,4608]{2,1,0:T(8,128)(2,1)}, u32[]{:S(2)}, u32[]{:S(2)}) collective-permute-start(bf16[4,32,4608]{2,1,0:T(8,128)(2,1)} %slice.679), channel_id=1, source_target_pairs={{0,48},{16,0},{32,16},{48,32},{1,49},{17,1},{33,17},{49,33},{2,50}... | collective-permute-start | bytes 3538952 | tf_op jit(solution)/shard_map/ppermute | solution.py:37
  180.8 30.7 %collective-permute-start.18 = (bf16[1024,3072]{1,0:T(8,128)(2,1)S(1)}, bf16[1024,3072]{1,0:T(8,128)(2,1)}, u32[]{:S(2)}, u32[]{:S(2)}) collective-permute-start(bf16[1024,3072]{1,0:T(8,128)(2,1)S(1)} %get-tuple-element.92.refs_8_.refs_2_.refs_4_), channel_id=1, source_target_pairs={{0,1},{1,0},{2,3},{3,2},{4,5},{5,4},{6,7},{7,6},{8,9},{9,8},{10,11... | collective-permute-start | bytes 18874376 | tf_op jit(solution)/shard_map/ag_dense/ppermute | solution.py:24
  183.0 16.0 %collective-permute-start.14 = (bf16[1024,2176]{1,0:T(8,128)(2,1)S(1)}, bf16[1024,2176]{1,0:T(8,128)(2,1)S(1)}, u32[]{:S(2)}, u32[]{:S(2)}) collective-permute-start(bf16[1024,2176]{1,0:T(8,128)(2,1)S(1)} %bitcast.443), channel_id=1, source_target_pairs={{0,1},{1,0},{2,3},{3,2},{4,5},{5,4},{6,7},{7,6},{8,9},{9,8},{10,11... | collective-permute-start | bytes 13369352 | tf_op jit(solution)/shard_map/ag_mixer/ppermute | solution.py:24
  183.1 22.5 %collective-permute-start.17 = (bf16[3072,512]{1,0:T(8,128)(2,1)S(1)}, bf16[3072,512]{1,0:T(8,128)(2,1)S(1)}, u32[]{:S(2)}, u32[]{:S(2)}) collective-permute-start(bf16[3072,512]{1,0:T(8,128)(2,1)S(1)} %get-tuple-element.94.own), channel_id=1, source_target_pairs={{0,1},{1,0},{2,3},{3,2},{4,5},{5,4},{6,7},{7,6},{8,9},{9,8},{10,11... | collective-permute-start | bytes 9437192 | tf_op jit(solution)/shard_map/ag_dense/ppermute | solution.py:24
  219.0 13.4 %collective-permute-start.19 = (bf16[256,1024]{1,0:T(8,128)(2,1)}, bf16[256,1024]{1,0:T(8,128)(2,1)}, u32[]{:S(2)}, u32[]{:S(2)}) collective-permute-start(bf16[256,1024]{1,0:T(8,128)(2,1)} %convert_element_type.303), channel_id=1, source_target_pairs={{0,64},{1,65},{2,66},{3,67},{4,68},{5,69},{6,70},{7,71},{8,72},{9,... | collective-permute-start | bytes 1572872 | tf_op jit(solution)/shard_map/ppermute | solution.py:41
  275.8 67.8 %collective-permute-start.21 = (bf16[256,7168]{1,0:T(8,128)(2,1)}, bf16[256,7168]{1,0:T(8,128)(2,1)}, u32[]{:S(2)}, u32[]{:S(2)}) collective-permute-start(bf16[256,7168]{1,0:T(8,128)(2,1)} %constant_dynamic-update-slice_fusion.52), channel_id=1, source_target_pairs={{0,1},{1,0},{2,3},{3,2},{4,5},{5,4},{6,7},{7,6},{8,9},{9,8},{10,11... | collective-permute-start | bytes 11010056 | tf_op jit(solution)/shard_map/ppermute | solution.py:24
  315.6 15.5 %collective-permute-start.20 = (bf16[256,1024]{1,0:T(8,128)(2,1)S(1)}, bf16[256,1024]{1,0:T(8,128)(2,1)S(1)}, u32[]{:S(2)}, u32[]{:S(2)}) collective-permute-start(bf16[256,1024]{1,0:T(8,128)(2,1)S(1)} %add_convert_fusion.5), channel_id=1, source_target_pairs={{64,0},{65,1},{66,2},{67,3},{68,4},{69,5},{70,6},{71,7},{72,8},{73... | collective-permute-start | bytes 1572872 | tf_op jit(solution)/shard_map/ppermute | solution.py:41
  337.7 10.1 %collective-permute-start.22 = (bf16[256,3072]{1,0:T(8,128)(2,1)S(1)}, bf16[256,3072]{1,0:T(8,128)(2,1)S(1)}, u32[]{:S(2)}, u32[]{:S(2)}) collective-permute-start(bf16[256,3072]{1,0:T(8,128)(2,1)S(1)} %get-tuple-element.120), channel_id=1, source_target_pairs={{0,1},{1,0},{2,3},{3,2},{4,5},{5,4},{6,7},{7,6},{8,9},{9,8},{10,11... | collective-permute-start | bytes 4718600 | tf_op jit(solution)/shard_map/b2/g_gu/ppermute | solution.py:24
  338.8 14.6 %collective-permute-start.23 = (bf16[256,512]{1,0:T(8,128)(2,1)S(1)}, bf16[256,512]{1,0:T(8,128)(2,1)S(1)}, u32[]{:S(2)}, u32[]{:S(2)}) collective-permute-start(bf16[256,512]{1,0:T(8,128)(2,1)S(1)} %get-tuple-element.256), channel_id=1, source_target_pairs={{0,1},{1,0},{2,3},{3,2},{4,5},{5,4},{6,7},{7,6},{8,9},{9,8},{10,11... | collective-permute-start | bytes 786440 | tf_op jit(solution)/shard_map/b2/g_down/ppermute | solution.py:24
  363.8 20.2 %collective-permute-start.25 = (bf16[4,128,768]{2,1,0:T(8,128)(2,1)}, bf16[4,128,768]{2,1,0:T(8,128)(2,1)}, u32[]{:S(2)}, u32[]{:S(2)}) collective-permute-start(bf16[4,128,768]{2,1,0:T(8,128)(2,1)} %get-tuple-element.216), channel_id=1, source_target_pairs={{0,48},{16,0},{32,16},{48,32},{1,49},{17,1},{33,17},{49,33},{2,50}... | collective-permute-start | bytes 2359304 | tf_op jit(solution)/shard_map/b2/g_gu/ppermute | solution.py:37
  366.8 20.3 %collective-permute-start.24 = (bf16[4,128,768]{2,1,0:T(8,128)(2,1)}, bf16[4,128,768]{2,1,0:T(8,128)(2,1)}, u32[]{:S(2)}, u32[]{:S(2)}) collective-permute-start(bf16[4,128,768]{2,1,0:T(8,128)(2,1)} %get-tuple-element.215), channel_id=1, source_target_pairs={{0,16},{16,32},{32,48},{48,0},{1,17},{17,33},{33,49},{49,1},{2,18}... | collective-permute-start | bytes 2359304 | tf_op jit(solution)/shard_map/b2/g_gu/ppermute | solution.py:37
  371.8 33.6 %collective-permute-start.27 = (bf16[640,512]{1,0:T(8,128)(2,1)}, bf16[640,512]{1,0:T(8,128)(2,1)S(1)}, u32[]{:S(2)}, u32[]{:S(2)}) collective-permute-start(bf16[640,512]{1,0:T(8,128)(2,1)} %get-tuple-element.231), channel_id=1, source_target_pairs={{0,2},{1,3},{2,4},{3,5},{4,6},{5,7},{6,0},{7,1},{8,10},{9,11},{10,... | collective-permute-start | bytes 1966088 | tf_op jit(solution)/shard_map/b2/rs_do/ppermute | solution.py:33
  372.8 32.6 %collective-permute-start.28 = (bf16[640,512]{1,0:T(8,128)(2,1)}, bf16[640,512]{1,0:T(8,128)(2,1)}, u32[]{:S(2)}, u32[]{:S(2)}) collective-permute-start(bf16[640,512]{1,0:T(8,128)(2,1)} %get-tuple-element.230), channel_id=1, source_target_pairs={{0,6},{1,7},{2,0},{3,1},{4,2},{5,3},{6,4},{7,5},{8,14},{9,15},{10,... | collective-permute-start | bytes 1966088 | tf_op jit(solution)/shard_map/b2/rs_do/ppermute | solution.py:33
  391.9 48.5 %collective-permute-start.29 = (bf16[8,128,768]{2,1,0:T(8,128)(2,1)}, bf16[8,128,768]{2,1,0:T(8,128)(2,1)}, u32[]{:S(2)}, u32[]{:S(2)}) collective-permute-start(bf16[8,128,768]{2,1,0:T(8,128)(2,1)} %pad_maximum_fusion.5), channel_id=1, source_target_pairs={{0,16},{16,32},{32,48},{48,0},{1,17},{17,33},{33,49},{49,1},{2,18}... | collective-permute-start | bytes 4718600 | tf_op jit(solution)/shard_map/b2/rs_gu/ppermute | solution.py:37
  391.9 48.5 %collective-permute-start.30 = (bf16[8,128,768]{2,1,0:T(8,128)(2,1)}, bf16[8,128,768]{2,1,0:T(8,128)(2,1)}, u32[]{:S(2)}, u32[]{:S(2)}) collective-permute-start(bf16[8,128,768]{2,1,0:T(8,128)(2,1)} %pad_maximum_fusion.6), channel_id=1, source_target_pairs={{0,48},{16,0},{32,16},{48,32},{1,49},{17,1},{33,17},{49,33},{2,50}... | collective-permute-start | bytes 4718600 | tf_op jit(solution)/shard_map/b2/rs_gu/ppermute | solution.py:37
  409.6 30.8 %collective-permute-start.31 = (bf16[2,640,512]{2,1,0:T(8,128)(2,1)}, bf16[2,640,512]{2,1,0:T(8,128)(2,1)}, u32[]{:S(2)}, u32[]{:S(2)}) collective-permute-start(bf16[2,640,512]{2,1,0:T(8,128)(2,1)} %pad_maximum_fusion.9), channel_id=1, source_target_pairs={{0,2},{1,3},{2,4},{3,5},{4,6},{5,7},{6,0},{7,1},{8,10},{9,11},{10,... | collective-permute-start | bytes 3932168 | tf_op jit(solution)/shard_map/b2/rs_do/ppermute | solution.py:33
  410.6 29.8 %collective-permute-start.32 = (bf16[2,640,512]{2,1,0:T(8,128)(2,1)}, bf16[2,640,512]{2,1,0:T(8,128)(2,1)}, u32[]{:S(2)}, u32[]{:S(2)}) collective-permute-start(bf16[2,640,512]{2,1,0:T(8,128)(2,1)} %pad_maximum_fusion.10), channel_id=1, source_target_pairs={{0,6},{1,7},{2,0},{3,1},{4,2},{5,3},{6,4},{7,5},{8,14},{9,15},{10,... | collective-permute-start | bytes 3932168 | tf_op jit(solution)/shard_map/b2/rs_do/ppermute | solution.py:33
  412.7 30.8 %collective-permute-start.33 = (bf16[256,2048]{1,0:T(8,128)(2,1)}, bf16[256,2048]{1,0:T(8,128)(2,1)}, u32[]{:S(2)}, u32[]{:S(2)}) collective-permute-start(bf16[256,2048]{1,0:T(8,128)(2,1)} %get-tuple-element.130), channel_id=1, source_target_pairs={{0,1},{1,0},{2,3},{3,2},{4,5},{5,4},{6,7},{7,6},{8,9},{9,8},{10,11... | collective-permute-start | bytes 3145736 | tf_op jit(solution)/shard_map/b2/g_qkv/ppermute | solution.py:24
  447.8 16.5 %collective-permute-start.40 = (bf16[128,2816]{1,0:T(8,128)(2,1)S(1)}, bf16[128,2816]{1,0:T(8,128)(2,1)S(1)}, u32[]{:S(2)}, u32[]{:S(2)}) collective-permute-start(bf16[128,2816]{1,0:T(8,128)(2,1)S(1)} %get-tuple-element.222), channel_id=1, source_target_pairs={{0,2},{1,3},{2,4},{3,5},{4,6},{5,7},{6,0},{7,1},{8,10},{9,11},{10,... | collective-permute-start | bytes 2162696 | tf_op jit(solution)/shard_map/b2/rs_qg/ppermute | solution.py:33
  448.3 16.1 %collective-permute-start.42 = (bf16[128,2816]{1,0:T(8,128)(2,1)S(1)}, bf16[128,2816]{1,0:T(8,128)(2,1)S(1)}, u32[]{:S(2)}, u32[]{:S(2)}) collective-permute-start(bf16[128,2816]{1,0:T(8,128)(2,1)S(1)} %get-tuple-element.223), channel_id=1, source_target_pairs={{0,6},{1,7},{2,0},{3,1},{4,2},{5,3},{6,4},{7,5},{8,14},{9,15},{10,... | collective-permute-start | bytes 2162696 | tf_op jit(solution)/shard_map/b2/rs_qg/ppermute | solution.py:33
  466.0 30.1 %collective-permute-start.43 = (bf16[2,128,2816]{2,1,0:T(8,128)(2,1)}, bf16[2,128,2816]{2,1,0:T(8,128)(2,1)}, u32[]{:S(2)}, u32[]{:S(2)}) collective-permute-start(bf16[2,128,2816]{2,1,0:T(8,128)(2,1)} %pad_maximum_fusion.8), channel_id=1, source_target_pairs={{0,6},{1,7},{2,0},{3,1},{4,2},{5,3},{6,4},{7,5},{8,14},{9,15},{10,... | collective-permute-start | bytes 4325384 | tf_op jit(solution)/shard_map/rs_qg/ppermute | solution.py:33
  469.6 31.0 %collective-permute-start.41 = (bf16[2,128,2816]{2,1,0:T(8,128)(2,1)}, bf16[2,128,2816]{2,1,0:T(8,128)(2,1)}, u32[]{:S(2)}, u32[]{:S(2)}) collective-permute-start(bf16[2,128,2816]{2,1,0:T(8,128)(2,1)} %pad_maximum_fusion.7), channel_id=1, source_target_pairs={{0,2},{1,3},{2,4},{3,5},{4,6},{5,7},{6,0},{7,1},{8,10},{9,11},{10,... | collective-permute-start | bytes 4325384 | tf_op jit(solution)/shard_map/rs_qg/ppermute | solution.py:33
  470.3 36.3 %collective-permute-start.34 = (f32[18,128]{1,0:T(8,128)S(1)}, f32[18,128]{1,0:T(8,128)S(1)}, u32[]{:S(2)}, u32[]{:S(2)}) collective-permute-start(f32[18,128]{1,0:T(8,128)S(1)} %maximum_bitcast_fusion.8), channel_id=1, source_target_pairs={{0,1},{1,0},{2,3},{3,2},{4,5},{5,4},{6,7},{7,6},{8,9},{9,8},{10,11... | collective-permute-start | bytes 27656 | tf_op jit(solution)/shard_map/ppermute | solution.py:46
  476.8 36.9 %collective-permute-start.45 = (bf16[640,512]{1,0:T(8,128)(2,1)}, bf16[640,512]{1,0:T(8,128)(2,1)}, u32[]{:S(2)}, u32[]{:S(2)}) collective-permute-start(bf16[640,512]{1,0:T(8,128)(2,1)} %fusion.16), channel_id=1, source_target_pairs={{0,8},{1,9},{2,10},{3,11},{4,12},{5,13},{6,14},{7,15},{8,0},{9,1},... | collective-permute-start | bytes 1966088 | tf_op jit(solution)/shard_map/b2/rs_do/ppermute | solution.py:28
  503.3 15.3 %collective-permute-start.44 = (bf16[128,2816]{1,0:T(8,128)(2,1)}, bf16[128,2816]{1,0:T(8,128)(2,1)}, u32[]{:S(2)}, u32[]{:S(2)}) collective-permute-start(bf16[128,2816]{1,0:T(8,128)(2,1)} %fusion.12), channel_id=1, source_target_pairs={{0,8},{1,9},{2,10},{3,11},{4,12},{5,13},{6,14},{7,15},{8,0},{9,1},... | collective-permute-start | bytes 2162696 | tf_op jit(solution)/shard_map/rs_qg/ppermute | solution.py:28
  513.7 9.9 %collective-permute-start.37 = (f32[18,128]{1,0:T(8,128)S(1)}, f32[18,128]{1,0:T(8,128)S(1)}, u32[]{:S(2)}, u32[]{:S(2)}) collective-permute-start(f32[18,128]{1,0:T(8,128)S(1)} %add.1474), channel_id=1, source_target_pairs={{0,8},{1,9},{2,10},{3,11},{4,12},{5,13},{6,14},{7,15},{8,0},{9,1},... | collective-permute-start | bytes 27656 | tf_op jit(solution)/shard_map/ppermute | solution.py:46
  526.3 8.1 %collective-permute-start.49 = (bf16[288,512]{1,0:T(8,128)(2,1)S(1)}, bf16[288,512]{1,0:T(8,128)(2,1)S(1)}, u32[]{:S(2)}, u32[]{:S(2)}) collective-permute-start(bf16[288,512]{1,0:T(8,128)(2,1)S(1)} %pad_maximum_fusion.24), channel_id=1, source_target_pairs={{0,48},{16,0},{32,16},{48,32},{1,49},{17,1},{33,17},{49,33},{2,50}... | collective-permute-start | bytes 884744 | tf_op jit(solution)/shard_map/rs_x/ppermute | solution.py:37
  529.1 7.0 %collective-permute-start.47 = (bf16[288,512]{1,0:T(8,128)(2,1)S(1)}, bf16[288,512]{1,0:T(8,128)(2,1)S(1)}, u32[]{:S(2)}, u32[]{:S(2)}) collective-permute-start(bf16[288,512]{1,0:T(8,128)(2,1)S(1)} %pad_maximum_fusion.23), channel_id=1, source_target_pairs={{0,16},{16,32},{32,48},{48,0},{1,17},{17,33},{33,49},{49,1},{2,18}... | collective-permute-start | bytes 884744 | tf_op jit(solution)/shard_map/rs_x/ppermute | solution.py:37
  530.5 7.4 %collective-permute-start.39 = (f32[18,128]{1,0:T(8,128)S(1)}, f32[18,128]{1,0:T(8,128)S(1)}, u32[]{:S(2)}, u32[]{:S(2)}) collective-permute-start(f32[18,128]{1,0:T(8,128)S(1)} %add.1476), channel_id=1, source_target_pairs={{0,32},{16,48},{32,0},{48,16},{1,33},{17,49},{33,1},{49,17},{2,34}... | collective-permute-start | bytes 27656 | tf_op jit(solution)/shard_map/ppermute | solution.py:48
  536.3 10.6 %collective-permute-start.50 = (bf16[480,512]{1,0:T(8,128)(2,1)S(1)}, bf16[480,512]{1,0:T(8,128)(2,1)S(1)}, u32[]{:S(2)}, u32[]{:S(2)}) collective-permute-start(bf16[480,512]{1,0:T(8,128)(2,1)S(1)} %constant_dynamic-update-slice_fusion.64), channel_id=1, source_target_pairs={{0,48},{16,0},{32,16},{48,32},{1,49},{17,1},{33,17},{49,33},{2,50}... | collective-permute-start | bytes 1474568 | tf_op jit(solution)/shard_map/fin/ppermute | solution.py:37
  537.9 12.3 %collective-permute-start.51 = (bf16[480,512]{1,0:T(8,128)(2,1)S(1)}, bf16[480,512]{1,0:T(8,128)(2,1)S(1)}, u32[]{:S(2)}, u32[]{:S(2)}) collective-permute-start(bf16[480,512]{1,0:T(8,128)(2,1)S(1)} %constant_dynamic-update-slice_fusion.64), channel_id=1, source_target_pairs={{0,16},{16,32},{32,48},{48,0},{1,17},{17,33},{33,49},{49,1},{2,18}... | collective-permute-start | bytes 1474568 | tf_op jit(solution)/shard_map/fin/ppermute | solution.py:37
  546.9 8.9 %collective-permute-start.53 = (bf16[240,512]{1,0:T(8,128)(2,1)S(1)}, bf16[240,512]{1,0:T(8,128)(2,1)S(1)}, u32[]{:S(2)}, u32[]{:S(2)}) collective-permute-start(bf16[240,512]{1,0:T(8,128)(2,1)S(1)} %slice.874), channel_id=1, source_target_pairs={{0,48},{16,0},{32,16},{48,32},{1,49},{17,1},{33,17},{49,33},{2,50}... | collective-permute-start | bytes 737288 | tf_op jit(solution)/shard_map/fin/ppermute | solution.py:37
  550.1 9.3 %collective-permute-start.52 = (bf16[240,512]{1,0:T(8,128)(2,1)S(1)}, bf16[240,512]{1,0:T(8,128)(2,1)S(1)}, u32[]{:S(2)}, u32[]{:S(2)}) collective-permute-start(bf16[240,512]{1,0:T(8,128)(2,1)S(1)} %slice.873), channel_id=1, source_target_pairs={{0,16},{16,32},{32,48},{48,0},{1,17},{17,33},{33,49},{49,1},{2,18}... | collective-permute-start | bytes 737288 | tf_op jit(solution)/shard_map/fin/ppermute | solution.py:37
  565.2 12.6 %collective-permute-start.54 = (bf16[960,512]{1,0:T(8,128)(2,1)S(1)}, bf16[960,512]{1,0:T(8,128)(2,1)S(1)}, u32[]{:S(2)}, u32[]{:S(2)}) collective-permute-start(bf16[960,512]{1,0:T(8,128)(2,1)S(1)} %constant_dynamic-update-slice_fusion.78), channel_id=1, source_target_pairs={{0,1},{1,0},{2,3},{3,2},{4,5},{5,4},{6,7},{7,6},{8,9},{9,8},{10,11... | collective-permute-start | bytes 2949128 | tf_op jit(solution)/shard_map/fin/ppermute | solution.py:24
  (89 other events, 845.8 us)

commit v4 on v3

--- a/solution.py
+++ b/solution.py
@@ -41,11 +41,15 @@
     return lax.ppermute(value, "section", [(0, 1)] if step > 0 else [(1, 0)])
 
 
-def summed(value):
-    for step in (1, 2, 4, 8):
-        value = value + lax.ppermute(value, "fsdp", [(i, i ^ step) for i in range(16)])
+def summed_x(value):
     for step in (1, 2):
         value = value + lax.ppermute(value, "dp", [(i, i ^ step) for i in range(4)])
+    return value
+
+
+def summed_over(value, *steps):
+    for step in steps:
+        value = value + lax.ppermute(value, "fsdp", [(i, i ^ step) for i in range(16)])
     return value
 
 
@@ -88,7 +92,49 @@
         out_specs=[pl.BlockSpec(memory_space=pltpu.VMEM)] * len(shapes),
         scratch_shapes=[pltpu.SemaphoreType.DMA((len(moves),))],
         compiler_params=pltpu.CompilerParams(vmem_limit_bytes=16 * 2**20),
+        cost_estimate=pl.CostEstimate(flops=2**20, bytes_accessed=2**16, transcendentals=0),
     )(jnp.stack(offsets).astype(jnp.int32), *pieces, *waits)
+
+
+def packing_kernel(moves, count, core_ref, *refs):
+    sources, outs, sems = refs[:count], refs[count:-1], refs[-1]
+    copies = []
+    for k, out in enumerate(outs):
+        half = core_ref[0] if k == 0 else 1 - core_ref[0]
+        for n, (source, row, half_width, column, width, at) in enumerate(moves):
+            start = pl.multiple_of(half * half_width + column, 128)
+            block = sources[source].at[pl.ds(row, 64), pl.ds(start, width)]
+            sem = sems.at[k * len(moves) + n]
+            copies.append(pltpu.make_async_copy(block, out.at[:, pl.ds(at, width)], sem))
+    for copy in copies:
+        copy.start()
+    for copy in copies:
+        copy.wait()
+
+
+def pack_halves(weights, gain_tile, core):
+    q, k, v, out, gate, up, down = weights
+    moves = []
+    for b in range(4):
+        moves += [(0, 0, 1024, 256 * b, 256), (1, 0, 512, 128 * b, 128), (2, 0, 512, 128 * b, 128)]
+    moves.append((7, 0, 0, 0, 128))
+    moves += [(3, 64 * m, 512, 0, 512) for m in range(2)]
+    for b in range(3):
+        moves += [(4, 0, 1536, 512 * b, 512), (5, 0, 1536, 512 * b, 512)]
+    moves += [(6, 64 * m, 512, 0, 512) for m in range(3)]
+    at, placed = 0, []
+    for move in moves:
+        placed.append((*move, at))
+        at += move[-1]
+    shape = jax.ShapeDtypeStruct((64, at), low)
+    return pl.pallas_call(
+        functools.partial(packing_kernel, tuple(placed), 8),
+        out_shape=[shape, shape],
+        in_specs=[pl.BlockSpec(memory_space=pltpu.SMEM)] + [pl.BlockSpec(memory_space=pl.ANY)] * 8,
+        out_specs=[pl.BlockSpec(memory_space=pltpu.VMEM)] * 2,
+        scratch_shapes=[pltpu.SemaphoreType.DMA((2 * len(placed),))],
+        compiler_params=pltpu.CompilerParams(vmem_limit_bytes=8 * 2**20),
+    )(core.reshape(1).astype(jnp.int32), q, k, v, out, gate, up, down, gain_tile)
 
 
 def joining_kernel(core_ref, own, other, out, sems):
@@ -117,6 +163,7 @@
         out_specs=pl.BlockSpec(memory_space=pltpu.VMEM),
         scratch_shapes=[pltpu.SemaphoreType.DMA((3,))],
         compiler_params=pltpu.CompilerParams(vmem_limit_bytes=16 * 2**20),
+        cost_estimate=pl.CostEstimate(flops=2**20, bytes_accessed=2**16, transcendentals=0),
     )(core.reshape(1).astype(jnp.int32), own, swap_core(own))
 
 
@@ -131,12 +178,12 @@
     return move_y(behind[0], 1)[None], move_y(ahead[1], -1)[None]
 
 
-def near_x(whole):
-    return move_x(whole, 1), move_x(whole, -1)
-
-
-def far_x(behind, ahead):
-    return move_x(behind[:4], 1), move_x(ahead[4:], -1)
+def near_x(first, second):
+    return move_x(first, 1), move_x(second, 1), move_x(first, -1), move_x(second, -1)
+
+
+def far_x(behind_first, behind_second, ahead_first, ahead_second):
+    return move_x(behind_first, 1), move_x(ahead_second, -1)
 
 
 def added(left, right):
@@ -201,7 +248,7 @@
         own = pick(values, zi, y)
         return (own.astype(f32) + second[0][k].astype(f32) + second[1][k].astype(f32)).astype(low)
 
-    return added(total(0, z), swap_z(total(1, 1 - z)))
+    return total(0, z), swap_z(total(1, 1 - z))
 
 
 def by_chip(gradient):
@@ -590,25 +637,10 @@
     )
     gain_tile = jnp.pad(gain_tile, ((0, 0), (0, 124)))
 
-    def column_half(index):
-        def cut(value):
-            return half_of(value[0], index, 1)
-
-        def mixed(parts, widths):
-            halves = [cut(p) for p in parts]
-            blocks = range(halves[0].shape[1] // widths[0])
-            return [h[:, b * w : (b + 1) * w] for b in blocks for h, w in zip(halves, widths)]
-
-        def rows_beside(value):
-            half = cut(value)
-            return [half[k : k + 64] for k in range(0, half.shape[0], 64)]
-
-        pieces = mixed((query_weight, key_weight, value_weight), (256, 128, 128)) + [gain_tile]
-        pieces += rows_beside(output_weight)
-        pieces += mixed((gate_weight, up_weight), (512, 512)) + rows_beside(down_weight)
-        return jnp.concatenate(pieces, axis=1)
-
-    chip = in_order(column_half(core), swap_core(column_half(1 - core)), core, 0)
+    shards = (query_weight, key_weight, value_weight, output_weight)
+    shards += (gate_weight, up_weight, down_weight)
+    kept, sent = pack_halves([shard[0] for shard in shards], gain_tile, core)
+    chip = in_order(kept, swap_core(sent), core, 0)
     zero = jnp.zeros_like(z)
     z_own = z ^ core
 
@@ -621,8 +653,8 @@
         m_z = swap_z(m_0)
         d_near, m_z = tied(d_near, m_z)
         d_far = far_y(*d_near)
-        d_all = jnp.concatenate([d_pair, *d_near, *d_far])
-        d_x = near_x(d_all)
+        d_all = (jnp.concatenate([d_pair, d_near[0]]), jnp.concatenate([d_near[1], *d_far]))
+        d_x = near_x(*d_all)
     with jax.named_scope("ag_mixer"):
         m_pair = jnp.stack([m_0, m_z])
         m_near = near_y(m_pair)
@@ -655,10 +687,9 @@
 
     def place_dense(part):
         moves, offsets = [], []
-        for piece, dx in enumerate((0, 1, 3, 2, 2)):
+        for piece, dx in enumerate((0, 0, 1, 1, 3, 3, 2, 2)):
             turn = (x - dx) & 3
-            kept = range(4) if piece == 3 else range(4, 8) if piece == 4 else range(8)
-            for index, n in enumerate(kept):
+            for index, n in enumerate(range(4 * (piece & 1), 4 * (piece & 1) + 4)):
                 dz, dy = origins[n]
                 moves.append((piece, index, 0, 0, 32, 3072, 0))
                 offsets.append(((z ^ dz) * 4 + ((y - dy) & 3)) * 128 + turn * 32)
@@ -666,7 +697,7 @@
                 for m in range(3):
                     moves.append((piece, index, 0, 3072 + 512 * m, 32, 512, 1))
                     offsets.append(block + 64 * m + (turn & 1) * 32)
-        return place((d_all, *d_x, *d_x_far), moves, offsets, ((MODEL, 3072), (3072, 512)), (part,))
+        return place((*d_all, *d_x, *d_x_far), moves, offsets, ((MODEL, 3072), (3072, 512)), (part, w_qkv[1]))
 
     own_dense = []
 
@@ -710,8 +741,8 @@
             g_gu = product(a2, a2_o, dgu[0], swap_core(dgu[1])).reshape(8, 128, 3072)
             da2, g_gu = tied(da2, g_gu)
 
-            def columns_of(place):
-                return lax.dynamic_slice_in_dim(g_gu, place * 768, 768, 2)
+            def columns_of(place, start=0, width=768):
+                return lax.dynamic_slice_in_dim(g_gu, place * 768 + start, width, 2)
 
             done["gu"] = (columns_of, reduce_x_first(columns_of, x))
         with jax.named_scope("g_down"):
@@ -726,36 +757,42 @@
             dr_o = swap_core(half_of(dr, 1 - core, 1))
             g_out = by_halves(att, att_o, half_of(dr, core, 1), dr_o)
             g_do = jnp.concatenate([done["down"], g_out], axis=2)
+            dr, g_do = tied(dr, g_do)
         with jax.named_scope("rs_do"):
             done["do"] = reduce_y_first(g_do, z_flip, y)
-        with jax.named_scope("rs_gu"):
-            columns_of, first = done["gu"]
-            ready = reduce_x_ready(columns_of, x, first)
-            dr, ready, g_do = tied(dr, ready, g_do)
-            done["gu2"] = near_x_two(*ready)
         return dr, g_do
 
     def between_heads(dr, dqkv_1, g_do):
+        first_x, first_y, dqkv_1 = tied(done["gu"][1], done["do"], dqkv_1)
         with jax.named_scope("g_qkv"):
             done["dqkv_o"] = swap_core(dqkv_1)
+        ready = []
+        with jax.named_scope("rs_gu"):
+            ready.append(reduce_x_ready(done["gu"][0], x, first_x))
         with jax.named_scope("rs_do"):
-            first, dqkv_1 = tied(done["do"], dqkv_1)
-            ready = reduce_y_ready(g_do, z_flip, y, first)
-            dr, ready = tied(dr, ready)
-            done["do2"] = near_y_two(*ready)
+            ready.append(reduce_y_ready(g_do, z_flip, y, first_y))
+        dr, ready = tied(dr, ready)
+        with jax.named_scope("rs_gu"):
+            done["gu2"] = near_x_two(*ready[0])
+        with jax.named_scope("rs_do"):
+            done["do2"] = near_y_two(*ready[1])
         return dr
 
     def after_attention(dqkv, da1, g_do):
-        own, second_gu, second = tied(dqkv[0], done["gu2"], done["do2"])
+        own = dqkv[0]
         with jax.named_scope("g_qkv"):
             g_qkv = by_chip(product(a1, a1_o, own, done["dqkv_o"]))
-        with jax.named_scope("rs_qg"):
-            mine = reduce_x_third(done["gu"][0], x, second_gu).reshape(2, 4, 128, 768)
-            both_parts = jnp.concatenate([g_qkv, mine], axis=3)
-            da1, both_parts = tied(da1, both_parts)
-            done["qg"] = (both_parts, reduce_y_first(both_parts, z, y))
+            da1, g_qkv = tied(da1, g_qkv)
+        with jax.named_scope("rs_q"):
+            first = reduce_y_first(g_qkv, z, y)
+        first, second = tied(first, done["do2"])
+        with jax.named_scope("rs_q"):
+            done["q"] = (g_qkv, reduce_y_second(g_qkv, z, y, first))
+        with jax.named_scope("rs_gu"):
+            mine = reduce_x_third(done["gu"][0], x, done["gu2"]).reshape(2, 4, 128, 768)
+            done["g"] = (mine, reduce_y_first(mine, z, y))
         with jax.named_scope("rs_do"):
-            done["s_do"] = reduce_z(g_do, z_flip, y, second)
+            done["s_do"] = added(*reduce_z(g_do, z_flip, y, second))
         return da1
 
     with jax.named_scope("b2"):
@@ -763,16 +800,27 @@
             cotangent, saved, weights, gains, tables, (after_dgu, after_dr, after_attention, between_heads)
         )
     endpoints = jnp.where(first_section, dh, out).reshape(1, 2, 1, 128, MODEL)
-    with jax.named_scope("rs_qg"):
-        g_qg, first = done["qg"]
-        s_qg = reduce_z(g_qg, z, y, reduce_y_second(g_qg, z, y, first))
+    g_qkv, q_second = done["q"]
+    mine, g_first = done["g"]
+    gain_part = jnp.concatenate(gain_grads).reshape(18, 128)
+    mine, gain_part = tied(mine, gain_part)
+    gain_part = summed_over(summed_x(gain_part), 1, 8)
+    q_second, g_first = tied(q_second, g_first)
+    with jax.named_scope("rs_gu"):
+        g_second = reduce_y_second(mine, z, y, g_first)
+    with jax.named_scope("rs_q"):
+        q_z = reduce_z(g_qkv, z, y, q_second)
+        q_z, g_second = tied(q_z, g_second)
+        s_q = added(*q_z)
+    with jax.named_scope("rs_gu"):
+        s_gu = added(*reduce_z(mine, z, y, g_second))
     with jax.named_scope("rs_x"):
-        s_do, s_qkv = quarters(done["s_do"][:384]), quarters(s_qg[:, :2048])
+        s_do, s_qkv = quarters(done["s_do"][:384]), quarters(s_q)
         s_o = quarters(done["s_do"][384:])
         blocks = [s_qkv[:, :, k : k + 512] for k in range(0, 2048, 512)] + [s_do, s_o]
         mine = reduce_x(jnp.concatenate(blocks, axis=1), x)
         m_qkv = jnp.concatenate([mine[k : k + 32] for k in range(0, 128, 32)], axis=1)
-        m_gu = jnp.concatenate([s_qg[k : k + 32, 2048:] for k in range(0, 128, 32)], axis=1)
+        m_gu = jnp.concatenate([s_gu[k : k + 32] for k in range(0, 128, 32)], axis=1)
     with jax.named_scope("fin"):
         parts = (m_qkv, m_gu, mine[128:224], mine[224:])
         qkv, gu, down, out_w = finish(parts, x, core)
@@ -786,7 +834,7 @@
 
         return in_order(*(part(p) for p in pair), core, 1)[None]
 
-    sums = summed(jnp.concatenate(gain_grads).reshape(18, 128)).reshape(-1)
+    sums = summed_over(gain_part, 2, 4).reshape(-1)
 
     def gain_rows(start, width):
         return lax.dynamic_slice_in_dim(sums, start + place_at * width, width, 0)[None]

time: 592 us -> 548 us (0.926)
  waiting for transfers between devices: 234 us -> 179 us
  Pallas kernels: 124 us -> 134 us
  starting transfers between devices: 88.8 us -> 96.2 us
    ppermute x16 -> x20, waiting for transfers between devices: 98.7 us -> 35.8 us  [move_y(): return lax.ppermute(value, 'fsdp', pairs)]
    ppermute x4 -> x5, waiting for transfers between devices: 24.2 us -> 34.1 us  [swap_z(): return lax.ppermute(value, 'fsdp', [(i, i ^ 8) for i in range(16)])]
    pallas_call x16, Pallas kernels: 111 us -> 120 us  [call(): pl.pallas_call(body, grid=(steps,), in_specs=specs, out_specs=[p[0] for p...]
    ppermute x16 -> x18, waiting for transfers between devices: 59.6 us -> 65.9 us  [move_x(): return lax.ppermute(value, 'dp', [(i, (i + step) % 4) for i in range(4)])]
    ppermute x16 -> x20, starting transfers between devices: 22.8 us -> 28.1 us  [move_y(): return lax.ppermute(value, 'fsdp', pairs)]
    ppermute x4 -> x5, starting transfers between devices: 10.4 us -> 13.3 us  [swap_z(): return lax.ppermute(value, 'fsdp', [(i, i ^ 8) for i in range(16)])]
    unnamed x251 -> x208, local copies, waits for them, and re-layouts: 51.3 us -> 53.9 us
    ppermute x16 -> x18, starting transfers between devices: 21.8 us -> 20.8 us  [move_x(): return lax.ppermute(value, 'dp', [(i, (i + step) % 4) for i in range(4)])]
  transfers between devices with their start and end apart: 55 -> 62, of which waited for: 28 -> 32; matrix products, arithmetic and copies ran while one was open for 9% -> 10% of each run, Pallas kernels for 14% -> 17%
where the time goes in v4:
time: 548 us; the launch traced here: 540 us
  waiting for transfers between devices  179 us (33%)
  Pallas kernels  134 us (24%)
  starting transfers between devices  96.2 us (18%)
  local copies, waits for them, and re-layouts  74.6 us (14%)
  other arithmetic  38.9 us (7%)
  matrix products  14 us (3%)
    pallas_call x16, Pallas kernels, call(): pl.pallas_call(body, grid=(steps,), in_specs=specs, out_specs=[p[0] for p...  120 us
    ppermute x18, waiting for transfers between devices, move_x(): return lax.ppermute(value, 'dp', [(i, (i + step) % 4) for i in range(4)])  65.9 us
    unnamed x208, local copies, waits for them, and re-layouts  53.9 us
    ppermute x20, waiting for transfers between devices, move_y(): return lax.ppermute(value, 'fsdp', pairs)  35.8 us
    ppermute x5, waiting for transfers between devices, swap_z(): return lax.ppermute(value, 'fsdp', [(i, i ^ 8) for i in range(16)])  34.1 us
    ppermute x20, starting transfers between devices, move_y(): return lax.ppermute(value, 'fsdp', pairs)  28.1 us
    ppermute x2, waiting for transfers between devices, move_section(): return lax.ppermute(value, 'section', [(0, 1)] if step > 0 else [(1, 0)])  24.7 us
    ppermute x18, starting transfers between devices, move_x(): return lax.ppermute(value, 'dp', [(i, (i + step) % 4) for i in range(4)])  20.8 us
  transfers between devices with their start and end apart: 62, of which 32 were waited for; matrix products, arithmetic and copies ran while one was open for 10% of the time, Pallas kernels for 17%

profile of v4, /device:TPU:1, one launch (start us, length us, event | category | flops | bytes accessed | tf_op | source)
XLA Modules:
  0.0 539.7 jit_solution(7363726874064410297)
XLA Ops:
  13.8 3.8 collective-permute-start.1
  17.8 6.9 %collective-permute-done.1 = bf16[32,4608]{1,0:T(8,128)(2,1)S(1)} collective-permute-done((bf16[32,4608]{1,0:T(8,128)(2,1)S(1)}, bf16[32,4608]{1,0:T(8,128)(2,1)S(1)}, u32[]{:S(2)}, u32[]{:S(2)}) %collective-permute-start.1) | collective-permute-done | bytes 294944 | tf_op jit(solution)/shard_map/ag_dense/ppermute | solution.py:28
  27.6 14.6 %collective-permute-done.4 = bf16[128,3200]{1,0:T(8,128)(2,1)S(1)} collective-permute-done((bf16[128,3200]{1,0:T(8,128)(2,1)S(1)}, bf16[128,3200]{1,0:T(8,128)(2,1)S(1)}, u32[]{:S(2)}, u32[]{:S(2)}) %collective-permute-start.4) | collective-permute-done | bytes 819232 | tf_op jit(solution)/shard_map/ag_dense/ppermute | solution.py:28
  43.7 2.8 collective-permute-start.9
  56.2 14.2 %collective-permute-done.7.refs_2_ = bf16[4,32,4608]{2,1,0:T(8,128)(2,1)} collective-permute-done((bf16[4,32,4608]{2,1,0:T(8,128)(2,1)S(1)}, bf16[4,32,4608]{2,1,0:T(8,128)(2,1)}, u32[]{:S(2)}, u32[]{:S(2)}) %collective-permute-start.7) | collective-permute-done | bytes 1179680 | tf_op jit(solution)/shard_map/ag_dense/ppermute | solution.py:37
  76.4 19.2 %collective-permute-done.10.refs_3_ = bf16[4,32,4608]{2,1,0:T(8,128)(2,1)S(1)} collective-permute-done((bf16[4,32,4608]{2,1,0:T(8,128)(2,1)S(1)}, bf16[4,32,4608]{2,1,0:T(8,128)(2,1)S(1)}, u32[]{:S(2)}, u32[]{:S(2)}) %collective-permute-start.10) | collective-permute-done | bytes 1179680 | tf_op jit(solution)/shard_map/ag_dense/ppermute | solution.py:37
  96.6 4.1 collective-permute-done.12.refs_5_
  107.7 13.1 %collective-permute-done.13 = bf16[128,3200]{1,0:T(8,128)(2,1)S(1)} collective-permute-done((bf16[128,3200]{1,0:T(8,128)(2,1)}, bf16[128,3200]{1,0:T(8,128)(2,1)S(1)}, u32[]{:S(2)}, u32[]{:S(2)}) %collective-permute-start.13) | collective-permute-done | bytes 819232 | tf_op jit(solution)/shard_map/ag_mixer/ppermute | solution.py:33
  125.7 4.6 ag_mixer.2
  130.3 5.6 %collective-permute-start.16 = (bf16[1024,2176]{1,0:T(8,128)(2,1)}, bf16[1024,2176]{1,0:T(8,128)(2,1)}, u32[]{:S(2)}, u32[]{:S(2)}) collective-permute-start(bf16[1024,2176]{1,0:T(8,128)(2,1)} %get-tuple-element.104.refs_6_.refs_10_), channel_id=1, source_target_pairs={{0,1},{1,0},{2,3},{3,2},{4,5},{5,4},{6,7},{7,6},{8,9},{9,8},{10,11... | collective-permute-start | bytes 13369352 | tf_op jit(solution)/shard_map/ag_mixer/ppermute | solution.py:24
  142.0 4.4 collective-permute-done.15.other
  148.7 8.6 %f1.5 = (f32[256,1024]{1,0:T(8,128)S(1)}, bf16[256,1024]{1,0:T(8,128)(2,1)S(1)}, f32[256,2048]{1,0:T(8,128)}, bf16[256,1024]{1,0:T(8,128)(2,1)}) custom-call(f32[256,1024]{1,0:T(8,128)S(1)} %bitcast_convert_fusion.refs_0_, f32[1,1024]{1,0:T(1,128)S(1)} %bitcast.420, f32[1,128]{1,0:T(1,128)S(1)} %broadcast_in_dim_reshape.4.refs_2_.refs_3_.refs_6_, ...), custom_call_target="tpu_custom_call" | custom-call | flops 1048576 | bytes 65536 | tf_op jit(solution)/shard_map/f1/pallas_call | solution.py:414
  157.3 7.4 %collective-permute-done.17.refs_6_ = bf16[4,32,4608]{2,1,0:T(8,128)(2,1)} collective-permute-done((bf16[4,32,4608]{2,1,0:T(8,128)(2,1)}, bf16[4,32,4608]{2,1,0:T(8,128)(2,1)}, u32[]{:S(2)}, u32[]{:S(2)}) %collective-permute-start.17) | collective-permute-done | bytes 1179680 | tf_op jit(solution)/shard_map/ppermute | solution.py:37
  164.7 5.7 %f1.6 = (bf16[1024,3072]{1,0:T(8,128)(2,1)S(1)}, bf16[3072,512]{1,0:T(8,128)(2,1)S(1)}) custom-call(s32[128]{0:T(128)S(1)} %stack.770.offsets, bf16[4,32,4608]{2,1,0:T(8,128)(2,1)S(1)} %copy-done.26, bf16[4,32,4608]{2,1,0:T(8,128)(2,1)S(1)} %copy-done.28, bf16[4,32,4608]{2,1,0:T(8,128)(2,1)} %collective-permute-done.7.refs_2_, ...), custom_call_target="tpu_custom_call" | custom-call | flops 1048576 | bytes 65536 | tf_op jit(solution)/shard_map/f1/pallas_call | solution.py:87
  171.9 8.1 %f1.7 = (f32[256,1024]{1,0:T(8,128)S(1)}, f32[256,2048]{1,0:T(8,128)}, bf16[256,1024]{1,0:T(8,128)(2,1)}) custom-call(f32[256,1024]{1,0:T(8,128)S(1)} %get-tuple-element.106.refs_8_.refs_0_, bf16[256,1024]{1,0:T(8,128)(2,1)S(1)} %get-tuple-element.107.refs_1_, f32[1,128]{1,0:T(1,128)S(1)} %broadcast_in_dim_reshape.4.refs_2_.refs_3_.refs_6_, ...), custom_call_target="tpu_custom_call" | custom-call | flops 1048576 | bytes 65536 | tf_op jit(solution)/shard_map/f1/pallas_call | solution.py:414
  180.0 5.9 %collective-permute-done.19.other = bf16[3072,512]{1,0:T(8,128)(2,1)S(1)} collective-permute-done((bf16[3072,512]{1,0:T(8,128)(2,1)S(1)}, bf16[3072,512]{1,0:T(8,128)(2,1)S(1)}, u32[]{:S(2)}, u32[]{:S(2)}) %collective-permute-start.19) | collective-permute-done | bytes 3145760 | tf_op jit(solution)/shard_map/ag_dense/ppermute | solution.py:24
  186.8 4.9 f1.8
  191.7 6.7 %f1.9 = (f32[256,1024]{1,0:T(8,128)S(1)}, f32[256,3072]{1,0:T(8,128)}, bf16[256,1536]{1,0:T(8,128)(2,1)}) custom-call(f32[256,1024]{1,0:T(8,128)S(1)} %get-tuple-element.115.refs_0_, bf16[256,1024]{1,0:T(8,128)(2,1)S(1)} %get-tuple-element.116.refs_1_, bf16[1024,3072]{1,0:T(8,128)(2,1)} %collective-permute-done.20.refs_2_.refs_3_, ...), custom_call_target="tpu_custom_call" | custom-call | flops 1048576 | bytes 65536 | tf_op jit(solution)/shard_map/f1/pallas_call | solution.py:414
  201.7 10.6 %collective-permute-done.21 = bf16[256,1024]{1,0:T(8,128)(2,1)} collective-permute-done((bf16[256,1024]{1,0:T(8,128)(2,1)}, bf16[256,1024]{1,0:T(8,128)(2,1)}, u32[]{:S(2)}, u32[]{:S(2)}) %collective-permute-start.21) | collective-permute-done | bytes 524320 | tf_op jit(solution)/shard_map/ppermute | solution.py:41
  216.2 7.5 %f2.4 = (f32[256,1024]{1,0:T(8,128)S(1)}, bf16[256,1024]{1,0:T(8,128)(2,1)S(1)}, f32[256,2048]{1,0:T(8,128)S(1)}, bf16[256,1024]{1,0:T(8,128)(2,1)S(1)}) custom-call(f32[256,1024]{1,0:T(8,128)S(1)} %get-tuple-element.243.refs_0_, f32[1,1024]{1,0:T(1,128)S(1)} %bitcast.421, f32[1,128]{1,0:T(1,128)S(1)} %broadcast_in_dim_reshape.4.refs_2_.refs_3_.refs_6_, ...), custom_call_target="tpu_custom_call" | custom-call | flops 1048576 | bytes 65536 | tf_op jit(solution)/shard_map/f2/pallas_call | solution.py:414
  225.1 7.6 %f2.5 = (f32[256,1024]{1,0:T(8,128)S(1)}, f32[256,2048]{1,0:T(8,128)S(1)}, bf16[256,1024]{1,0:T(8,128)(2,1)S(1)}) custom-call(f32[256,1024]{1,0:T(8,128)S(1)} %get-tuple-element.118.refs_0_, bf16[256,1024]{1,0:T(8,128)(2,1)S(1)} %get-tuple-element.119.refs_1_, f32[1,128]{1,0:T(1,128)S(1)} %broadcast_in_dim_reshape.4.refs_2_.refs_3_.refs_6_, ...), custom_call_target="tpu_custom_call" | custom-call | flops 1048576 | bytes 65536 | tf_op jit(solution)/shard_map/f2/pallas_call | solution.py:414
  234.1 4.2 f2.6
  240.5 6.0 %f2.7 = (f32[256,1024]{1,0:T(8,128)S(1)}, f32[256,3072]{1,0:T(8,128)S(1)}, bf16[256,1536]{1,0:T(8,128)(2,1)S(1)}) custom-call(f32[256,1024]{1,0:T(8,128)S(1)} %get-tuple-element.121.refs_0_, bf16[256,1024]{1,0:T(8,128)(2,1)S(1)} %get-tuple-element.122.refs_1_, bf16[1024,3072]{1,0:T(8,128)(2,1)} %collective-permute-done.20.refs_2_.refs_3_, ...), custom_call_target="tpu_custom_call" | custom-call | flops 1048576 | bytes 65536 | tf_op jit(solution)/shard_map/f2/pallas_call | solution.py:414
  252.7 6.0 %b1.4 = (bf16[256,3072]{1,0:T(8,128)(2,1)}, f32[256,1024]{1,0:T(8,128)S(1)}) custom-call(bf16[256,1024]{1,0:T(8,128)(2,1)S(1)} %bitcast.409, bf16[3072,1024]{1,0:T(8,128)(2,1)S(1)} %bitcast.406, f32[256,3072]{1,0:T(8,128)S(1)} %copy-done.17, bf16[1024,3072]{1,0:T(8,128)(2,1)} %collective-permute-done.20.refs_2_.refs_3_), custom_call_target="tpu_custom_call" | custom-call | flops 1048576 | bytes 65536 | tf_op jit(solution)/shard_map/b1/pallas_call | solution.py:414
  258.7 4.9 b1.5
  265.7 11.4 %b1.6 = (bf16[256,2048]{1,0:T(8,128)(2,1)}, f32[256,1024]{1,0:T(8,128)S(1)}, f32[1,128]{1,0:T(1,128)S(1)}, f32[1,128]{1,0:T(1,128)S(1)}) custom-call(bf16[256,1024]{1,0:T(8,128)(2,1)S(1)} %fusion.69.refs_0_.refs_3_, bf16[2048,1024]{1,0:T(8,128)(2,1)S(1)} %copy-done.4, f32[256,2048]{1,0:T(8,128)S(1)} %copy-done.23, ...), custom_call_target="tpu_custom_call" | custom-call | flops 1048576 | bytes 65536 | tf_op jit(solution)/shard_map/b1/pallas_call | solution.py:414
  277.1 11.4 %b1.7 = (bf16[256,2048]{1,0:T(8,128)(2,1)}, f32[256,1024]{1,0:T(8,128)S(1)}, f32[1,128]{1,0:T(1,128)}, f32[1,128]{1,0:T(1,128)}) custom-call(f32[256,1024]{1,0:T(8,128)S(1)} %get-tuple-element.128.refs_0_, f32[1,128]{1,0:T(1,128)S(1)} %get-tuple-element.129.refs_1_, f32[1,128]{1,0:T(1,128)S(1)} %get-tuple-element.130.refs_2_, ...), custom_call_target="tpu_custom_call" | custom-call | flops 1048576 | bytes 65536 | tf_op jit(solution)/shard_map/b1/pallas_call | solution.py:414
  291.6 14.1 %collective-permute-done.22 = bf16[256,1024]{1,0:T(8,128)(2,1)S(1)} collective-permute-done((bf16[256,1024]{1,0:T(8,128)(2,1)S(1)}, bf16[256,1024]{1,0:T(8,128)(2,1)S(1)}, u32[]{:S(2)}, u32[]{:S(2)}) %collective-permute-start.22) | collective-permute-done | bytes 524320 | tf_op jit(solution)/shard_map/ppermute | solution.py:41
  306.9 6.2 %b2.4 = (bf16[256,3072]{1,0:T(8,128)(2,1)}, f32[256,1024]{1,0:T(8,128)S(1)}) custom-call(bf16[256,1024]{1,0:T(8,128)(2,1)S(1)} %get-tuple-element.240.refs_0_.refs_1_, bf16[3072,1024]{1,0:T(8,128)(2,1)S(1)} %bitcast.406, f32[256,3072]{1,0:T(8,128)S(1)} %copy-done.18, bf16[1024,3072]{1,0:T(8,128)(2,1)} %collective-permute-done.20.refs_2_.refs_3_), custom_call_target="tpu_custom_call" | custom-call | flops 1048576 | bytes 65536 | tf_op jit(solution)/shard_map/b2/pallas_call | solution.py:414
  326.3 4.4 b2.5
  335.0 6.9 %convolution_convert_fusion = bf16[1024,3072]{1,0:T(8,128)(2,1)} fusion(bf16[256,3072]{1,0:T(8,128)(2,1)} %collective-permute-done.24, bf16[256,3072]{1,0:T(8,128)(2,1)S(1)} %get-tuple-element.139, bf16[256,1024]{1,0:T(8,128)(2,1)S(1)} %get-tuple-element.272, bf16[256,1024]{1,0:T(8,128)(2,1)S(1)} %copy-done.36), kind=kOutput, calls=%fused_computation | convolution fusion | flops 3232759808 | bytes 10485760 | tf_op jit(solution)/shard_map/b2/g_gu/dot_general | solution.py:610
  349.0 3.3 constant_dynamic-slice_fusion.5
  363.7 11.2 %b2.6 = (bf16[256,2048]{1,0:T(8,128)(2,1)}, f32[256,1024]{1,0:T(8,128)S(1)}, f32[1,128]{1,0:T(1,128)S(1)}, f32[1,128]{1,0:T(1,128)S(1)}) custom-call(bf16[256,1024]{1,0:T(8,128)(2,1)S(1)} %get-tuple-element.155.refs_0_.refs_3_, bf16[2048,1024]{1,0:T(8,128)(2,1)S(1)} %copy-done.5, f32[256,2048]{1,0:T(8,128)S(1)} %copy-done.24, ...), custom_call_target="tpu_custom_call" | custom-call | flops 1048576 | bytes 65536 | tf_op jit(solution)/shard_map/b2/pallas_call | solution.py:414
  395.7 10.9 %b2.7 = (bf16[256,2048]{1,0:T(8,128)(2,1)S(1)}, f32[256,1024]{1,0:T(8,128)S(1)}, f32[1,128]{1,0:T(1,128)S(1)}, f32[1,128]{1,0:T(1,128)S(1)}) custom-call(f32[256,1024]{1,0:T(8,128)S(1)} %copy-done.44, f32[1,128]{1,0:T(1,128)S(1)} %get-tuple-element.146.refs_1_, f32[1,128]{1,0:T(1,128)S(1)} %get-tuple-element.147.refs_2_, ...), custom_call_target="tpu_custom_call" | custom-call | flops 1048576 | bytes 65536 | tf_op jit(solution)/shard_map/b2/pallas_call | solution.py:414
  406.6 3.6 convolution_convert_fusion.1
  413.4 5.1 collective-permute-done.42
  420.3 9.3 %collective-permute-done.40 = bf16[128,2048]{1,0:T(8,128)(2,1)S(1)} collective-permute-done((bf16[128,2048]{1,0:T(8,128)(2,1)}, bf16[128,2048]{1,0:T(8,128)(2,1)S(1)}, u32[]{:S(2)}, u32[]{:S(2)}) %collective-permute-start.40) | collective-permute-done | bytes 524320 | tf_op jit(solution)/shard_map/b2/rs_q/ppermute | solution.py:33
  435.9 3.0 add_convert_fusion
  439.0 2.8 collective-permute-done.34
  446.1 4.5 collective-permute-start.36
  452.4 3.4 collective-permute-start.37
  456.9 3.3 collective-permute-start.51
  462.9 3.4 collective-permute-start.48
  476.3 9.3 %collective-permute-done.48 = bf16[128,2048]{1,0:T(8,128)(2,1)S(1)} collective-permute-done((bf16[128,2048]{1,0:T(8,128)(2,1)S(1)}, bf16[128,2048]{1,0:T(8,128)(2,1)S(1)}, u32[]{:S(2)}, u32[]{:S(2)}) %collective-permute-start.48) | collective-permute-done | bytes 524320 | tf_op jit(solution)/shard_map/rs_q/ppermute | solution.py:28
  497.8 3.2 collective-permute-done.53
  504.0 5.7 %collective-permute-done.57 = bf16[480,512]{1,0:T(8,128)(2,1)S(1)} collective-permute-done((bf16[480,512]{1,0:T(8,128)(2,1)S(1)}, bf16[480,512]{1,0:T(8,128)(2,1)S(1)}, u32[]{:S(2)}, u32[]{:S(2)}) %collective-permute-start.57) | collective-permute-done | bytes 491552 | tf_op jit(solution)/shard_map/fin/ppermute | solution.py:37
  511.4 5.5 %collective-permute-done.60 = bf16[240,512]{1,0:T(8,128)(2,1)S(1)} collective-permute-done((bf16[240,512]{1,0:T(8,128)(2,1)S(1)}, bf16[240,512]{1,0:T(8,128)(2,1)S(1)}, u32[]{:S(2)}, u32[]{:S(2)}) %collective-permute-start.60) | collective-permute-done | bytes 245792 | tf_op jit(solution)/shard_map/fin/ppermute | solution.py:37
  524.0 6.4 %collective-permute-start.61 = (bf16[960,512]{1,0:T(8,128)(2,1)S(1)}, bf16[960,512]{1,0:T(8,128)(2,1)S(1)}, u32[]{:S(2)}, u32[]{:S(2)}) collective-permute-start(bf16[960,512]{1,0:T(8,128)(2,1)S(1)} %dynamic-slice_dynamic-update-slice_fusion.7), channel_id=1, source_target_pairs={{0,1},{1,0},{2,3},{3,2},{4,5},{5,4},{6,7},{7,6},{8,9},{9,8},{10,11... | collective-permute-start | bytes 2949128 | tf_op jit(solution)/shard_map/fin/ppermute | solution.py:24
  (448 shorter events, 201.1 us)
Async XLA Ops:
  13.8 10.8 %collective-permute-start.1 = (bf16[32,4608]{1,0:T(8,128)(2,1)S(1)}, bf16[32,4608]{1,0:T(8,128)(2,1)S(1)}, u32[]{:S(2)}, u32[]{:S(2)}) collective-permute-start(bf16[32,4608]{1,0:T(8,128)(2,1)S(1)} %fusion.45), channel_id=1, source_target_pairs={{0,8},{1,9},{2,10},{3,11},{4,12},{5,13},{6,14},{7,15},{8,0},{9,1},... | collective-permute-start | bytes 884744 | tf_op jit(solution)/shard_map/ag_dense/ppermute | solution.py:28
  17.7 24.6 %collective-permute-start.4 = (bf16[128,3200]{1,0:T(8,128)(2,1)S(1)}, bf16[128,3200]{1,0:T(8,128)(2,1)S(1)}, u32[]{:S(2)}, u32[]{:S(2)}) collective-permute-start(bf16[128,3200]{1,0:T(8,128)(2,1)S(1)} %fusion.32), channel_id=1, source_target_pairs={{0,8},{1,9},{2,10},{3,11},{4,12},{5,13},{6,14},{7,15},{8,0},{9,1},... | collective-permute-start | bytes 2457608 | tf_op jit(solution)/shard_map/ag_dense/ppermute | solution.py:28
  24.7 17.5 %collective-permute-start.2 = (bf16[2,32,4608]{2,1,0:T(8,128)(2,1)S(1)}, bf16[2,32,4608]{2,1,0:T(8,128)(2,1)S(1)}, u32[]{:S(2)}, u32[]{:S(2)}) collective-permute-start(bf16[2,32,4608]{2,1,0:T(8,128)(2,1)S(1)} %pad_maximum_fusion.12), channel_id=1, source_target_pairs={{0,2},{1,3},{2,4},{3,5},{4,6},{5,7},{6,0},{7,1},{8,10},{9,11},{10,... | collective-permute-start | bytes 1769480 | tf_op jit(solution)/shard_map/ag_dense/ppermute | solution.py:33
  26.1 16.1 %collective-permute-start.3 = (bf16[2,32,4608]{2,1,0:T(8,128)(2,1)S(1)}, bf16[2,32,4608]{2,1,0:T(8,128)(2,1)S(1)}, u32[]{:S(2)}, u32[]{:S(2)}) collective-permute-start(bf16[2,32,4608]{2,1,0:T(8,128)(2,1)S(1)} %pad_maximum_fusion.12), channel_id=1, source_target_pairs={{0,6},{1,7},{2,0},{3,1},{4,2},{5,3},{6,4},{7,5},{8,14},{9,15},{10,... | collective-permute-start | bytes 1769480 | tf_op jit(solution)/shard_map/ag_dense/ppermute | solution.py:33
  42.4 28.0 %collective-permute-start.7 = (bf16[4,32,4608]{2,1,0:T(8,128)(2,1)S(1)}, bf16[4,32,4608]{2,1,0:T(8,128)(2,1)}, u32[]{:S(2)}, u32[]{:S(2)}) collective-permute-start(bf16[4,32,4608]{2,1,0:T(8,128)(2,1)S(1)} %pad_maximum_fusion.8.refs_0_), channel_id=1, source_target_pairs={{0,16},{16,32},{32,48},{48,0},{1,17},{17,33},{33,49},{49,1},{2,18}... | collective-permute-start | bytes 3538952 | tf_op jit(solution)/shard_map/ag_dense/ppermute | solution.py:37
  46.5 8.4 %collective-permute-start.8 = (bf16[32,4608]{1,0:T(8,128)(2,1)S(1)}, bf16[32,4608]{1,0:T(8,128)(2,1)S(1)}, u32[]{:S(2)}, u32[]{:S(2)}) collective-permute-start(bf16[32,4608]{1,0:T(8,128)(2,1)S(1)} %slice_bitcast_fusion.3), channel_id=1, source_target_pairs={{0,2},{1,3},{2,4},{3,5},{4,6},{5,7},{6,0},{7,1},{8,10},{9,11},{10,... | collective-permute-start | bytes 884744 | tf_op jit(solution)/shard_map/ag_dense/ppermute | solution.py:33
  46.7 54.0 %collective-permute-start.5 = (bf16[2,128,3200]{2,1,0:T(8,128)(2,1)S(1)}, bf16[2,128,3200]{2,1,0:T(8,128)(2,1)S(1)}, u32[]{:S(2)}, u32[]{:S(2)}) collective-permute-start(bf16[2,128,3200]{2,1,0:T(8,128)(2,1)S(1)} %pad_maximum_fusion.3.refs_0_), channel_id=1, source_target_pairs={{0,2},{1,3},{2,4},{3,5},{4,6},{5,7},{6,0},{7,1},{8,10},{9,11},{10,... | collective-permute-start | bytes 4915208 | tf_op jit(solution)/shard_map/ag_mixer/ppermute | solution.py:33
  46.8 54.0 %collective-permute-start.6 = (bf16[2,128,3200]{2,1,0:T(8,128)(2,1)S(1)}, bf16[2,128,3200]{2,1,0:T(8,128)(2,1)S(1)}, u32[]{:S(2)}, u32[]{:S(2)}) collective-permute-start(bf16[2,128,3200]{2,1,0:T(8,128)(2,1)S(1)} %pad_maximum_fusion.3.refs_0_), channel_id=1, source_target_pairs={{0,6},{1,7},{2,0},{3,1},{4,2},{5,3},{6,4},{7,5},{8,14},{9,15},{10,... | collective-permute-start | bytes 4915208 | tf_op jit(solution)/shard_map/ag_mixer/ppermute | solution.py:33
  51.7 23.7 %collective-permute-start.11 = (bf16[4,32,4608]{2,1,0:T(8,128)(2,1)S(1)}, bf16[4,32,4608]{2,1,0:T(8,128)(2,1)S(1)}, u32[]{:S(2)}, u32[]{:S(2)}) collective-permute-start(bf16[4,32,4608]{2,1,0:T(8,128)(2,1)S(1)} %pad_maximum_fusion.8.refs_0_), channel_id=1, source_target_pairs={{0,48},{16,0},{32,16},{48,32},{1,49},{17,1},{33,17},{49,33},{2,50}... | collective-permute-start | bytes 3538952 | tf_op jit(solution)/shard_map/ag_dense/ppermute | solution.py:37
  55.0 40.5 %collective-permute-start.10 = (bf16[4,32,4608]{2,1,0:T(8,128)(2,1)S(1)}, bf16[4,32,4608]{2,1,0:T(8,128)(2,1)S(1)}, u32[]{:S(2)}, u32[]{:S(2)}) collective-permute-start(bf16[4,32,4608]{2,1,0:T(8,128)(2,1)S(1)} %pad_maximum_fusion.9.refs_1_), channel_id=1, source_target_pairs={{0,16},{16,32},{32,48},{48,0},{1,17},{17,33},{33,49},{49,1},{2,18}... | collective-permute-start | bytes 3538952 | tf_op jit(solution)/shard_map/ag_dense/ppermute | solution.py:37
  70.4 30.3 %collective-permute-start.12 = (bf16[4,32,4608]{2,1,0:T(8,128)(2,1)S(1)}, bf16[4,32,4608]{2,1,0:T(8,128)(2,1)}, u32[]{:S(2)}, u32[]{:S(2)}) collective-permute-start(bf16[4,32,4608]{2,1,0:T(8,128)(2,1)S(1)} %pad_maximum_fusion.9.refs_1_), channel_id=1, source_target_pairs={{0,48},{16,0},{32,16},{48,32},{1,49},{17,1},{33,17},{49,33},{2,50}... | collective-permute-start | bytes 3538952 | tf_op jit(solution)/shard_map/ag_dense/ppermute | solution.py:37
  102.9 17.8 %collective-permute-start.13 = (bf16[128,3200]{1,0:T(8,128)(2,1)}, bf16[128,3200]{1,0:T(8,128)(2,1)S(1)}, u32[]{:S(2)}, u32[]{:S(2)}) collective-permute-start(bf16[128,3200]{1,0:T(8,128)(2,1)} %slice_bitcast_fusion.1), channel_id=1, source_target_pairs={{0,2},{1,3},{2,4},{3,5},{4,6},{5,7},{6,0},{7,1},{8,10},{9,11},{10,... | collective-permute-start | bytes 2457608 | tf_op jit(solution)/shard_map/ag_mixer/ppermute | solution.py:33
  104.9 15.9 %collective-permute-start.14 = (bf16[128,3200]{1,0:T(8,128)(2,1)}, bf16[128,3200]{1,0:T(8,128)(2,1)S(1)}, u32[]{:S(2)}, u32[]{:S(2)}) collective-permute-start(bf16[128,3200]{1,0:T(8,128)(2,1)} %slice_bitcast_fusion), channel_id=1, source_target_pairs={{0,6},{1,7},{2,0},{3,1},{4,2},{5,3},{6,4},{7,5},{8,14},{9,15},{10,... | collective-permute-start | bytes 2457608 | tf_op jit(solution)/shard_map/ag_mixer/ppermute | solution.py:33
  130.3 34.3 %collective-permute-start.16 = (bf16[1024,2176]{1,0:T(8,128)(2,1)}, bf16[1024,2176]{1,0:T(8,128)(2,1)}, u32[]{:S(2)}, u32[]{:S(2)}) collective-permute-start(bf16[1024,2176]{1,0:T(8,128)(2,1)} %get-tuple-element.104.refs_6_.refs_10_), channel_id=1, source_target_pairs={{0,1},{1,0},{2,3},{3,2},{4,5},{5,4},{6,7},{7,6},{8,9},{9,8},{10,11... | collective-permute-start | bytes 13369352 | tf_op jit(solution)/shard_map/ag_mixer/ppermute | solution.py:24
  135.9 10.5 %collective-permute-start.15 = (bf16[2048,512]{1,0:T(8,128)(2,1)}, bf16[2048,512]{1,0:T(8,128)(2,1)}, u32[]{:S(2)}, u32[]{:S(2)}) collective-permute-start(bf16[2048,512]{1,0:T(8,128)(2,1)} %get-tuple-element.105.own), channel_id=1, source_target_pairs={{0,1},{1,0},{2,3},{3,2},{4,5},{5,4},{6,7},{7,6},{8,9},{9,8},{10,11... | collective-permute-start | bytes 6291464 | tf_op jit(solution)/shard_map/ag_mixer/ppermute | solution.py:24
  136.0 28.7 %collective-permute-start.17 = (bf16[4,32,4608]{2,1,0:T(8,128)(2,1)}, bf16[4,32,4608]{2,1,0:T(8,128)(2,1)}, u32[]{:S(2)}, u32[]{:S(2)}) collective-permute-start(bf16[4,32,4608]{2,1,0:T(8,128)(2,1)} %collective-permute-done.7.refs_2_), channel_id=1, source_target_pairs={{0,16},{16,32},{32,48},{48,0},{1,17},{17,33},{33,49},{49,1},{2,18}... | collective-permute-start | bytes 3538952 | tf_op jit(solution)/shard_map/ppermute | solution.py:37
  137.0 27.7 %collective-permute-start.18 = (bf16[4,32,4608]{2,1,0:T(8,128)(2,1)}, bf16[4,32,4608]{2,1,0:T(8,128)(2,1)}, u32[]{:S(2)}, u32[]{:S(2)}) collective-permute-start(bf16[4,32,4608]{2,1,0:T(8,128)(2,1)} %collective-permute-done.12.refs_5_), channel_id=1, source_target_pairs={{0,48},{16,0},{32,16},{48,32},{1,49},{17,1},{33,17},{49,33},{2,50}... | collective-permute-start | bytes 3538952 | tf_op jit(solution)/shard_map/ppermute | solution.py:37
  170.4 21.3 %collective-permute-start.20 = (bf16[1024,3072]{1,0:T(8,128)(2,1)S(1)}, bf16[1024,3072]{1,0:T(8,128)(2,1)}, u32[]{:S(2)}, u32[]{:S(2)}) collective-permute-start(bf16[1024,3072]{1,0:T(8,128)(2,1)S(1)} %get-tuple-element.112.refs_8_.refs_2_.refs_4_), channel_id=1, source_target_pairs={{0,1},{1,0},{2,3},{3,2},{4,5},{5,4},{6,7},{7,6},{8,9},{9,8},{10,11... | collective-permute-start | bytes 18874376 | tf_op jit(solution)/shard_map/ag_dense/ppermute | solution.py:24
  171.8 14.2 %collective-permute-start.19 = (bf16[3072,512]{1,0:T(8,128)(2,1)S(1)}, bf16[3072,512]{1,0:T(8,128)(2,1)S(1)}, u32[]{:S(2)}, u32[]{:S(2)}) collective-permute-start(bf16[3072,512]{1,0:T(8,128)(2,1)S(1)} %get-tuple-element.114.own), channel_id=1, source_target_pairs={{0,1},{1,0},{2,3},{3,2},{4,5},{5,4},{6,7},{7,6},{8,9},{9,8},{10,11... | collective-permute-start | bytes 9437192 | tf_op jit(solution)/shard_map/ag_dense/ppermute | solution.py:24
  199.3 13.1 %collective-permute-start.21 = (bf16[256,1024]{1,0:T(8,128)(2,1)}, bf16[256,1024]{1,0:T(8,128)(2,1)}, u32[]{:S(2)}, u32[]{:S(2)}) collective-permute-start(bf16[256,1024]{1,0:T(8,128)(2,1)} %convert_element_type.378), channel_id=1, source_target_pairs={{0,64},{1,65},{2,66},{3,67},{4,68},{5,69},{6,70},{7,71},{8,72},{9,... | collective-permute-start | bytes 1572872 | tf_op jit(solution)/shard_map/ppermute | solution.py:41
  251.3 79.5 %collective-permute-start.23 = (bf16[256,7168]{1,0:T(8,128)(2,1)}, bf16[256,7168]{1,0:T(8,128)(2,1)}, u32[]{:S(2)}, u32[]{:S(2)}) collective-permute-start(bf16[256,7168]{1,0:T(8,128)(2,1)} %constant_dynamic-update-slice_fusion), channel_id=1, source_target_pairs={{0,1},{1,0},{2,3},{3,2},{4,5},{5,4},{6,7},{7,6},{8,9},{9,8},{10,11... | collective-permute-start | bytes 11010056 | tf_op jit(solution)/shard_map/ppermute | solution.py:24
  290.2 15.5 %collective-permute-start.22 = (bf16[256,1024]{1,0:T(8,128)(2,1)S(1)}, bf16[256,1024]{1,0:T(8,128)(2,1)S(1)}, u32[]{:S(2)}, u32[]{:S(2)}) collective-permute-start(bf16[256,1024]{1,0:T(8,128)(2,1)S(1)} %add_convert_fusion.5), channel_id=1, source_target_pairs={{64,0},{65,1},{66,2},{67,3},{68,4},{69,5},{70,6},{71,7},{72,8},{73... | collective-permute-start | bytes 1572872 | tf_op jit(solution)/shard_map/ppermute | solution.py:41
  314.0 21.0 %collective-permute-start.24 = (bf16[256,3072]{1,0:T(8,128)(2,1)}, bf16[256,3072]{1,0:T(8,128)(2,1)}, u32[]{:S(2)}, u32[]{:S(2)}) collective-permute-start(bf16[256,3072]{1,0:T(8,128)(2,1)} %get-tuple-element.140), channel_id=1, source_target_pairs={{0,1},{1,0},{2,3},{3,2},{4,5},{5,4},{6,7},{7,6},{8,9},{9,8},{10,11... | collective-permute-start | bytes 4718600 | tf_op jit(solution)/shard_map/b2/g_gu/ppermute | solution.py:24
  316.3 25.6 %collective-permute-start.25 = (bf16[256,512]{1,0:T(8,128)(2,1)S(1)}, bf16[256,512]{1,0:T(8,128)(2,1)S(1)}, u32[]{:S(2)}, u32[]{:S(2)}) collective-permute-start(bf16[256,512]{1,0:T(8,128)(2,1)S(1)} %get-tuple-element.294), channel_id=1, source_target_pairs={{0,1},{1,0},{2,3},{3,2},{4,5},{5,4},{6,7},{7,6},{8,9},{9,8},{10,11... | collective-permute-start | bytes 786440 | tf_op jit(solution)/shard_map/b2/g_down/ppermute | solution.py:24
  352.3 22.6 %collective-permute-start.27 = (bf16[4,128,768]{2,1,0:T(8,128)(2,1)}, bf16[4,128,768]{2,1,0:T(8,128)(2,1)}, u32[]{:S(2)}, u32[]{:S(2)}) collective-permute-start(bf16[4,128,768]{2,1,0:T(8,128)(2,1)} %get-tuple-element.247), channel_id=1, source_target_pairs={{0,16},{16,32},{32,48},{48,0},{1,17},{17,33},{33,49},{49,1},{2,18}... | collective-permute-start | bytes 2359304 | tf_op jit(solution)/shard_map/b2/g_gu/ppermute | solution.py:37
  353.2 21.8 %collective-permute-start.28 = (bf16[4,128,768]{2,1,0:T(8,128)(2,1)}, bf16[4,128,768]{2,1,0:T(8,128)(2,1)}, u32[]{:S(2)}, u32[]{:S(2)}) collective-permute-start(bf16[4,128,768]{2,1,0:T(8,128)(2,1)} %get-tuple-element.248), channel_id=1, source_target_pairs={{0,48},{16,0},{32,16},{48,32},{1,49},{17,1},{33,17},{49,33},{2,50}... | collective-permute-start | bytes 2359304 | tf_op jit(solution)/shard_map/b2/g_gu/ppermute | solution.py:37
  359.6 18.1 %collective-permute-start.29 = (bf16[640,512]{1,0:T(8,128)(2,1)S(1)}, bf16[640,512]{1,0:T(8,128)(2,1)S(1)}, u32[]{:S(2)}, u32[]{:S(2)}) collective-permute-start(bf16[640,512]{1,0:T(8,128)(2,1)S(1)} %get-tuple-element.255), channel_id=1, source_target_pairs={{0,2},{1,3},{2,4},{3,5},{4,6},{5,7},{6,0},{7,1},{8,10},{9,11},{10,... | collective-permute-start | bytes 1966088 | tf_op jit(solution)/shard_map/b2/rs_do/ppermute | solution.py:33
  361.2 16.5 %collective-permute-start.30 = (bf16[640,512]{1,0:T(8,128)(2,1)S(1)}, bf16[640,512]{1,0:T(8,128)(2,1)S(1)}, u32[]{:S(2)}, u32[]{:S(2)}) collective-permute-start(bf16[640,512]{1,0:T(8,128)(2,1)S(1)} %get-tuple-element.254), channel_id=1, source_target_pairs={{0,6},{1,7},{2,0},{3,1},{4,2},{5,3},{6,4},{7,5},{8,14},{9,15},{10,... | collective-permute-start | bytes 1966088 | tf_op jit(solution)/shard_map/b2/rs_do/ppermute | solution.py:33
  377.7 28.8 %collective-permute-start.31 = (bf16[256,2048]{1,0:T(8,128)(2,1)}, bf16[256,2048]{1,0:T(8,128)(2,1)}, u32[]{:S(2)}, u32[]{:S(2)}) collective-permute-start(bf16[256,2048]{1,0:T(8,128)(2,1)} %get-tuple-element.158), channel_id=1, source_target_pairs={{0,1},{1,0},{2,3},{3,2},{4,5},{5,4},{6,7},{7,6},{8,9},{9,8},{10,11... | collective-permute-start | bytes 3145736 | tf_op jit(solution)/shard_map/b2/g_qkv/ppermute | solution.py:24
  386.4 32.1 %collective-permute-start.42 = (bf16[2,640,512]{2,1,0:T(8,128)(2,1)}, bf16[2,640,512]{2,1,0:T(8,128)(2,1)}, u32[]{:S(2)}, u32[]{:S(2)}) collective-permute-start(bf16[2,640,512]{2,1,0:T(8,128)(2,1)} %pad_maximum_fusion.6), channel_id=1, source_target_pairs={{0,2},{1,3},{2,4},{3,5},{4,6},{5,7},{6,0},{7,1},{8,10},{9,11},{10,... | collective-permute-start | bytes 3932168 | tf_op jit(solution)/shard_map/b2/rs_do/ppermute | solution.py:33
  387.6 32.7 %collective-permute-start.43 = (bf16[2,640,512]{2,1,0:T(8,128)(2,1)}, bf16[2,640,512]{2,1,0:T(8,128)(2,1)}, u32[]{:S(2)}, u32[]{:S(2)}) collective-permute-start(bf16[2,640,512]{2,1,0:T(8,128)(2,1)} %pad_maximum_fusion.7), channel_id=1, source_target_pairs={{0,6},{1,7},{2,0},{3,1},{4,2},{5,3},{6,4},{7,5},{8,14},{9,15},{10,... | collective-permute-start | bytes 3932168 | tf_op jit(solution)/shard_map/b2/rs_do/ppermute | solution.py:33
  389.2 46.7 %collective-permute-start.33 = (bf16[8,128,768]{2,1,0:T(8,128)(2,1)}, bf16[8,128,768]{2,1,0:T(8,128)(2,1)}, u32[]{:S(2)}, u32[]{:S(2)}) collective-permute-start(bf16[8,128,768]{2,1,0:T(8,128)(2,1)} %pad_maximum_fusion.5), channel_id=1, source_target_pairs={{0,48},{16,0},{32,16},{48,32},{1,49},{17,1},{33,17},{49,33},{2,50}... | collective-permute-start | bytes 4718600 | tf_op jit(solution)/shard_map/b2/rs_gu/ppermute | solution.py:37
  390.6 45.3 %collective-permute-start.32 = (bf16[8,128,768]{2,1,0:T(8,128)(2,1)}, bf16[8,128,768]{2,1,0:T(8,128)(2,1)}, u32[]{:S(2)}, u32[]{:S(2)}) collective-permute-start(bf16[8,128,768]{2,1,0:T(8,128)(2,1)} %pad_maximum_fusion.4), channel_id=1, source_target_pairs={{0,16},{16,32},{32,48},{48,0},{1,17},{17,33},{33,49},{49,1},{2,18}... | collective-permute-start | bytes 4718600 | tf_op jit(solution)/shard_map/b2/rs_gu/ppermute | solution.py:37
  413.4 16.3 %collective-permute-start.40 = (bf16[128,2048]{1,0:T(8,128)(2,1)}, bf16[128,2048]{1,0:T(8,128)(2,1)S(1)}, u32[]{:S(2)}, u32[]{:S(2)}) collective-permute-start(bf16[128,2048]{1,0:T(8,128)(2,1)} %get-tuple-element.261), channel_id=1, source_target_pairs={{0,2},{1,3},{2,4},{3,5},{4,6},{5,7},{6,0},{7,1},{8,10},{9,11},{10,... | collective-permute-start | bytes 1572872 | tf_op jit(solution)/shard_map/b2/rs_q/ppermute | solution.py:33
  418.5 12.5 %collective-permute-start.41 = (bf16[128,2048]{1,0:T(8,128)(2,1)S(1)}, bf16[128,2048]{1,0:T(8,128)(2,1)}, u32[]{:S(2)}, u32[]{:S(2)}) collective-permute-start(bf16[128,2048]{1,0:T(8,128)(2,1)S(1)} %get-tuple-element.260), channel_id=1, source_target_pairs={{0,6},{1,7},{2,0},{3,1},{4,2},{5,3},{6,4},{7,5},{8,14},{9,15},{10,... | collective-permute-start | bytes 1572872 | tf_op jit(solution)/shard_map/b2/rs_q/ppermute | solution.py:33
  433.0 28.2 %collective-permute-start.44 = (bf16[2,128,2048]{2,1,0:T(8,128)(2,1)S(1)}, bf16[2,128,2048]{2,1,0:T(8,128)(2,1)S(1)}, u32[]{:S(2)}, u32[]{:S(2)}) collective-permute-start(bf16[2,128,2048]{2,1,0:T(8,128)(2,1)S(1)} %pad_maximum_fusion.10), channel_id=1, source_target_pairs={{0,2},{1,3},{2,4},{3,5},{4,6},{5,7},{6,0},{7,1},{8,10},{9,11},{10,... | collective-permute-start | bytes 3145736 | tf_op jit(solution)/shard_map/b2/rs_q/ppermute | solution.py:33
  433.2 28.0 %collective-permute-start.45 = (bf16[2,128,2048]{2,1,0:T(8,128)(2,1)S(1)}, bf16[2,128,2048]{2,1,0:T(8,128)(2,1)S(1)}, u32[]{:S(2)}, u32[]{:S(2)}) collective-permute-start(bf16[2,128,2048]{2,1,0:T(8,128)(2,1)S(1)} %pad_maximum_fusion.11), channel_id=1, source_target_pairs={{0,6},{1,7},{2,0},{3,1},{4,2},{5,3},{6,4},{7,5},{8,14},{9,15},{10,... | collective-permute-start | bytes 3145736 | tf_op jit(solution)/shard_map/b2/rs_q/ppermute | solution.py:33
  443.4 17.8 %collective-permute-start.46 = (bf16[128,768]{1,0:T(8,128)(2,1)S(1)}, bf16[128,768]{1,0:T(8,128)(2,1)S(1)}, u32[]{:S(2)}, u32[]{:S(2)}) collective-permute-start(bf16[128,768]{1,0:T(8,128)(2,1)S(1)} %get-tuple-element.282), channel_id=1, source_target_pairs={{0,2},{1,3},{2,4},{3,5},{4,6},{5,7},{6,0},{7,1},{8,10},{9,11},{10,... | collective-permute-start | bytes 589832 | tf_op jit(solution)/shard_map/b2/rs_gu/ppermute | solution.py:33
  443.5 17.7 %collective-permute-start.47 = (bf16[128,768]{1,0:T(8,128)(2,1)S(1)}, bf16[128,768]{1,0:T(8,128)(2,1)S(1)}, u32[]{:S(2)}, u32[]{:S(2)}) collective-permute-start(bf16[128,768]{1,0:T(8,128)(2,1)S(1)} %get-tuple-element.281), channel_id=1, source_target_pairs={{0,6},{1,7},{2,0},{3,1},{4,2},{5,3},{6,4},{7,5},{8,14},{9,15},{10,... | collective-permute-start | bytes 589832 | tf_op jit(solution)/shard_map/b2/rs_gu/ppermute | solution.py:33
  456.9 17.5 %collective-permute-start.51 = (bf16[640,512]{1,0:T(8,128)(2,1)S(1)}, bf16[640,512]{1,0:T(8,128)(2,1)S(1)}, u32[]{:S(2)}, u32[]{:S(2)}) collective-permute-start(bf16[640,512]{1,0:T(8,128)(2,1)S(1)} %fusion.12), channel_id=1, source_target_pairs={{0,8},{1,9},{2,10},{3,11},{4,12},{5,13},{6,14},{7,15},{8,0},{9,1},... | collective-permute-start | bytes 1966088 | tf_op jit(solution)/shard_map/b2/rs_do/ppermute | solution.py:28
  461.1 9.6 %collective-permute-start.38 = (f32[18,128]{1,0:T(8,128)S(1)}, f32[18,128]{1,0:T(8,128)S(1)}, u32[]{:S(2)}, u32[]{:S(2)}) collective-permute-start(f32[18,128]{1,0:T(8,128)S(1)} %add.1485), channel_id=1, source_target_pairs={{0,2},{1,3},{2,0},{3,1},{4,6},{5,7},{6,4},{7,5},{8,10},{9,11},{10,... | collective-permute-start | bytes 27656 | tf_op jit(solution)/shard_map/ppermute | solution.py:52
  462.9 22.7 %collective-permute-start.48 = (bf16[128,2048]{1,0:T(8,128)(2,1)S(1)}, bf16[128,2048]{1,0:T(8,128)(2,1)S(1)}, u32[]{:S(2)}, u32[]{:S(2)}) collective-permute-start(bf16[128,2048]{1,0:T(8,128)(2,1)S(1)} %get-tuple-element.244), channel_id=1, source_target_pairs={{0,8},{1,9},{2,10},{3,11},{4,12},{5,13},{6,14},{7,15},{8,0},{9,1},... | collective-permute-start | bytes 1572872 | tf_op jit(solution)/shard_map/rs_q/ppermute | solution.py:28
  466.5 9.7 %collective-permute-start.49 = (bf16[2,128,768]{2,1,0:T(8,128)(2,1)S(1)}, bf16[2,128,768]{2,1,0:T(8,128)(2,1)S(1)}, u32[]{:S(2)}, u32[]{:S(2)}) collective-permute-start(bf16[2,128,768]{2,1,0:T(8,128)(2,1)S(1)} %pad_maximum_fusion.16), channel_id=1, source_target_pairs={{0,2},{1,3},{2,4},{3,5},{4,6},{5,7},{6,0},{7,1},{8,10},{9,11},{10,... | collective-permute-start | bytes 1179656 | tf_op jit(solution)/shard_map/rs_gu/ppermute | solution.py:33
  468.1 8.2 %collective-permute-start.50 = (bf16[2,128,768]{2,1,0:T(8,128)(2,1)S(1)}, bf16[2,128,768]{2,1,0:T(8,128)(2,1)S(1)}, u32[]{:S(2)}, u32[]{:S(2)}) collective-permute-start(bf16[2,128,768]{2,1,0:T(8,128)(2,1)S(1)} %pad_maximum_fusion.17), channel_id=1, source_target_pairs={{0,6},{1,7},{2,0},{3,1},{4,2},{5,3},{6,4},{7,5},{8,14},{9,15},{10,... | collective-permute-start | bytes 1179656 | tf_op jit(solution)/shard_map/rs_gu/ppermute | solution.py:33
  470.7 32.0 %collective-permute-start.39 = (f32[18,128]{1,0:T(8,128)S(1)}, f32[18,128]{1,0:T(8,128)S(1)}, u32[]{:S(2)}, u32[]{:S(2)}) collective-permute-start(f32[18,128]{1,0:T(8,128)S(1)} %add.1486), channel_id=1, source_target_pairs={{0,4},{1,5},{2,6},{3,7},{4,0},{5,1},{6,2},{7,3},{8,12},{9,13},{10,... | collective-permute-start | bytes 27656 | tf_op jit(solution)/shard_map/ppermute | solution.py:52
  501.2 8.5 %collective-permute-start.57 = (bf16[480,512]{1,0:T(8,128)(2,1)S(1)}, bf16[480,512]{1,0:T(8,128)(2,1)S(1)}, u32[]{:S(2)}, u32[]{:S(2)}) collective-permute-start(bf16[480,512]{1,0:T(8,128)(2,1)S(1)} %slice_dynamic-update-slice_fusion), channel_id=1, source_target_pairs={{0,48},{16,0},{32,16},{48,32},{1,49},{17,1},{33,17},{49,33},{2,50}... | collective-permute-start | bytes 1474568 | tf_op jit(solution)/shard_map/fin/ppermute | solution.py:37
  501.3 10.0 %collective-permute-start.58 = (bf16[480,512]{1,0:T(8,128)(2,1)S(1)}, bf16[480,512]{1,0:T(8,128)(2,1)S(1)}, u32[]{:S(2)}, u32[]{:S(2)}) collective-permute-start(bf16[480,512]{1,0:T(8,128)(2,1)S(1)} %slice_dynamic-update-slice_fusion), channel_id=1, source_target_pairs={{0,16},{16,32},{32,48},{48,0},{1,17},{17,33},{33,49},{49,1},{2,18}... | collective-permute-start | bytes 1474568 | tf_op jit(solution)/shard_map/fin/ppermute | solution.py:37
  524.0 8.6 %collective-permute-start.61 = (bf16[960,512]{1,0:T(8,128)(2,1)S(1)}, bf16[960,512]{1,0:T(8,128)(2,1)S(1)}, u32[]{:S(2)}, u32[]{:S(2)}) collective-permute-start(bf16[960,512]{1,0:T(8,128)(2,1)S(1)} %dynamic-slice_dynamic-update-slice_fusion.7), channel_id=1, source_target_pairs={{0,1},{1,0},{2,3},{3,2},{4,5},{5,4},{6,7},{7,6},{8,9},{9,8},{10,11... | collective-permute-start | bytes 2949128 | tf_op jit(solution)/shard_map/fin/ppermute | solution.py:24
  (97 other events, 641.2 us)

commit v5 on v4

--- a/solution.py
+++ b/solution.py
@@ -653,13 +653,14 @@
         m_z = swap_z(m_0)
         d_near, m_z = tied(d_near, m_z)
         d_far = far_y(*d_near)
+        m_pair = jnp.stack([m_0, m_z])
+        d_far, m_pair = tied(d_far, m_pair)
         d_all = (jnp.concatenate([d_pair, d_near[0]]), jnp.concatenate([d_near[1], *d_far]))
         d_x = near_x(*d_all)
     with jax.named_scope("ag_mixer"):
-        m_pair = jnp.stack([m_0, m_z])
         m_near = near_y(m_pair)
-        m_near, d_x = tied(m_near, d_x)
         m_far = far_y(*m_near)
+        m_far, d_x = tied(m_far, d_x)
         moves, offsets = [], []
         spots = [(0, 0), (0, 1), (1, 0), (1, 1), (2, 0), (2, 1), (3, 0), (4, 0)]
         for (piece, index), (dz, dy) in zip(spots, origins):

time: 548 us -> 539 us (0.984)
    ppermute x18, waiting for transfers between devices: 65.9 us -> 44.5 us  [move_x(): return lax.ppermute(value, 'dp', [(i, (i + step) % 4) for i in range(4)])]
    ppermute x20, waiting for transfers between devices: 35.8 us -> 53.9 us  [move_y(): return lax.ppermute(value, 'fsdp', pairs)]
    unnamed x208 -> x194, local copies, waits for them, and re-layouts: 53.9 us -> 50.2 us
  transfers between devices with their start and end apart: 62 -> 62, of which waited for: 32 -> 27; matrix products, arithmetic and copies ran while one was open for 10% -> 10% of each run, Pallas kernels for 17% -> 17%
where the time goes in v5:
time: 539 us; the launch traced here: 530 us
  waiting for transfers between devices  176 us (33%)
  Pallas kernels  135 us (25%)
  starting transfers between devices  92.4 us (17%)
  local copies, waits for them, and re-layouts  71.6 us (13%)
  other arithmetic  38.8 us (7%)
  matrix products  14.1 us (3%)
    pallas_call x16, Pallas kernels, call(): pl.pallas_call(body, grid=(steps,), in_specs=specs, out_specs=[p[0] for p...  120 us
    ppermute x20, waiting for transfers between devices, move_y(): return lax.ppermute(value, 'fsdp', pairs)  53.9 us
    unnamed x194, local copies, waits for them, and re-layouts  50.2 us
    ppermute x18, waiting for transfers between devices, move_x(): return lax.ppermute(value, 'dp', [(i, (i + step) % 4) for i in range(4)])  44.5 us
    ppermute x5, waiting for transfers between devices, swap_z(): return lax.ppermute(value, 'fsdp', [(i, i ^ 8) for i in range(16)])  34.1 us
    ppermute x20, starting transfers between devices, move_y(): return lax.ppermute(value, 'fsdp', pairs)  25.8 us
    ppermute x2, waiting for transfers between devices, move_section(): return lax.ppermute(value, 'section', [(0, 1)] if step > 0 else [(1, 0)])  24.6 us
    ppermute x18, starting transfers between devices, move_x(): return lax.ppermute(value, 'dp', [(i, (i + step) % 4) for i in range(4)])  19.6 us
  transfers between devices with their start and end apart: 62, of which 27 were waited for; matrix products, arithmetic and copies ran while one was open for 10% of the time, Pallas kernels for 17%

profile of v5, /device:TPU:1, one launch (start us, length us, event | category | flops | bytes accessed | tf_op | source)
XLA Modules:
  0.0 530.2 jit_solution(14026535516492914726)
XLA Ops:
  13.8 3.8 collective-permute-start.1
  17.8 6.9 %collective-permute-done.1 = bf16[32,4608]{1,0:T(8,128)(2,1)S(1)} collective-permute-done((bf16[32,4608]{1,0:T(8,128)(2,1)S(1)}, bf16[32,4608]{1,0:T(8,128)(2,1)S(1)}, u32[]{:S(2)}, u32[]{:S(2)}) %collective-permute-start.1) | collective-permute-done | bytes 294944 | tf_op jit(solution)/shard_map/ag_dense/ppermute | solution.py:28
  27.6 14.6 %collective-permute-done.4 = bf16[128,3200]{1,0:T(8,128)(2,1)S(1)} collective-permute-done((bf16[128,3200]{1,0:T(8,128)(2,1)S(1)}, bf16[128,3200]{1,0:T(8,128)(2,1)S(1)}, u32[]{:S(2)}, u32[]{:S(2)}) %collective-permute-start.4) | collective-permute-done | bytes 819232 | tf_op jit(solution)/shard_map/ag_dense/ppermute | solution.py:28
  48.2 5.5 %collective-permute-done.5 = bf16[32,4608]{1,0:T(8,128)(2,1)S(1)} collective-permute-done((bf16[32,4608]{1,0:T(8,128)(2,1)S(1)}, bf16[32,4608]{1,0:T(8,128)(2,1)S(1)}, u32[]{:S(2)}, u32[]{:S(2)}) %collective-permute-start.5) | collective-permute-done | bytes 294944 | tf_op jit(solution)/shard_map/ag_dense/ppermute | solution.py:33
  58.7 31.3 %collective-permute-done.7.refs_1_ = bf16[2,128,3200]{2,1,0:T(8,128)(2,1)S(1)} collective-permute-done((bf16[2,128,3200]{2,1,0:T(8,128)(2,1)S(1)}, bf16[2,128,3200]{2,1,0:T(8,128)(2,1)S(1)}, u32[]{:S(2)}, u32[]{:S(2)}) %collective-permute-start.7) | collective-permute-done | bytes 1638432 | tf_op jit(solution)/shard_map/ag_mixer/ppermute | solution.py:33
  95.9 18.7 %collective-permute-done.14.refs_5_ = bf16[4,32,4608]{2,1,0:T(8,128)(2,1)} collective-permute-done((bf16[4,32,4608]{2,1,0:T(8,128)(2,1)}, bf16[4,32,4608]{2,1,0:T(8,128)(2,1)}, u32[]{:S(2)}, u32[]{:S(2)}) %collective-permute-start.14) | collective-permute-done | bytes 1179680 | tf_op jit(solution)/shard_map/ag_dense/ppermute | solution.py:37
  117.5 5.6 %ag_mixer.2 = (bf16[1024,2176]{1,0:T(8,128)(2,1)}, bf16[2048,512]{1,0:T(8,128)(2,1)}) custom-call(s32[40]{0:T(128)S(1)} %stack.632.offsets, bf16[2,128,3200]{2,1,0:T(8,128)(2,1)S(1)} %pad_maximum_fusion.3.refs_0_, bf16[2,128,3200]{2,1,0:T(8,128)(2,1)S(1)} %copy-done.30, bf16[2,128,3200]{2,1,0:T(8,128)(2,1)S(1)} %copy-done.32, ...), custom_call_target="tpu_custom_call" | custom-call | flops 1048576 | bytes 65536 | tf_op jit(solution)/shard_map/ag_mixer/pallas_call | solution.py:87
  123.0 4.1 collective-permute-start.16
  127.3 2.9 collective-permute-start.18
  133.3 4.4 collective-permute-done.15.other
  139.9 8.5 %f1.5 = (f32[256,1024]{1,0:T(8,128)S(1)}, bf16[256,1024]{1,0:T(8,128)(2,1)S(1)}, f32[256,2048]{1,0:T(8,128)}, bf16[256,1024]{1,0:T(8,128)(2,1)}) custom-call(f32[256,1024]{1,0:T(8,128)S(1)} %bitcast_convert_fusion.refs_0_, f32[1,1024]{1,0:T(1,128)S(1)} %bitcast.418, f32[1,128]{1,0:T(1,128)S(1)} %broadcast_in_dim_reshape.4.refs_2_.refs_3_.refs_6_, ...), custom_call_target="tpu_custom_call" | custom-call | flops 1048576 | bytes 65536 | tf_op jit(solution)/shard_map/f1/pallas_call | solution.py:414
  148.4 7.4 %collective-permute-done.17.refs_6_ = bf16[4,32,4608]{2,1,0:T(8,128)(2,1)S(1)} collective-permute-done((bf16[4,32,4608]{2,1,0:T(8,128)(2,1)}, bf16[4,32,4608]{2,1,0:T(8,128)(2,1)S(1)}, u32[]{:S(2)}, u32[]{:S(2)}) %collective-permute-start.17) | collective-permute-done | bytes 1179680 | tf_op jit(solution)/shard_map/ppermute | solution.py:37
  155.8 5.4 %f1.6 = (bf16[1024,3072]{1,0:T(8,128)(2,1)S(1)}, bf16[3072,512]{1,0:T(8,128)(2,1)S(1)}) custom-call(s32[128]{0:T(128)S(1)} %stack.770.offsets, bf16[4,32,4608]{2,1,0:T(8,128)(2,1)S(1)} %copy-done.26, bf16[4,32,4608]{2,1,0:T(8,128)(2,1)} %constant_dynamic-update-slice_fusion.refs_1_, bf16[4,32,4608]{2,1,0:T(8,128)(2,1)} %collective-permute-done.11.refs_2_, ...), custom_call_target="tpu_custom_call" | custom-call | flops 1048576 | bytes 65536 | tf_op jit(solution)/shard_map/f1/pallas_call | solution.py:87
  162.7 8.1 %f1.7 = (f32[256,1024]{1,0:T(8,128)S(1)}, f32[256,2048]{1,0:T(8,128)}, bf16[256,1024]{1,0:T(8,128)(2,1)}) custom-call(f32[256,1024]{1,0:T(8,128)S(1)} %get-tuple-element.112.refs_8_.refs_0_, bf16[256,1024]{1,0:T(8,128)(2,1)S(1)} %get-tuple-element.113.refs_1_, f32[1,128]{1,0:T(1,128)S(1)} %broadcast_in_dim_reshape.4.refs_2_.refs_3_.refs_6_, ...), custom_call_target="tpu_custom_call" | custom-call | flops 1048576 | bytes 65536 | tf_op jit(solution)/shard_map/f1/pallas_call | solution.py:414
  170.8 5.9 %collective-permute-done.19.other = bf16[3072,512]{1,0:T(8,128)(2,1)S(1)} collective-permute-done((bf16[3072,512]{1,0:T(8,128)(2,1)S(1)}, bf16[3072,512]{1,0:T(8,128)(2,1)S(1)}, u32[]{:S(2)}, u32[]{:S(2)}) %collective-permute-start.19) | collective-permute-done | bytes 3145760 | tf_op jit(solution)/shard_map/ag_dense/ppermute | solution.py:24
  177.6 4.9 f1.8
  182.5 6.7 %f1.9 = (f32[256,1024]{1,0:T(8,128)S(1)}, f32[256,3072]{1,0:T(8,128)}, bf16[256,1536]{1,0:T(8,128)(2,1)}) custom-call(f32[256,1024]{1,0:T(8,128)S(1)} %get-tuple-element.121.refs_0_, bf16[256,1024]{1,0:T(8,128)(2,1)S(1)} %get-tuple-element.122.refs_1_, bf16[1024,3072]{1,0:T(8,128)(2,1)} %collective-permute-done.20.refs_2_.refs_3_, ...), custom_call_target="tpu_custom_call" | custom-call | flops 1048576 | bytes 65536 | tf_op jit(solution)/shard_map/f1/pallas_call | solution.py:414
  192.8 10.7 %collective-permute-done.21 = bf16[256,1024]{1,0:T(8,128)(2,1)} collective-permute-done((bf16[256,1024]{1,0:T(8,128)(2,1)}, bf16[256,1024]{1,0:T(8,128)(2,1)}, u32[]{:S(2)}, u32[]{:S(2)}) %collective-permute-start.21) | collective-permute-done | bytes 524320 | tf_op jit(solution)/shard_map/ppermute | solution.py:41
  207.4 7.5 %f2.4 = (f32[256,1024]{1,0:T(8,128)S(1)}, bf16[256,1024]{1,0:T(8,128)(2,1)S(1)}, f32[256,2048]{1,0:T(8,128)S(1)}, bf16[256,1024]{1,0:T(8,128)(2,1)S(1)}) custom-call(f32[256,1024]{1,0:T(8,128)S(1)} %get-tuple-element.249.refs_0_, f32[1,1024]{1,0:T(1,128)S(1)} %bitcast.419, f32[1,128]{1,0:T(1,128)S(1)} %broadcast_in_dim_reshape.4.refs_2_.refs_3_.refs_6_, ...), custom_call_target="tpu_custom_call" | custom-call | flops 1048576 | bytes 65536 | tf_op jit(solution)/shard_map/f2/pallas_call | solution.py:414
  216.2 7.6 %f2.5 = (f32[256,1024]{1,0:T(8,128)S(1)}, f32[256,2048]{1,0:T(8,128)S(1)}, bf16[256,1024]{1,0:T(8,128)(2,1)S(1)}) custom-call(f32[256,1024]{1,0:T(8,128)S(1)} %get-tuple-element.124.refs_0_, bf16[256,1024]{1,0:T(8,128)(2,1)S(1)} %get-tuple-element.125.refs_1_, f32[1,128]{1,0:T(1,128)S(1)} %broadcast_in_dim_reshape.4.refs_2_.refs_3_.refs_6_, ...), custom_call_target="tpu_custom_call" | custom-call | flops 1048576 | bytes 65536 | tf_op jit(solution)/shard_map/f2/pallas_call | solution.py:414
  225.3 4.2 f2.6
  231.6 6.1 %f2.7 = (f32[256,1024]{1,0:T(8,128)S(1)}, f32[256,3072]{1,0:T(8,128)S(1)}, bf16[256,1536]{1,0:T(8,128)(2,1)S(1)}) custom-call(f32[256,1024]{1,0:T(8,128)S(1)} %get-tuple-element.127.refs_0_, bf16[256,1024]{1,0:T(8,128)(2,1)S(1)} %get-tuple-element.128.refs_1_, bf16[1024,3072]{1,0:T(8,128)(2,1)} %collective-permute-done.20.refs_2_.refs_3_, ...), custom_call_target="tpu_custom_call" | custom-call | flops 1048576 | bytes 65536 | tf_op jit(solution)/shard_map/f2/pallas_call | solution.py:414
  243.7 6.1 %b1.4 = (bf16[256,3072]{1,0:T(8,128)(2,1)}, f32[256,1024]{1,0:T(8,128)S(1)}) custom-call(bf16[256,1024]{1,0:T(8,128)(2,1)S(1)} %bitcast.409, bf16[3072,1024]{1,0:T(8,128)(2,1)S(1)} %bitcast.406, f32[256,3072]{1,0:T(8,128)S(1)} %copy-done.17, bf16[1024,3072]{1,0:T(8,128)(2,1)} %collective-permute-done.20.refs_2_.refs_3_), custom_call_target="tpu_custom_call" | custom-call | flops 1048576 | bytes 65536 | tf_op jit(solution)/shard_map/b1/pallas_call | solution.py:414
  249.8 5.0 b1.5
  256.8 11.4 %b1.6 = (bf16[256,2048]{1,0:T(8,128)(2,1)}, f32[256,1024]{1,0:T(8,128)S(1)}, f32[1,128]{1,0:T(1,128)S(1)}, f32[1,128]{1,0:T(1,128)S(1)}) custom-call(bf16[256,1024]{1,0:T(8,128)(2,1)S(1)} %fusion.68.refs_0_.refs_3_, bf16[2048,1024]{1,0:T(8,128)(2,1)S(1)} %copy-done.4, f32[256,2048]{1,0:T(8,128)S(1)} %copy-done.23, ...), custom_call_target="tpu_custom_call" | custom-call | flops 1048576 | bytes 65536 | tf_op jit(solution)/shard_map/b1/pallas_call | solution.py:414
  268.2 11.3 %b1.7 = (bf16[256,2048]{1,0:T(8,128)(2,1)}, f32[256,1024]{1,0:T(8,128)S(1)}, f32[1,128]{1,0:T(1,128)}, f32[1,128]{1,0:T(1,128)}) custom-call(f32[256,1024]{1,0:T(8,128)S(1)} %get-tuple-element.134.refs_0_, f32[1,128]{1,0:T(1,128)S(1)} %get-tuple-element.135.refs_1_, f32[1,128]{1,0:T(1,128)S(1)} %get-tuple-element.136.refs_2_, ...), custom_call_target="tpu_custom_call" | custom-call | flops 1048576 | bytes 65536 | tf_op jit(solution)/shard_map/b1/pallas_call | solution.py:414
  282.8 13.9 %collective-permute-done.22 = bf16[256,1024]{1,0:T(8,128)(2,1)S(1)} collective-permute-done((bf16[256,1024]{1,0:T(8,128)(2,1)S(1)}, bf16[256,1024]{1,0:T(8,128)(2,1)S(1)}, u32[]{:S(2)}, u32[]{:S(2)}) %collective-permute-start.22) | collective-permute-done | bytes 524320 | tf_op jit(solution)/shard_map/ppermute | solution.py:41
  297.9 6.2 %b2.4 = (bf16[256,3072]{1,0:T(8,128)(2,1)}, f32[256,1024]{1,0:T(8,128)S(1)}) custom-call(bf16[256,1024]{1,0:T(8,128)(2,1)S(1)} %get-tuple-element.246.refs_0_.refs_1_, bf16[3072,1024]{1,0:T(8,128)(2,1)S(1)} %bitcast.406, f32[256,3072]{1,0:T(8,128)S(1)} %copy-done.18, bf16[1024,3072]{1,0:T(8,128)(2,1)} %collective-permute-done.20.refs_2_.refs_3_), custom_call_target="tpu_custom_call" | custom-call | flops 1048576 | bytes 65536 | tf_op jit(solution)/shard_map/b2/pallas_call | solution.py:414
  310.5 2.8 copy-done.8
  317.5 4.4 b2.5
  326.2 6.9 %convolution_convert_fusion = bf16[1024,3072]{1,0:T(8,128)(2,1)} fusion(bf16[256,3072]{1,0:T(8,128)(2,1)} %collective-permute-done.24, bf16[256,3072]{1,0:T(8,128)(2,1)S(1)} %get-tuple-element.145, bf16[256,1024]{1,0:T(8,128)(2,1)S(1)} %get-tuple-element.278, bf16[256,1024]{1,0:T(8,128)(2,1)S(1)} %copy-done.34), kind=kOutput, calls=%fused_computation | convolution fusion | flops 3232759808 | bytes 10485760 | tf_op jit(solution)/shard_map/b2/g_gu/dot_general | solution.py:610
  340.2 3.3 constant_dynamic-slice_fusion.5
  355.0 11.2 %b2.6 = (bf16[256,2048]{1,0:T(8,128)(2,1)}, f32[256,1024]{1,0:T(8,128)S(1)}, f32[1,128]{1,0:T(1,128)S(1)}, f32[1,128]{1,0:T(1,128)S(1)}) custom-call(bf16[256,1024]{1,0:T(8,128)(2,1)S(1)} %get-tuple-element.161.refs_0_.refs_3_, bf16[2048,1024]{1,0:T(8,128)(2,1)S(1)} %copy-done.5, f32[256,2048]{1,0:T(8,128)S(1)} %copy-done.24, ...), custom_call_target="tpu_custom_call" | custom-call | flops 1048576 | bytes 65536 | tf_op jit(solution)/shard_map/b2/pallas_call | solution.py:414
  386.2 10.9 %b2.7 = (bf16[256,2048]{1,0:T(8,128)(2,1)S(1)}, f32[256,1024]{1,0:T(8,128)S(1)}, f32[1,128]{1,0:T(1,128)S(1)}, f32[1,128]{1,0:T(1,128)S(1)}) custom-call(f32[256,1024]{1,0:T(8,128)S(1)} %copy-done.38, f32[1,128]{1,0:T(1,128)S(1)} %get-tuple-element.152.refs_1_, f32[1,128]{1,0:T(1,128)S(1)} %get-tuple-element.153.refs_2_, ...), custom_call_target="tpu_custom_call" | custom-call | flops 1048576 | bytes 65536 | tf_op jit(solution)/shard_map/b2/pallas_call | solution.py:414
  397.2 3.6 convolution_convert_fusion.1
  403.9 5.1 collective-permute-done.42
  410.9 9.2 %collective-permute-done.40 = bf16[128,2048]{1,0:T(8,128)(2,1)S(1)} collective-permute-done((bf16[128,2048]{1,0:T(8,128)(2,1)}, bf16[128,2048]{1,0:T(8,128)(2,1)S(1)}, u32[]{:S(2)}, u32[]{:S(2)}) %collective-permute-start.40) | collective-permute-done | bytes 524320 | tf_op jit(solution)/shard_map/b2/rs_q/ppermute | solution.py:33
  426.2 3.0 add_convert_fusion
  429.3 2.8 collective-permute-done.34
  436.5 4.6 collective-permute-start.36
  442.9 3.5 collective-permute-start.37
  447.4 3.3 collective-permute-start.51
  453.1 3.5 collective-permute-start.48
  466.8 9.3 %collective-permute-done.48 = bf16[128,2048]{1,0:T(8,128)(2,1)S(1)} collective-permute-done((bf16[128,2048]{1,0:T(8,128)(2,1)S(1)}, bf16[128,2048]{1,0:T(8,128)(2,1)S(1)}, u32[]{:S(2)}, u32[]{:S(2)}) %collective-permute-start.48) | collective-permute-done | bytes 524320 | tf_op jit(solution)/shard_map/rs_q/ppermute | solution.py:28
  488.3 3.2 collective-permute-done.53
  494.5 5.7 %collective-permute-done.57 = bf16[480,512]{1,0:T(8,128)(2,1)S(1)} collective-permute-done((bf16[480,512]{1,0:T(8,128)(2,1)S(1)}, bf16[480,512]{1,0:T(8,128)(2,1)S(1)}, u32[]{:S(2)}, u32[]{:S(2)}) %collective-permute-start.57) | collective-permute-done | bytes 491552 | tf_op jit(solution)/shard_map/fin/ppermute | solution.py:37
  501.9 5.5 %collective-permute-done.60 = bf16[240,512]{1,0:T(8,128)(2,1)S(1)} collective-permute-done((bf16[240,512]{1,0:T(8,128)(2,1)S(1)}, bf16[240,512]{1,0:T(8,128)(2,1)S(1)}, u32[]{:S(2)}, u32[]{:S(2)}) %collective-permute-start.60) | collective-permute-done | bytes 245792 | tf_op jit(solution)/shard_map/fin/ppermute | solution.py:37
  514.5 6.4 %collective-permute-start.61 = (bf16[960,512]{1,0:T(8,128)(2,1)S(1)}, bf16[960,512]{1,0:T(8,128)(2,1)S(1)}, u32[]{:S(2)}, u32[]{:S(2)}) collective-permute-start(bf16[960,512]{1,0:T(8,128)(2,1)S(1)} %dynamic-slice_dynamic-update-slice_fusion.7), channel_id=1, source_target_pairs={{0,1},{1,0},{2,3},{3,2},{4,5},{5,4},{6,7},{7,6},{8,9},{9,8},{10,11... | collective-permute-start | bytes 2949128 | tf_op jit(solution)/shard_map/fin/ppermute | solution.py:24
  (434 shorter events, 184.7 us)
Async XLA Ops:
  13.8 10.8 %collective-permute-start.1 = (bf16[32,4608]{1,0:T(8,128)(2,1)S(1)}, bf16[32,4608]{1,0:T(8,128)(2,1)S(1)}, u32[]{:S(2)}, u32[]{:S(2)}) collective-permute-start(bf16[32,4608]{1,0:T(8,128)(2,1)S(1)} %fusion.44), channel_id=1, source_target_pairs={{0,8},{1,9},{2,10},{3,11},{4,12},{5,13},{6,14},{7,15},{8,0},{9,1},... | collective-permute-start | bytes 884744 | tf_op jit(solution)/shard_map/ag_dense/ppermute | solution.py:28
  17.7 24.6 %collective-permute-start.4 = (bf16[128,3200]{1,0:T(8,128)(2,1)S(1)}, bf16[128,3200]{1,0:T(8,128)(2,1)S(1)}, u32[]{:S(2)}, u32[]{:S(2)}) collective-permute-start(bf16[128,3200]{1,0:T(8,128)(2,1)S(1)} %pad_maximum_fusion.11), channel_id=1, source_target_pairs={{0,8},{1,9},{2,10},{3,11},{4,12},{5,13},{6,14},{7,15},{8,0},{9,1},... | collective-permute-start | bytes 2457608 | tf_op jit(solution)/shard_map/ag_dense/ppermute | solution.py:28
  24.7 17.5 %collective-permute-start.2 = (bf16[2,32,4608]{2,1,0:T(8,128)(2,1)S(1)}, bf16[2,32,4608]{2,1,0:T(8,128)(2,1)S(1)}, u32[]{:S(2)}, u32[]{:S(2)}) collective-permute-start(bf16[2,32,4608]{2,1,0:T(8,128)(2,1)S(1)} %pad_maximum_fusion.12), channel_id=1, source_target_pairs={{0,2},{1,3},{2,4},{3,5},{4,6},{5,7},{6,0},{7,1},{8,10},{9,11},{10,... | collective-permute-start | bytes 1769480 | tf_op jit(solution)/shard_map/ag_dense/ppermute | solution.py:33
  26.1 16.1 %collective-permute-start.3 = (bf16[2,32,4608]{2,1,0:T(8,128)(2,1)S(1)}, bf16[2,32,4608]{2,1,0:T(8,128)(2,1)S(1)}, u32[]{:S(2)}, u32[]{:S(2)}) collective-permute-start(bf16[2,32,4608]{2,1,0:T(8,128)(2,1)S(1)} %pad_maximum_fusion.12), channel_id=1, source_target_pairs={{0,6},{1,7},{2,0},{3,1},{4,2},{5,3},{6,4},{7,5},{8,14},{9,15},{10,... | collective-permute-start | bytes 1769480 | tf_op jit(solution)/shard_map/ag_dense/ppermute | solution.py:33
  42.4 50.7 %collective-permute-start.11 = (bf16[4,32,4608]{2,1,0:T(8,128)(2,1)S(1)}, bf16[4,32,4608]{2,1,0:T(8,128)(2,1)}, u32[]{:S(2)}, u32[]{:S(2)}) collective-permute-start(bf16[4,32,4608]{2,1,0:T(8,128)(2,1)S(1)} %pad_maximum_fusion.8.refs_0_), channel_id=1, source_target_pairs={{0,16},{16,32},{32,48},{48,0},{1,17},{17,33},{33,49},{49,1},{2,18}... | collective-permute-start | bytes 3538952 | tf_op jit(solution)/shard_map/ag_dense/ppermute | solution.py:37
  43.7 52.2 %collective-permute-start.13 = (bf16[4,32,4608]{2,1,0:T(8,128)(2,1)S(1)}, bf16[4,32,4608]{2,1,0:T(8,128)(2,1)}, u32[]{:S(2)}, u32[]{:S(2)}) collective-permute-start(bf16[4,32,4608]{2,1,0:T(8,128)(2,1)S(1)} %pad_maximum_fusion.8.refs_0_), channel_id=1, source_target_pairs={{0,48},{16,0},{32,16},{48,32},{1,49},{17,1},{33,17},{49,33},{2,50}... | collective-permute-start | bytes 3538952 | tf_op jit(solution)/shard_map/ag_dense/ppermute | solution.py:37
  45.2 8.5 %collective-permute-start.5 = (bf16[32,4608]{1,0:T(8,128)(2,1)S(1)}, bf16[32,4608]{1,0:T(8,128)(2,1)S(1)}, u32[]{:S(2)}, u32[]{:S(2)}) collective-permute-start(bf16[32,4608]{1,0:T(8,128)(2,1)S(1)} %slice_bitcast_fusion.3), channel_id=1, source_target_pairs={{0,2},{1,3},{2,4},{3,5},{4,6},{5,7},{6,0},{7,1},{8,10},{9,11},{10,... | collective-permute-start | bytes 884744 | tf_op jit(solution)/shard_map/ag_dense/ppermute | solution.py:33
  53.7 36.3 %collective-permute-start.7 = (bf16[2,128,3200]{2,1,0:T(8,128)(2,1)S(1)}, bf16[2,128,3200]{2,1,0:T(8,128)(2,1)S(1)}, u32[]{:S(2)}, u32[]{:S(2)}) collective-permute-start(bf16[2,128,3200]{2,1,0:T(8,128)(2,1)S(1)} %pad_maximum_fusion.3.refs_0_), channel_id=1, source_target_pairs={{0,2},{1,3},{2,4},{3,5},{4,6},{5,7},{6,0},{7,1},{8,10},{9,11},{10,... | collective-permute-start | bytes 4915208 | tf_op jit(solution)/shard_map/ag_mixer/ppermute | solution.py:33
  55.6 36.5 %collective-permute-start.8 = (bf16[2,128,3200]{2,1,0:T(8,128)(2,1)S(1)}, bf16[2,128,3200]{2,1,0:T(8,128)(2,1)S(1)}, u32[]{:S(2)}, u32[]{:S(2)}) collective-permute-start(bf16[2,128,3200]{2,1,0:T(8,128)(2,1)S(1)} %pad_maximum_fusion.3.refs_0_), channel_id=1, source_target_pairs={{0,6},{1,7},{2,0},{3,1},{4,2},{5,3},{6,4},{7,5},{8,14},{9,15},{10,... | collective-permute-start | bytes 4915208 | tf_op jit(solution)/shard_map/ag_mixer/ppermute | solution.py:33
  58.7 37.2 %collective-permute-start.12 = (bf16[4,32,4608]{2,1,0:T(8,128)(2,1)}, bf16[4,32,4608]{2,1,0:T(8,128)(2,1)}, u32[]{:S(2)}, u32[]{:S(2)}) collective-permute-start(bf16[4,32,4608]{2,1,0:T(8,128)(2,1)} %constant_dynamic-update-slice_fusion.refs_1_), channel_id=1, source_target_pairs={{0,16},{16,32},{32,48},{48,0},{1,17},{17,33},{33,49},{49,1},{2,18}... | collective-permute-start | bytes 3538952 | tf_op jit(solution)/shard_map/ag_dense/ppermute | solution.py:37
  89.9 24.6 %collective-permute-start.14 = (bf16[4,32,4608]{2,1,0:T(8,128)(2,1)}, bf16[4,32,4608]{2,1,0:T(8,128)(2,1)}, u32[]{:S(2)}, u32[]{:S(2)}) collective-permute-start(bf16[4,32,4608]{2,1,0:T(8,128)(2,1)} %constant_dynamic-update-slice_fusion.refs_1_), channel_id=1, source_target_pairs={{0,48},{16,0},{32,16},{48,32},{1,49},{17,1},{33,17},{49,33},{2,50}... | collective-permute-start | bytes 3538952 | tf_op jit(solution)/shard_map/ag_dense/ppermute | solution.py:37
  92.1 22.5 %collective-permute-start.9 = (bf16[128,3200]{1,0:T(8,128)(2,1)}, bf16[128,3200]{1,0:T(8,128)(2,1)}, u32[]{:S(2)}, u32[]{:S(2)}) collective-permute-start(bf16[128,3200]{1,0:T(8,128)(2,1)} %slice_bitcast_fusion.1), channel_id=1, source_target_pairs={{0,2},{1,3},{2,4},{3,5},{4,6},{5,7},{6,0},{7,1},{8,10},{9,11},{10,... | collective-permute-start | bytes 2457608 | tf_op jit(solution)/shard_map/ag_mixer/ppermute | solution.py:33
  93.6 21.0 %collective-permute-start.10 = (bf16[128,3200]{1,0:T(8,128)(2,1)}, bf16[128,3200]{1,0:T(8,128)(2,1)}, u32[]{:S(2)}, u32[]{:S(2)}) collective-permute-start(bf16[128,3200]{1,0:T(8,128)(2,1)} %slice_bitcast_fusion), channel_id=1, source_target_pairs={{0,6},{1,7},{2,0},{3,1},{4,2},{5,3},{6,4},{7,5},{8,14},{9,15},{10,... | collective-permute-start | bytes 2457608 | tf_op jit(solution)/shard_map/ag_mixer/ppermute | solution.py:33
  123.0 32.8 %collective-permute-start.16 = (bf16[1024,2176]{1,0:T(8,128)(2,1)}, bf16[1024,2176]{1,0:T(8,128)(2,1)}, u32[]{:S(2)}, u32[]{:S(2)}) collective-permute-start(bf16[1024,2176]{1,0:T(8,128)(2,1)} %get-tuple-element.110.refs_6_.refs_10_), channel_id=1, source_target_pairs={{0,1},{1,0},{2,3},{3,2},{4,5},{5,4},{6,7},{7,6},{8,9},{9,8},{10,11... | collective-permute-start | bytes 13369352 | tf_op jit(solution)/shard_map/ag_mixer/ppermute | solution.py:24
  127.2 10.5 %collective-permute-start.15 = (bf16[2048,512]{1,0:T(8,128)(2,1)}, bf16[2048,512]{1,0:T(8,128)(2,1)}, u32[]{:S(2)}, u32[]{:S(2)}) collective-permute-start(bf16[2048,512]{1,0:T(8,128)(2,1)} %get-tuple-element.111.own), channel_id=1, source_target_pairs={{0,1},{1,0},{2,3},{3,2},{4,5},{5,4},{6,7},{7,6},{8,9},{9,8},{10,11... | collective-permute-start | bytes 6291464 | tf_op jit(solution)/shard_map/ag_mixer/ppermute | solution.py:24
  127.3 28.6 %collective-permute-start.17 = (bf16[4,32,4608]{2,1,0:T(8,128)(2,1)}, bf16[4,32,4608]{2,1,0:T(8,128)(2,1)S(1)}, u32[]{:S(2)}, u32[]{:S(2)}) collective-permute-start(bf16[4,32,4608]{2,1,0:T(8,128)(2,1)} %collective-permute-done.11.refs_2_), channel_id=1, source_target_pairs={{0,16},{16,32},{32,48},{48,0},{1,17},{17,33},{33,49},{49,1},{2,18}... | collective-permute-start | bytes 3538952 | tf_op jit(solution)/shard_map/ppermute | solution.py:37
  127.3 28.6 %collective-permute-start.18 = (bf16[4,32,4608]{2,1,0:T(8,128)(2,1)}, bf16[4,32,4608]{2,1,0:T(8,128)(2,1)}, u32[]{:S(2)}, u32[]{:S(2)}) collective-permute-start(bf16[4,32,4608]{2,1,0:T(8,128)(2,1)} %collective-permute-done.14.refs_5_), channel_id=1, source_target_pairs={{0,48},{16,0},{32,16},{48,32},{1,49},{17,1},{33,17},{49,33},{2,50}... | collective-permute-start | bytes 3538952 | tf_op jit(solution)/shard_map/ppermute | solution.py:37
  161.3 21.2 %collective-permute-start.20 = (bf16[1024,3072]{1,0:T(8,128)(2,1)S(1)}, bf16[1024,3072]{1,0:T(8,128)(2,1)}, u32[]{:S(2)}, u32[]{:S(2)}) collective-permute-start(bf16[1024,3072]{1,0:T(8,128)(2,1)S(1)} %get-tuple-element.118.refs_8_.refs_2_.refs_4_), channel_id=1, source_target_pairs={{0,1},{1,0},{2,3},{3,2},{4,5},{5,4},{6,7},{7,6},{8,9},{9,8},{10,11... | collective-permute-start | bytes 18874376 | tf_op jit(solution)/shard_map/ag_dense/ppermute | solution.py:24
  162.6 14.2 %collective-permute-start.19 = (bf16[3072,512]{1,0:T(8,128)(2,1)S(1)}, bf16[3072,512]{1,0:T(8,128)(2,1)S(1)}, u32[]{:S(2)}, u32[]{:S(2)}) collective-permute-start(bf16[3072,512]{1,0:T(8,128)(2,1)S(1)} %get-tuple-element.120.own), channel_id=1, source_target_pairs={{0,1},{1,0},{2,3},{3,2},{4,5},{5,4},{6,7},{7,6},{8,9},{9,8},{10,11... | collective-permute-start | bytes 9437192 | tf_op jit(solution)/shard_map/ag_dense/ppermute | solution.py:24
  190.1 13.4 %collective-permute-start.21 = (bf16[256,1024]{1,0:T(8,128)(2,1)}, bf16[256,1024]{1,0:T(8,128)(2,1)}, u32[]{:S(2)}, u32[]{:S(2)}) collective-permute-start(bf16[256,1024]{1,0:T(8,128)(2,1)} %convert_element_type.378), channel_id=1, source_target_pairs={{0,64},{1,65},{2,66},{3,67},{4,68},{5,69},{6,70},{7,71},{8,72},{9,... | collective-permute-start | bytes 1572872 | tf_op jit(solution)/shard_map/ppermute | solution.py:41
  242.4 79.5 %collective-permute-start.23 = (bf16[256,7168]{1,0:T(8,128)(2,1)}, bf16[256,7168]{1,0:T(8,128)(2,1)}, u32[]{:S(2)}, u32[]{:S(2)}) collective-permute-start(bf16[256,7168]{1,0:T(8,128)(2,1)} %constant_dynamic-update-slice_fusion.3), channel_id=1, source_target_pairs={{0,1},{1,0},{2,3},{3,2},{4,5},{5,4},{6,7},{7,6},{8,9},{9,8},{10,11... | collective-permute-start | bytes 11010056 | tf_op jit(solution)/shard_map/ppermute | solution.py:24
  281.3 15.4 %collective-permute-start.22 = (bf16[256,1024]{1,0:T(8,128)(2,1)S(1)}, bf16[256,1024]{1,0:T(8,128)(2,1)S(1)}, u32[]{:S(2)}, u32[]{:S(2)}) collective-permute-start(bf16[256,1024]{1,0:T(8,128)(2,1)S(1)} %add_convert_fusion.5), channel_id=1, source_target_pairs={{64,0},{65,1},{66,2},{67,3},{68,4},{69,5},{70,6},{71,7},{72,8},{73... | collective-permute-start | bytes 1572872 | tf_op jit(solution)/shard_map/ppermute | solution.py:41
  305.1 21.0 %collective-permute-start.24 = (bf16[256,3072]{1,0:T(8,128)(2,1)}, bf16[256,3072]{1,0:T(8,128)(2,1)}, u32[]{:S(2)}, u32[]{:S(2)}) collective-permute-start(bf16[256,3072]{1,0:T(8,128)(2,1)} %get-tuple-element.146), channel_id=1, source_target_pairs={{0,1},{1,0},{2,3},{3,2},{4,5},{5,4},{6,7},{7,6},{8,9},{9,8},{10,11... | collective-permute-start | bytes 4718600 | tf_op jit(solution)/shard_map/b2/g_gu/ppermute | solution.py:24
  307.5 25.6 %collective-permute-start.25 = (bf16[256,512]{1,0:T(8,128)(2,1)S(1)}, bf16[256,512]{1,0:T(8,128)(2,1)S(1)}, u32[]{:S(2)}, u32[]{:S(2)}) collective-permute-start(bf16[256,512]{1,0:T(8,128)(2,1)S(1)} %get-tuple-element.300), channel_id=1, source_target_pairs={{0,1},{1,0},{2,3},{3,2},{4,5},{5,4},{6,7},{7,6},{8,9},{9,8},{10,11... | collective-permute-start | bytes 786440 | tf_op jit(solution)/shard_map/b2/g_down/ppermute | solution.py:24
  343.5 22.8 %collective-permute-start.27 = (bf16[4,128,768]{2,1,0:T(8,128)(2,1)}, bf16[4,128,768]{2,1,0:T(8,128)(2,1)}, u32[]{:S(2)}, u32[]{:S(2)}) collective-permute-start(bf16[4,128,768]{2,1,0:T(8,128)(2,1)} %get-tuple-element.253), channel_id=1, source_target_pairs={{0,16},{16,32},{32,48},{48,0},{1,17},{17,33},{33,49},{49,1},{2,18}... | collective-permute-start | bytes 2359304 | tf_op jit(solution)/shard_map/b2/g_gu/ppermute | solution.py:37
  344.3 21.9 %collective-permute-start.28 = (bf16[4,128,768]{2,1,0:T(8,128)(2,1)}, bf16[4,128,768]{2,1,0:T(8,128)(2,1)}, u32[]{:S(2)}, u32[]{:S(2)}) collective-permute-start(bf16[4,128,768]{2,1,0:T(8,128)(2,1)} %get-tuple-element.254), channel_id=1, source_target_pairs={{0,48},{16,0},{32,16},{48,32},{1,49},{17,1},{33,17},{49,33},{2,50}... | collective-permute-start | bytes 2359304 | tf_op jit(solution)/shard_map/b2/g_gu/ppermute | solution.py:37
  350.9 17.2 %collective-permute-start.29 = (bf16[640,512]{1,0:T(8,128)(2,1)S(1)}, bf16[640,512]{1,0:T(8,128)(2,1)S(1)}, u32[]{:S(2)}, u32[]{:S(2)}) collective-permute-start(bf16[640,512]{1,0:T(8,128)(2,1)S(1)} %get-tuple-element.261), channel_id=1, source_target_pairs={{0,2},{1,3},{2,4},{3,5},{4,6},{5,7},{6,0},{7,1},{8,10},{9,11},{10,... | collective-permute-start | bytes 1966088 | tf_op jit(solution)/shard_map/b2/rs_do/ppermute | solution.py:33
  351.0 17.2 %collective-permute-start.30 = (bf16[640,512]{1,0:T(8,128)(2,1)S(1)}, bf16[640,512]{1,0:T(8,128)(2,1)S(1)}, u32[]{:S(2)}, u32[]{:S(2)}) collective-permute-start(bf16[640,512]{1,0:T(8,128)(2,1)S(1)} %get-tuple-element.260), channel_id=1, source_target_pairs={{0,6},{1,7},{2,0},{3,1},{4,2},{5,3},{6,4},{7,5},{8,14},{9,15},{10,... | collective-permute-start | bytes 1966088 | tf_op jit(solution)/shard_map/b2/rs_do/ppermute | solution.py:33
  368.1 29.0 %collective-permute-start.31 = (bf16[256,2048]{1,0:T(8,128)(2,1)}, bf16[256,2048]{1,0:T(8,128)(2,1)}, u32[]{:S(2)}, u32[]{:S(2)}) collective-permute-start(bf16[256,2048]{1,0:T(8,128)(2,1)} %get-tuple-element.164), channel_id=1, source_target_pairs={{0,1},{1,0},{2,3},{3,2},{4,5},{5,4},{6,7},{7,6},{8,9},{9,8},{10,11... | collective-permute-start | bytes 3145736 | tf_op jit(solution)/shard_map/b2/g_qkv/ppermute | solution.py:24
  377.1 31.9 %collective-permute-start.42 = (bf16[2,640,512]{2,1,0:T(8,128)(2,1)}, bf16[2,640,512]{2,1,0:T(8,128)(2,1)}, u32[]{:S(2)}, u32[]{:S(2)}) collective-permute-start(bf16[2,640,512]{2,1,0:T(8,128)(2,1)} %pad_maximum_fusion.6), channel_id=1, source_target_pairs={{0,2},{1,3},{2,4},{3,5},{4,6},{5,7},{6,0},{7,1},{8,10},{9,11},{10,... | collective-permute-start | bytes 3932168 | tf_op jit(solution)/shard_map/b2/rs_do/ppermute | solution.py:33
  377.1 33.8 %collective-permute-start.43 = (bf16[2,640,512]{2,1,0:T(8,128)(2,1)}, bf16[2,640,512]{2,1,0:T(8,128)(2,1)}, u32[]{:S(2)}, u32[]{:S(2)}) collective-permute-start(bf16[2,640,512]{2,1,0:T(8,128)(2,1)} %pad_maximum_fusion.7), channel_id=1, source_target_pairs={{0,6},{1,7},{2,0},{3,1},{4,2},{5,3},{6,4},{7,5},{8,14},{9,15},{10,... | collective-permute-start | bytes 3932168 | tf_op jit(solution)/shard_map/b2/rs_do/ppermute | solution.py:33
  379.8 46.5 %collective-permute-start.33 = (bf16[8,128,768]{2,1,0:T(8,128)(2,1)}, bf16[8,128,768]{2,1,0:T(8,128)(2,1)}, u32[]{:S(2)}, u32[]{:S(2)}) collective-permute-start(bf16[8,128,768]{2,1,0:T(8,128)(2,1)} %pad_maximum_fusion.5), channel_id=1, source_target_pairs={{0,48},{16,0},{32,16},{48,32},{1,49},{17,1},{33,17},{49,33},{2,50}... | collective-permute-start | bytes 4718600 | tf_op jit(solution)/shard_map/b2/rs_gu/ppermute | solution.py:37
  381.2 45.0 %collective-permute-start.32 = (bf16[8,128,768]{2,1,0:T(8,128)(2,1)}, bf16[8,128,768]{2,1,0:T(8,128)(2,1)}, u32[]{:S(2)}, u32[]{:S(2)}) collective-permute-start(bf16[8,128,768]{2,1,0:T(8,128)(2,1)} %pad_maximum_fusion.4), channel_id=1, source_target_pairs={{0,16},{16,32},{32,48},{48,0},{1,17},{17,33},{33,49},{49,1},{2,18}... | collective-permute-start | bytes 4718600 | tf_op jit(solution)/shard_map/b2/rs_gu/ppermute | solution.py:37
  403.9 16.2 %collective-permute-start.40 = (bf16[128,2048]{1,0:T(8,128)(2,1)}, bf16[128,2048]{1,0:T(8,128)(2,1)S(1)}, u32[]{:S(2)}, u32[]{:S(2)}) collective-permute-start(bf16[128,2048]{1,0:T(8,128)(2,1)} %get-tuple-element.267), channel_id=1, source_target_pairs={{0,2},{1,3},{2,4},{3,5},{4,6},{5,7},{6,0},{7,1},{8,10},{9,11},{10,... | collective-permute-start | bytes 1572872 | tf_op jit(solution)/shard_map/b2/rs_q/ppermute | solution.py:33
  409.0 12.3 %collective-permute-start.41 = (bf16[128,2048]{1,0:T(8,128)(2,1)S(1)}, bf16[128,2048]{1,0:T(8,128)(2,1)}, u32[]{:S(2)}, u32[]{:S(2)}) collective-permute-start(bf16[128,2048]{1,0:T(8,128)(2,1)S(1)} %get-tuple-element.266), channel_id=1, source_target_pairs={{0,6},{1,7},{2,0},{3,1},{4,2},{5,3},{6,4},{7,5},{8,14},{9,15},{10,... | collective-permute-start | bytes 1572872 | tf_op jit(solution)/shard_map/b2/rs_q/ppermute | solution.py:33
  423.3 28.0 %collective-permute-start.44 = (bf16[2,128,2048]{2,1,0:T(8,128)(2,1)S(1)}, bf16[2,128,2048]{2,1,0:T(8,128)(2,1)S(1)}, u32[]{:S(2)}, u32[]{:S(2)}) collective-permute-start(bf16[2,128,2048]{2,1,0:T(8,128)(2,1)S(1)} %pad_maximum_fusion.9), channel_id=1, source_target_pairs={{0,2},{1,3},{2,4},{3,5},{4,6},{5,7},{6,0},{7,1},{8,10},{9,11},{10,... | collective-permute-start | bytes 3145736 | tf_op jit(solution)/shard_map/b2/rs_q/ppermute | solution.py:33
  423.5 27.8 %collective-permute-start.45 = (bf16[2,128,2048]{2,1,0:T(8,128)(2,1)S(1)}, bf16[2,128,2048]{2,1,0:T(8,128)(2,1)S(1)}, u32[]{:S(2)}, u32[]{:S(2)}) collective-permute-start(bf16[2,128,2048]{2,1,0:T(8,128)(2,1)S(1)} %pad_maximum_fusion.10), channel_id=1, source_target_pairs={{0,6},{1,7},{2,0},{3,1},{4,2},{5,3},{6,4},{7,5},{8,14},{9,15},{10,... | collective-permute-start | bytes 3145736 | tf_op jit(solution)/shard_map/b2/rs_q/ppermute | solution.py:33
  433.8 17.5 %collective-permute-start.46 = (bf16[128,768]{1,0:T(8,128)(2,1)S(1)}, bf16[128,768]{1,0:T(8,128)(2,1)S(1)}, u32[]{:S(2)}, u32[]{:S(2)}) collective-permute-start(bf16[128,768]{1,0:T(8,128)(2,1)S(1)} %get-tuple-element.288), channel_id=1, source_target_pairs={{0,2},{1,3},{2,4},{3,5},{4,6},{5,7},{6,0},{7,1},{8,10},{9,11},{10,... | collective-permute-start | bytes 589832 | tf_op jit(solution)/shard_map/b2/rs_gu/ppermute | solution.py:33
  433.8 17.5 %collective-permute-start.47 = (bf16[128,768]{1,0:T(8,128)(2,1)S(1)}, bf16[128,768]{1,0:T(8,128)(2,1)S(1)}, u32[]{:S(2)}, u32[]{:S(2)}) collective-permute-start(bf16[128,768]{1,0:T(8,128)(2,1)S(1)} %get-tuple-element.287), channel_id=1, source_target_pairs={{0,6},{1,7},{2,0},{3,1},{4,2},{5,3},{6,4},{7,5},{8,14},{9,15},{10,... | collective-permute-start | bytes 589832 | tf_op jit(solution)/shard_map/b2/rs_gu/ppermute | solution.py:33
  447.4 17.5 %collective-permute-start.51 = (bf16[640,512]{1,0:T(8,128)(2,1)S(1)}, bf16[640,512]{1,0:T(8,128)(2,1)S(1)}, u32[]{:S(2)}, u32[]{:S(2)}) collective-permute-start(bf16[640,512]{1,0:T(8,128)(2,1)S(1)} %fusion.12), channel_id=1, source_target_pairs={{0,8},{1,9},{2,10},{3,11},{4,12},{5,13},{6,14},{7,15},{8,0},{9,1},... | collective-permute-start | bytes 1966088 | tf_op jit(solution)/shard_map/b2/rs_do/ppermute | solution.py:28
  451.3 9.6 %collective-permute-start.38 = (f32[18,128]{1,0:T(8,128)S(1)}, f32[18,128]{1,0:T(8,128)S(1)}, u32[]{:S(2)}, u32[]{:S(2)}) collective-permute-start(f32[18,128]{1,0:T(8,128)S(1)} %add.1485), channel_id=1, source_target_pairs={{0,2},{1,3},{2,0},{3,1},{4,6},{5,7},{6,4},{7,5},{8,10},{9,11},{10,... | collective-permute-start | bytes 27656 | tf_op jit(solution)/shard_map/ppermute | solution.py:52
  453.1 23.1 %collective-permute-start.48 = (bf16[128,2048]{1,0:T(8,128)(2,1)S(1)}, bf16[128,2048]{1,0:T(8,128)(2,1)S(1)}, u32[]{:S(2)}, u32[]{:S(2)}) collective-permute-start(bf16[128,2048]{1,0:T(8,128)(2,1)S(1)} %get-tuple-element.250), channel_id=1, source_target_pairs={{0,8},{1,9},{2,10},{3,11},{4,12},{5,13},{6,14},{7,15},{8,0},{9,1},... | collective-permute-start | bytes 1572872 | tf_op jit(solution)/shard_map/rs_q/ppermute | solution.py:28
  456.7 10.1 %collective-permute-start.49 = (bf16[2,128,768]{2,1,0:T(8,128)(2,1)S(1)}, bf16[2,128,768]{2,1,0:T(8,128)(2,1)S(1)}, u32[]{:S(2)}, u32[]{:S(2)}) collective-permute-start(bf16[2,128,768]{2,1,0:T(8,128)(2,1)S(1)} %pad_maximum_fusion.16), channel_id=1, source_target_pairs={{0,2},{1,3},{2,4},{3,5},{4,6},{5,7},{6,0},{7,1},{8,10},{9,11},{10,... | collective-permute-start | bytes 1179656 | tf_op jit(solution)/shard_map/rs_gu/ppermute | solution.py:33
  458.3 8.5 %collective-permute-start.50 = (bf16[2,128,768]{2,1,0:T(8,128)(2,1)S(1)}, bf16[2,128,768]{2,1,0:T(8,128)(2,1)S(1)}, u32[]{:S(2)}, u32[]{:S(2)}) collective-permute-start(bf16[2,128,768]{2,1,0:T(8,128)(2,1)S(1)} %pad_maximum_fusion.17), channel_id=1, source_target_pairs={{0,6},{1,7},{2,0},{3,1},{4,2},{5,3},{6,4},{7,5},{8,14},{9,15},{10,... | collective-permute-start | bytes 1179656 | tf_op jit(solution)/shard_map/rs_gu/ppermute | solution.py:33
  460.9 32.4 %collective-permute-start.39 = (f32[18,128]{1,0:T(8,128)S(1)}, f32[18,128]{1,0:T(8,128)S(1)}, u32[]{:S(2)}, u32[]{:S(2)}) collective-permute-start(f32[18,128]{1,0:T(8,128)S(1)} %add.1486), channel_id=1, source_target_pairs={{0,4},{1,5},{2,6},{3,7},{4,0},{5,1},{6,2},{7,3},{8,12},{9,13},{10,... | collective-permute-start | bytes 27656 | tf_op jit(solution)/shard_map/ppermute | solution.py:52
  491.7 8.5 %collective-permute-start.57 = (bf16[480,512]{1,0:T(8,128)(2,1)S(1)}, bf16[480,512]{1,0:T(8,128)(2,1)S(1)}, u32[]{:S(2)}, u32[]{:S(2)}) collective-permute-start(bf16[480,512]{1,0:T(8,128)(2,1)S(1)} %slice_dynamic-update-slice_fusion), channel_id=1, source_target_pairs={{0,48},{16,0},{32,16},{48,32},{1,49},{17,1},{33,17},{49,33},{2,50}... | collective-permute-start | bytes 1474568 | tf_op jit(solution)/shard_map/fin/ppermute | solution.py:37
  491.8 10.0 %collective-permute-start.58 = (bf16[480,512]{1,0:T(8,128)(2,1)S(1)}, bf16[480,512]{1,0:T(8,128)(2,1)S(1)}, u32[]{:S(2)}, u32[]{:S(2)}) collective-permute-start(bf16[480,512]{1,0:T(8,128)(2,1)S(1)} %slice_dynamic-update-slice_fusion), channel_id=1, source_target_pairs={{0,16},{16,32},{32,48},{48,0},{1,17},{17,33},{33,49},{49,1},{2,18}... | collective-permute-start | bytes 1474568 | tf_op jit(solution)/shard_map/fin/ppermute | solution.py:37
  514.5 8.6 %collective-permute-start.61 = (bf16[960,512]{1,0:T(8,128)(2,1)S(1)}, bf16[960,512]{1,0:T(8,128)(2,1)S(1)}, u32[]{:S(2)}, u32[]{:S(2)}) collective-permute-start(bf16[960,512]{1,0:T(8,128)(2,1)S(1)} %dynamic-slice_dynamic-update-slice_fusion.7), channel_id=1, source_target_pairs={{0,1},{1,0},{2,3},{3,2},{4,5},{5,4},{6,7},{7,6},{8,9},{9,8},{10,11... | collective-permute-start | bytes 2949128 | tf_op jit(solution)/shard_map/fin/ppermute | solution.py:24
  (89 other events, 588.4 us)
